TPU v7x, 512 devices: a whole 4x8x8 slice. The times are simulated.
512 devices in a mesh: batch: 8 (over z), pos: 64 (over y, x, core).
Axes of the slice: x: 4, y: 8, z: 8, core: 2. Of those that a mesh axis runs over, the one named last changes fastest.
Arguments:
- cand_proj: bfloat16 [8192, 4096], P(('batch', 'pos')), may hold values from -6 to 6
- cand_input: bfloat16 [8192, 1024], P(('batch', 'pos')), may hold values from -6 to 6
- kv_pool: bfloat16 [64, 2, 2048, 1024], P('batch', None, 'pos'), may hold values from -6 to 6
- page_owner: int32 [8, 64, 8], P('batch', 'pos'), may hold values from 0 to 7, as said below
- page_slot: int32 [8, 64, 8], P('batch', 'pos'), may hold values from 0 to 7, as said below
- lengths: int32 [8], P('batch'), may hold values from 4096 to 16384
- block_mask: int32 [8, 8, 128], P('batch', None, 'pos'), may hold values 0 or 1
- out_gain: float32 [1024], replicated, may hold values from 0.5 to 1.5
- out_weight: bfloat16 [1024, 1024], replicated, may hold values from -0.1875 to 0.1875
Outputs:
- cand_output: bfloat16 [8192, 1024], P(('batch', 'pos'))
Inputs may be any that keep to these rules, and one draw needn't show every extreme that they name: `page_owner`: for each user and each index of pos, every index of batch appears exactly 1 times among the 8 pages. At one index of pos, the pairs (page_owner, page_slot) of all users are distinct.
All inputs are finite; a program needn't handle non-finite values. No bound on the sum of `block_mask` on one device may be relied on, other than what follows from the above.
Results may differ from a plain program's by a relative error of at most 0.0095.
Values may be sent and summed in bfloat16 or wider, within the bound.
No kernel may reach another device: no remote copies, remote signals or barrier semaphores. Data moves between devices by JAX's collectives and lax.ppermute only.
A program may use at most 128 MiB of HBM per device.

v0:
```python
import jax
import jax.numpy as jnp
from jax import lax
from jax.sharding import PartitionSpec as P

HEADS = 8
TILE = 128


eps = 1e-05


def attend_block(query, keys, values, allowed, scale):
    scores = jnp.einsum("rhd,thd->hrt", query, keys, preferred_element_type=jnp.float32) * scale
    weight = jnp.where(allowed[None], jax.nn.silu(scores), 0.0).astype(jnp.bfloat16)
    return jnp.einsum("hrt,thd->rhd", weight, values, preferred_element_type=jnp.float32)


def local_attention(query, row_mask, hist_keys, hist_vals, live, scale):
    rows = query.shape[0]
    allowed = jnp.repeat(row_mask, TILE, axis=1) & live[None, :]
    total = attend_block(query, hist_keys, hist_vals, allowed, scale)
    return total.reshape(rows, -1)


def on_device(
    cand_proj, cand_input, kv_pool, page_owner, page_slot, lengths, block_mask, out_gain, out_weight
):
    width = cand_input.shape[1]
    headsize = width // HEADS
    scale = headsize ** (-0.5)
    owners = page_owner.reshape(-1)
    slot_list = page_slot.reshape(-1)
    order = jnp.argsort(owners, stable=True)
    wanted = slot_list[order]
    served = lax.all_to_all(wanted, "batch", split_axis=0, concat_axis=0, tiled=True)
    fetched = lax.all_to_all(kv_pool[served], "batch", split_axis=0, concat_axis=0, tiled=True)
    local_kv = fetched[jnp.argsort(order)]
    hist_pair = jnp.stack(
        [local_kv[:, 0].reshape(-1, width), local_kv[:, 1].reshape(-1, width)], axis=0
    )
    hist_len = hist_pair.shape[1]
    mask_cols = block_mask[0]
    cand_tiles = mask_cols.shape[0]
    position = lax.axis_index("pos")
    act = jax.nn.silu(cand_proj.astype(jnp.float32)).astype(jnp.bfloat16)
    u_act = act[:, :width]
    v_act = act[:, width : 2 * width]
    q_act = act[:, 2 * width : 3 * width]
    k_act = act[:, 3 * width :]
    hist_keys = hist_pair[0].reshape(-1, HEADS, headsize)
    hist_vals = hist_pair[1].reshape(-1, HEADS, headsize)
    live = position * hist_len + jnp.arange(hist_len, dtype=jnp.int32) < lengths[0]
    piece = lax.all_gather(q_act, "pos", axis=0, tiled=True)
    rows = piece.shape[0]
    row_tile = jnp.arange(rows, dtype=jnp.int32) // TILE
    onehot = (row_tile[:, None] == jnp.arange(cand_tiles, dtype=jnp.int32)[None, :]).astype(
        jnp.float32
    )
    row_mask = jnp.dot(onehot, mask_cols.astype(jnp.float32)) > 0.5
    partials = local_attention(
        piece.reshape(rows, HEADS, headsize), row_mask, hist_keys, hist_vals, live, scale
    )
    attn = lax.psum_scatter(partials, "pos", scatter_dimension=0, tiled=True)
    rows_here = attn.shape[0]
    query_own = q_act.astype(jnp.float32).reshape(rows_here, HEADS, headsize)
    key_own = k_act.astype(jnp.float32).reshape(rows_here, HEADS, headsize)
    own = jax.nn.silu(jnp.sum(query_own * key_own, axis=-1) * scale).astype(jnp.bfloat16)
    own_term = own.astype(jnp.float32)[:, :, None] * v_act.astype(jnp.float32).reshape(
        rows_here, HEADS, headsize
    )
    attn = attn + own_term.reshape(rows_here, width)
    mean = jnp.mean(attn, axis=-1, keepdims=True)
    centered = attn - mean
    var = jnp.mean(centered * centered, axis=-1, keepdims=True)
    normed = (centered * lax.rsqrt(var + eps) * out_gain * u_act.astype(jnp.float32)).astype(
        jnp.bfloat16
    )
    result = cand_input.astype(jnp.float32) + jnp.dot(
        normed, out_weight, preferred_element_type=jnp.float32
    )
    return result.astype(jnp.bfloat16)


def solution(mesh):
    placed = (
        P(("batch", "pos"), None),
        P(("batch", "pos"), None),
        P("batch", None, "pos", None),
        P("batch", "pos", None),
        P("batch", "pos", None),
        P("batch"),
        P("batch", None, "pos"),
        P(),
        P(),
    )
    return jax.shard_map(
        on_device, mesh=mesh, in_specs=placed, out_specs=P(("batch", "pos"), None), check_vma=False
    )
```

profile of v0, /device:TPU:1, one launch (start us, length us, event | category | flops | bytes accessed | tf_op | source)
XLA Modules:
  0.0 269.7 jit_solution(8081544453103778378)
XLA Ops:
  6.5 1.1 fusion.10
  7.7 0.6 slice.31
  8.3 0.0 all-gather.2.cloned.1.call-update
  8.3 1.6 sort.34
  10.0 1.3 gather_fusion
  11.3 0.1 copy.40
  11.4 17.2 %all_to_all.17 = s32[8,1,1]{2,1,0:T(1,128)S(1)} all-to-all(s32[8,1,1]{2,1,0:T(1,128)S(1)} %copy.40), channel_id=1, replica_groups=mesh['batch'=8,'pos'=64] {'batch'}, dimensions={0} | all-to-all | bytes 64 | tf_op jit(solution)/shard_map/all_to_all | solution.py:36
  28.5 0.2 reduce
  28.8 2.8 %gather_fusion.1 = bf16[8,2,32,1024]{3,2,1,0:T(8,128)(2,1)} fusion(bf16[8,2,32,1024]{3,2,1,0:T(8,128)(2,1)} %param.11, s32[1024]{0:T(1024)S(1)} %pad_clamp_fusion.1), kind=kCustom, calls=%fused_computation.1 | custom fusion | bytes 2097184 | tf_op jit(solution)/shard_map/gather | solution.py:37
  31.6 3.6 %all-to-all-start.1 = ((bf16[8,2,32,1024]{3,2,1,0:T(8,128)(2,1)}), bf16[8,2,32,1024]{3,2,1,0:T(8,128)(2,1)S(1)}, u32[]{:S(2)}, u32[]{:S(2)}) async-start(bf16[8,2,32,1024]{3,2,1,0:T(8,128)(2,1)} %gather_fusion.1), calls=%async_computation.1 | async-start | bytes 2097152 | tf_op jit(solution)/shard_map/all_to_all | solution.py:37
  35.2 0.0 reduce-scatter.4.cloned.1.call-start
  35.3 0.9 sort.35
  36.9 0.3 convolution_compare_fusion
  37.2 0.2 bitcast_and_fusion
  37.4 1.1 copy.41
  38.5 25.8 %all-to-all-done.1 = bf16[8,2,32,1024]{3,2,1,0:T(8,128)(2,1)S(1)} async-done(((bf16[8,2,32,1024]{3,2,1,0:T(8,128)(2,1)}), bf16[8,2,32,1024]{3,2,1,0:T(8,128)(2,1)S(1)}, u32[]{:S(2)}, u32[]{:S(2)}) %all-to-all-start.1) | async-done | bytes 1048608 | tf_op jit(solution)/shard_map/all_to_all | solution.py:37
  64.3 1.6 gather_fusion.2
  65.9 1.3 fusion.29
  67.2 0.1 copy.52
  67.3 0.1 copy.53
  67.4 31.7 %all-gather.2.cloned.1.call-done = bf16[1024,1024]{1,0:T(8,128)(2,1)} async-done(((bf16[16,1024]{1,0:T(8,128)(2,1)}), bf16[1024,1024]{1,0:T(8,128)(2,1)}) %all-gather.2.cloned.1.call-update) | async-done | bytes 2097168 | tf_op jit(solution)/shard_map/all_gather | solution.py:54
  99.1 3.9 %copy.42 = bf16[1024,1024]{0,1:T(8,128)(2,1)} copy(bf16[1024,1024]{1,0:T(8,128)(2,1)} %all-gather.2.cloned.1.call-done) | data formatting | bytes 4194304 | tf_op jit(solution)/shard_map/all_gather | solution.py:54
  103.0 7.6 %fusion = f32[8,128,1024]{2,1,0:T(8,128)} fusion(pred[1024,256]{1,0:T(8,128)(4,1)S(1)} %copy-done.1, bf16[1024,8,128]{0,2,1:T(8,128)(2,1)} %bitcast.40, bf16[256,8,128]{2,1,0:T(8,128)(2,1)S(1)} %bitcast.43, bf16[256,8,128]{2,1,0:T(8,128)(2,1)S(1)} %bitcast.44), kind=kOutput, calls=%fused_computation.4 | convolution fusion | flops 1088421888 | bytes 7602176 | tf_op jit(solution)/shard_map/hrt,thd->rhd/dot_general | solution.py:16
  110.6 5.3 %copy.50 = f32[1024,1024]{1,0:T(8,128)} copy(f32[1024,1024]{0,1:T(8,128)} %bitcast.39) | data formatting | bytes 8388608
  116.0 0.1 reduce_sum.27
  116.1 0.1 copy.46
  116.2 0.1 copy.47
  116.3 144.3 %reduce-scatter.4.cloned.1.call-done = f32[16,1024]{1,0:T(8,128)} async-done(((f32[1024,1024]{1,0:T(8,128)}), f32[16,1024]{1,0:T(8,128)}) %reduce-scatter.4.cloned.1.call-update) | async-done | bytes 65552 | tf_op jit(solution)/shard_map/reduce_scatter | solution.py:64
  260.5 0.1 mul.84
  260.6 1.0 fusion.27
  261.6 0.2 multiply_reduce_fusion
  261.8 1.0 fusion.3
  (27 shorter events, 0.1 us)
Async XLA Ops:
  6.5 255.3 %copy-start = (bf16[1024,1024]{1,0:T(8,128)(2,1)S(1)}, bf16[1024,1024]{1,0:T(8,128)(2,1)}, u32[]{:S(2)}) copy-start(bf16[1024,1024]{1,0:T(8,128)(2,1)} %param.17) | copy-start | bytes 6291460
  6.5 30.3 %copy-start.4 = (s32[1,8,2]{1,2,0:T(2,128)S(1)}, s32[1,8,2]{1,2,0:T(2,128)}, u32[]{:S(2)}) copy-start(s32[1,8,2]{1,2,0:T(2,128)} %param.15) | copy-start | bytes 196
  6.5 92.5 %all-gather.2.cloned.1.call-start = ((), (), s32[]{:S(2)}) async-start(), calls=%async_computation.3 | async-start | bytes 2129920 | tf_op jit(solution)/shard_map/all_gather | solution.py:54
  31.6 32.7 %all-to-all-start.1 = ((bf16[8,2,32,1024]{3,2,1,0:T(8,128)(2,1)}), bf16[8,2,32,1024]{3,2,1,0:T(8,128)(2,1)S(1)}, u32[]{:S(2)}, u32[]{:S(2)}) async-start(bf16[8,2,32,1024]{3,2,1,0:T(8,128)(2,1)} %gather_fusion.1), calls=%async_computation.1 | async-start | bytes 2097152 | tf_op jit(solution)/shard_map/all_to_all | solution.py:37
  35.2 225.3 %reduce-scatter.4.cloned.1.call-start = ((), (), s32[]{:S(2)}) async-start(), calls=%async_computation.4 | async-start | bytes 4259840 | tf_op jit(solution)/shard_map/reduce_scatter | solution.py:64
  65.9 37.2 %copy-start.1 = (pred[1024,256]{1,0:T(8,128)(4,1)S(1)}, pred[1024,256]{1,0:T(8,128)(4,1)}, u32[]{:S(2)}) copy-start(pred[1024,256]{1,0:T(8,128)(4,1)} %copy.41) | copy-start | bytes 786436
  115.9 145.9 %copy-start.2 = (bf16[16,1024]{1,0:T(8,128)(2,1)S(1)}, bf16[16,1024]{1,0:T(8,128)(2,1)}, u32[]{:S(2)}) copy-start(bf16[16,1024]{1,0:T(8,128)(2,1)} %param.10) | copy-start | bytes 98308
  115.9 145.9 %copy-start.3 = (f32[1024]{0:T(1024)S(1)}, f32[1024]{0:T(1024)}, u32[]{:S(2)}) copy-start(f32[1024]{0:T(1024)} %param.16) | copy-start | bytes 12292
Sparse Core Ops, SparseCore 0:
  10.7 88.3 all-gather.1
  116.1 144.3 reduce-scatter.3
where the time goes:
time: 274 us; the launch traced here: 270 us
  waiting for transfers between devices  202 us (74%)
  local copies, waits for them, and re-layouts  18.6 us (7%)
  blocking collectives  17.2 us (6%)
  between operations  14.2 us (5%)
  matrix products  8.93 us (3%)
  other arithmetic  5.45 us (2%)
  starting transfers between devices  3.6 us (1%)
    reduce_scatter x1, waiting for transfers between devices, on_device(): attn = lax.psum_scatter(partials, 'pos', scatter_dimension=0, tiled=True)  144 us
    all_gather x1, waiting for transfers between devices, on_device(): piece = lax.all_gather(q_act, 'pos', axis=0, tiled=True)  31.7 us
    all_to_all x1, waiting for transfers between devices, on_device(): lax.all_to_all(kv_pool[served], 'batch', split_axis=0, concat_axis=0, til...  25.8 us
    all_to_all x1, blocking collectives, on_device(): lax.all_to_all(wanted, 'batch', split_axis=0, concat_axis=0, tiled=True)  17.2 us
    dot_general x1, matrix products, attend_block(): jnp.einsum('hrt,thd->rhd', weight, values, preferred_element_type=jnp.flo...  7.56 us
    unnamed x14, local copies, waits for them, and re-layouts  5.57 us
  transfers between devices with their start and end apart: 3, of which 3 were waited for; matrix products, arithmetic and copies ran while one was open for 4% of the time, Pallas kernels for 0%

commit v1 on v0

v1 whole, which is shorter than its diff:
```python
import functools

import jax
import jax.numpy as jnp
from jax import lax
from jax.experimental import pallas as pl
from jax.experimental.pallas import tpu as pltpu
from jax.sharding import Mesh
from jax.sharding import PartitionSpec as P

HEADS = 8
PAGE = 32
eps = 1e-05

PLANE = ("y", "x", "c")
SPREAD = ("z", "x", "c")


def exchange(array, axes):
    return lax.all_to_all(array, axes, split_axis=0, concat_axis=0, tiled=True)


def split_pages_kernel(slot_ref, page_ref, out_ref):
    hd = out_ref.shape[2]
    for h in range(HEADS):
        for kv in range(2):
            out_ref[h, kv * PAGE : (kv + 1) * PAGE, :] = page_ref[0, kv, :, h * hd : (h + 1) * hd]


def split_pages(slots, kv_pool):
    count, _, page, width = kv_pool.shape
    users = slots.shape[0]
    hd = width // HEADS
    return pl.pallas_call(
        split_pages_kernel,
        grid_spec=pltpu.PrefetchScalarGridSpec(
            num_scalar_prefetch=1,
            grid=(users,),
            in_specs=[pl.BlockSpec((1, 2, page, width), lambda u, slot: (slot[u], 0, 0, 0))],
            out_specs=pl.BlockSpec((HEADS, 2 * page, hd), lambda u, slot: (u, 0, 0)),
        ),
        out_shape=jax.ShapeDtypeStruct((users * HEADS, 2 * page, hd), kv_pool.dtype),
        name="split_pages",
    )(slots, kv_pool)


def attend_kernel(scale, q_ref, kv_ref, mask_ref, out_ref, acc_ref):
    rows, hd = q_ref.shape
    pages = kv_ref.shape[0]
    step = 8
    span = step * PAGE
    tiles = mask_ref.shape[0]
    q = q_ref[...]
    for i in range(pages // step):
        block = kv_ref[i * step : (i + 1) * step]
        keys = block[:, :PAGE, :].reshape(span, hd)
        values = block[:, PAGE:, :].reshape(span, hd)
        half = lax.dot_general(q, keys, (((1,), (1,)), ((), ())), preferred_element_type=jnp.float32)
        half = half * (0.5 * scale)
        weight = (half + half * jnp.tanh(half)).astype(jnp.bfloat16)
        allowed = mask_ref[:, i * span : (i + 1) * span]
        weight = weight.reshape(tiles, rows // tiles, span) * allowed[:, None, :]
        part = jnp.dot(weight.reshape(rows, span), values, preferred_element_type=jnp.float32)
        if i == 0:
            acc_ref[...] = part
        else:
            acc_ref[...] += part
    out_ref[...] = acc_ref[...].astype(out_ref.dtype)


def attend(query, pages, mask, scale):
    rows, hd = query.shape
    return pl.pallas_call(
        functools.partial(attend_kernel, scale),
        in_specs=[pl.BlockSpec(memory_space=pltpu.VMEM)] * 3,
        out_specs=pl.BlockSpec(memory_space=pltpu.VMEM),
        out_shape=jax.ShapeDtypeStruct((rows, hd), jnp.bfloat16),
        scratch_shapes=[pltpu.VMEM((rows, hd), jnp.float32)],
        compiler_params=pltpu.CompilerParams(vmem_limit_bytes=40 * 1024 * 1024),
        name="attend",
    )(query, pages, mask)


def on_device(
    cand_proj, cand_input, kv_pool, page_owner, page_slot, lengths, block_mask, out_gain, out_weight
):
    rows, width = cand_input.shape
    hd = width // HEADS
    scale = hd ** (-0.5)
    n_z, n_y = lax.axis_size("z"), lax.axis_size("y")
    n_h = lax.axis_size("x") * lax.axis_size("c")
    me_z = lax.axis_index("z")
    me_h = lax.axis_index(("x", "c"))
    position = lax.axis_index(PLANE)

    owners, slots = page_owner.reshape(-1), page_slot.reshape(-1)
    pages = owners.shape[0]
    hit = (owners[None, :] == jnp.arange(n_z, dtype=jnp.int32)[:, None]).astype(jnp.int32)
    index = jnp.arange(pages, dtype=jnp.int32)
    slot_of = jnp.sum(hit * slots[None, :], axis=1)
    live = jnp.clip(lengths[0] - (position * pages + index) * PAGE, 0, PAGE)
    live_of = jnp.sum(hit * live[None, :], axis=1)
    seen = jnp.repeat(block_mask[0], pages // block_mask.shape[2], axis=1)
    seen_of = jnp.sum(hit[:, None, :] * seen[None, :, :], axis=2)
    tiles = seen.shape[0]
    info = jnp.concatenate([slot_of[:, None], live_of[:, None], seen_of], axis=1).reshape(-1)
    info = jnp.pad(info, (0, 128 - info.shape[0]))
    told = exchange(jnp.broadcast_to(info[None], (n_z * n_h, 128)), SPREAD)
    told = told[:, : n_z * (tiles + 2)].reshape(n_z, n_h, n_z, tiles + 2)
    served = lax.dynamic_index_in_dim(told[:, :, :, 0], me_h, 1, keepdims=False)
    served = lax.dynamic_index_in_dim(served, me_z, 1, keepdims=False)
    mine = lax.dynamic_index_in_dim(told, me_z, 0, keepdims=False)
    mine = mine.transpose(2, 1, 0)
    alive = jnp.arange(PAGE, dtype=jnp.int32) < mine[1][:, :, None]
    mask = (mine[2:, :, :, None] == 1) & alive[None]
    mask = mask.reshape(tiles, -1).astype(jnp.bfloat16)

    act = jax.nn.silu(cand_proj.astype(jnp.float32)).astype(jnp.bfloat16)
    u_act = act[:, :width]
    v_act = act[:, width : 2 * width]
    q_act = act[:, 2 * width : 3 * width]
    k_act = act[:, 3 * width :]
    by_head = q_act.reshape(rows, HEADS, hd).transpose(1, 0, 2)
    sent = jnp.broadcast_to(by_head[None], (n_y, HEADS, rows, hd)).reshape(n_y * HEADS, rows, hd)
    query = exchange(sent, PLANE).reshape(-1, hd)

    got = exchange(split_pages(served, kv_pool), SPREAD)
    part = attend(query, got, mask, scale)
    back = exchange(part.reshape(n_y * n_h, rows, hd), PLANE)
    attn = jnp.sum(back.reshape(n_y, HEADS, rows, hd).astype(jnp.float32), axis=0)
    attn = attn.transpose(1, 0, 2)

    query_own = q_act.astype(jnp.float32).reshape(rows, HEADS, hd)
    key_own = k_act.astype(jnp.float32).reshape(rows, HEADS, hd)
    own = jax.nn.silu(jnp.sum(query_own * key_own, axis=-1) * scale).astype(jnp.bfloat16)
    attn = attn + own.astype(jnp.float32)[:, :, None] * v_act.astype(jnp.float32).reshape(
        rows, HEADS, hd
    )
    attn = attn.reshape(rows, width)
    mean = jnp.mean(attn, axis=-1, keepdims=True)
    centered = attn - mean
    var = jnp.mean(centered * centered, axis=-1, keepdims=True)
    normed = (centered * lax.rsqrt(var + eps) * out_gain * u_act.astype(jnp.float32)).astype(
        jnp.bfloat16
    )
    result = cand_input.astype(jnp.float32) + jnp.dot(
        normed, out_weight, preferred_element_type=jnp.float32
    )
    return result.astype(jnp.bfloat16)


def solution(mesh):
    n_z, n_p = mesh.shape["batch"], mesh.shape["pos"]
    cores, n_x = 2, HEADS // 2
    grid = Mesh(mesh.devices.reshape(n_z, n_p // HEADS, n_x, cores), ("z", "y", "x", "c"))
    rows = P(("z", "y", "x", "c"), None)
    placed = (
        rows,
        rows,
        P("z", None, PLANE, None),
        P("z", PLANE, None),
        P("z", PLANE, None),
        P("z"),
        P("z", None, PLANE),
        P(),
        P(),
    )
    return jax.shard_map(on_device, mesh=grid, in_specs=placed, out_specs=rows, check_vma=False)
```

time: 274 us -> 111 us (0.41); the launches traced: 270 us -> 110 us
  waiting for transfers between devices: 202 us -> 48.6 us
  starting transfers between devices: 3.6 us -> 35.8 us
  blocking collectives: 17.2 us -> 0 us
  between operations: 14.2 us -> 1.01 us
  local copies, waits for them, and re-layouts: 18.6 us -> 8.83 us
  Pallas kernels: 0 us -> 8.37 us
  matrix products: 8.93 us -> 1.81 us
    reduce_scatter x1 -> x0, waiting for transfers between devices: 144 us -> none  [on_device(): attn = lax.psum_scatter(partials, 'pos', scatter_dimension=0, tiled=True)]
    all_to_all x1 -> x4, starting transfers between devices: 3.56 us -> 35.8 us  [exchange(): return lax.all_to_all(array, axes, split_axis=0, concat_axis=0, tiled=True)]
    all_gather x1 -> x0, waiting for transfers between devices: 31.7 us -> none  [on_device(): piece = lax.all_gather(q_act, 'pos', axis=0, tiled=True)]
    all_to_all x1 -> x4, waiting for transfers between devices: 25.8 us -> 48.6 us  [exchange(): return lax.all_to_all(array, axes, split_axis=0, concat_axis=0, tiled=True)]
    all_to_all x1 -> x0, blocking collectives: 17.2 us -> none  [on_device(): lax.all_to_all(wanted, 'batch', split_axis=0, concat_axis=0, tiled=True)]
    pallas_call x0 -> x2, Pallas kernels: none -> 8.37 us  [the longest x1 5.92 us: split_pages(): pl.pallas_call(split_pages_kernel, grid_spec=pltpu.PrefetchScalarGridSpec...]
    dot_general x2 -> x0, matrix products: 7.88 us -> none  [the longest x1 7.56 us: attend_block(): jnp.einsum('hrt,thd->rhd', weight, values, preferred_element_type=jnp.flo...]
    gather x3 -> x0, local copies, waits for them, and re-layouts: 5.72 us -> none  [the longest x1 2.82 us: on_device(): kv_pool[served]]
  transfers between devices with their start and end apart: 3 -> 4, of which waited for: 3 -> 4; matrix products, arithmetic and copies ran while one was open for 4% -> 8% of each run, Pallas kernels for 0% -> 5%
where the time goes in v1:
time: 111 us; the launch traced here: 110 us
  waiting for transfers between devices  48.6 us (44%)
  starting transfers between devices  35.8 us (32%)
  local copies, waits for them, and re-layouts  8.83 us (8%)
  Pallas kernels  8.37 us (8%)
  other arithmetic  5.62 us (5%)
  matrix products  1.81 us (2%)
    all_to_all x4, waiting for transfers between devices, exchange(): return lax.all_to_all(array, axes, split_axis=0, concat_axis=0, tiled=True)  48.6 us
    all_to_all x4, starting transfers between devices, exchange(): return lax.all_to_all(array, axes, split_axis=0, concat_axis=0, tiled=True)  35.8 us
    pallas_call x1, Pallas kernels, split_pages(): pl.pallas_call(split_pages_kernel, grid_spec=pltpu.PrefetchScalarGridSpec...  5.92 us
    pallas_call x1, Pallas kernels, attend(): pl.pallas_call(functools.partial(attend_kernel, scale), in_specs=[pl.Bloc...  2.45 us
  transfers between devices with their start and end apart: 4, of which 4 were waited for; matrix products, arithmetic and copies ran while one was open for 8% of the time, Pallas kernels for 5%

profile of v1, /device:TPU:1, one launch (start us, length us, event | category | flops | bytes accessed | tf_op | source)
XLA Modules:
  0.0 110.0 jit_solution(9592046706049998693)
XLA Ops:
  0.8 0.7 fusion.15
  1.5 0.8 select_reduce_fusion.1
  2.5 0.7 broadcast_in_dim.13
  3.2 0.2 multiply_reduce_fusion.1
  3.6 0.6 broadcast_in_dim.14
  4.2 14.8 %all-to-all-start.1 = ((s32[64,1,128]{2,1,0:T(1,128)}), s32[64,1,128]{2,1,0:T(1,128)S(1)}, u32[]{:S(2)}, u32[]{:S(2)}) async-start(s32[64,1,128]{2,1,0:T(1,128)} %broadcast_in_dim.14), calls=%async_computation.1 | async-start | bytes 65536 | tf_op jit(solution)/shard_map/all_to_all | solution.py:20
  19.1 1.0 fusion.4
  20.1 0.6 copy-done.2
  20.8 7.6 %all-to-all-done.1 = s32[64,1,128]{2,1,0:T(1,128)S(1)} async-done(((s32[64,1,128]{2,1,0:T(1,128)}), s32[64,1,128]{2,1,0:T(1,128)S(1)}, u32[]{:S(2)}, u32[]{:S(2)}) %all-to-all-start.1) | async-done | bytes 32800 | tf_op jit(solution)/shard_map/all_to_all | solution.py:20
  28.4 0.8 broadcast_in_dim.10
  29.1 9.0 %all-to-all-start = ((bf16[64,16,128]{2,1,0:T(8,128)(2,1)}), bf16[64,16,128]{2,1,0:T(8,128)(2,1)S(1)}, u32[]{:S(2)}, u32[]{:S(2)}) async-start(bf16[64,16,128]{2,1,0:T(8,128)(2,1)} %bitcast.1), calls=%async_computation | async-start | bytes 524288 | tf_op jit(solution)/shard_map/all_to_all | solution.py:20
  38.2 0.1 reshape.118
  38.3 0.8 dynamic-slice_reduce_fusion.slot_ref
  39.1 5.9 %split_pages.1 = bf16[64,64,128]{2,1,0:T(8,128)(2,1)} custom-call(s32[8]{0:T(128)} %dynamic-slice_reduce_fusion.slot_ref, bf16[8,2,32,1024]{3,2,1,0:T(8,128)(2,1)} %page_ref.1), custom_call_target="tpu_custom_call" | custom-call | tf_op jit(solution)/shard_map/split_pages/pallas_call | solution.py:34
  45.0 6.3 %all-to-all-done = bf16[64,16,128]{2,1,0:T(8,128)(2,1)S(1)} async-done(((bf16[64,16,128]{2,1,0:T(8,128)(2,1)}), bf16[64,16,128]{2,1,0:T(8,128)(2,1)S(1)}, u32[]{:S(2)}, u32[]{:S(2)}) %all-to-all-start) | async-done | bytes 262176 | tf_op jit(solution)/shard_map/all_to_all | solution.py:20
  51.3 4.3 %all-to-all-start.2 = ((bf16[64,64,128]{2,1,0:T(8,128)(2,1)}), bf16[64,64,128]{2,1,0:T(8,128)(2,1)S(1)}, u32[]{:S(2)}, u32[]{:S(2)}) async-start(bf16[64,64,128]{2,1,0:T(8,128)(2,1)} %split_pages.1), calls=%async_computation.2 | async-start | bytes 2097152 | tf_op jit(solution)/shard_map/all_to_all | solution.py:20
  55.7 0.8 dynamic-slice_bitcast_fusion
  56.7 0.8 and.20
  57.5 1.0 and.21
  58.5 0.7 copy.62
  59.2 0.8 iota_compare_fusion
  60.0 0.7 lt.38
  60.6 0.7 and_convert_fusion.mask_ref
  61.3 22.5 %all-to-all-done.2.kv_ref = bf16[64,64,128]{2,1,0:T(8,128)(2,1)S(1)} async-done(((bf16[64,64,128]{2,1,0:T(8,128)(2,1)}), bf16[64,64,128]{2,1,0:T(8,128)(2,1)S(1)}, u32[]{:S(2)}, u32[]{:S(2)}) %all-to-all-start.2) | async-done | bytes 1048608 | tf_op jit(solution)/shard_map/all_to_all | solution.py:20
  83.8 2.5 %attend.1 = bf16[1024,128]{1,0:T(8,128)(2,1)S(1)} custom-call(bf16[1024,128]{1,0:T(8,128)(2,1)S(1)} %bitcast.57, bf16[64,64,128]{2,1,0:T(8,128)(2,1)S(1)} %all-to-all-done.2.kv_ref, bf16[8,2048]{1,0:T(8,128)(2,1)S(1)} %and_convert_fusion.mask_ref), custom_call_target="tpu_custom_call" | custom-call | tf_op jit(solution)/shard_map/attend/pallas_call | solution.py:73
  86.3 0.7 copy-done.1
  87.0 7.6 %all-to-all-start.3 = ((bf16[64,16,128]{2,1,0:T(8,128)(2,1)}), bf16[64,16,128]{2,1,0:T(8,128)(2,1)S(1)}, u32[]{:S(2)}, u32[]{:S(2)}) async-start(bf16[64,16,128]{2,1,0:T(8,128)(2,1)} %bitcast.58), calls=%async_computation.3 | async-start | bytes 524288 | tf_op jit(solution)/shard_map/all_to_all | solution.py:20
  94.6 0.8 multiply_bitcast_fusion
  95.6 12.2 %all-to-all-done.3 = bf16[64,16,128]{2,1,0:T(8,128)(2,1)S(1)} async-done(((bf16[64,16,128]{2,1,0:T(8,128)(2,1)}), bf16[64,16,128]{2,1,0:T(8,128)(2,1)S(1)}, u32[]{:S(2)}, u32[]{:S(2)}) %all-to-all-start.3) | async-done | bytes 262176 | tf_op jit(solution)/shard_map/all_to_all | solution.py:20
  107.8 0.2 fusion.17
  108.0 0.2 multiply_reduce_fusion
  108.2 1.8 %fusion = bf16[16,1024]{1,0:T(8,128)(2,1)} fusion(bf16[1024,1024]{1,0:T(8,128)(2,1)S(1)} %copy-done, bf16[16,1024]{1,0:T(8,128)(2,1)S(1)} %copy-done.4, bf16[16,4096]{1,0:T(8,128)(2,1)} %copy-done.2, f32[1024]{0:T(1024)S(1)} %copy-done.5, f32[16]{0:T(128)S(1)} %add_rsqrt_fusion, f32[16]{0:T(128)S(1)} %broadcast_multiply_fusion, ...), kind=kOutput, calls=%fused_computation.1 | convolution fusion | flops 33701888 | bytes 2265216 | tf_op jit(solution)/shard_map/dot_general | solution.py:146
  (30 shorter events, 0.9 us)
Async XLA Ops:
  0.0 108.2 %copy-start = (bf16[1024,1024]{1,0:T(8,128)(2,1)S(1)}, bf16[1024,1024]{1,0:T(8,128)(2,1)}, u32[]{:S(2)}) copy-start(bf16[1024,1024]{1,0:T(8,128)(2,1)} %param.17) | copy-start | bytes 6291460
  4.2 24.1 %all-to-all-start.1 = ((s32[64,1,128]{2,1,0:T(1,128)}), s32[64,1,128]{2,1,0:T(1,128)S(1)}, u32[]{:S(2)}, u32[]{:S(2)}) async-start(s32[64,1,128]{2,1,0:T(1,128)} %broadcast_in_dim.14), calls=%async_computation.1 | async-start | bytes 65536 | tf_op jit(solution)/shard_map/all_to_all | solution.py:20
  20.1 0.6 copy-start.2
  29.1 22.2 %all-to-all-start = ((bf16[64,16,128]{2,1,0:T(8,128)(2,1)}), bf16[64,16,128]{2,1,0:T(8,128)(2,1)S(1)}, u32[]{:S(2)}, u32[]{:S(2)}) async-start(bf16[64,16,128]{2,1,0:T(8,128)(2,1)} %bitcast.1), calls=%async_computation | async-start | bytes 524288 | tf_op jit(solution)/shard_map/all_to_all | solution.py:20
  38.3 13.0 %copy-start.3 = (s32[8,8,8,10]{3,2,1,0:T(8,128)}, s32[8,8,8,10]{3,2,1,0:T(8,128)S(1)}, u32[]{:S(2)}) copy-start(s32[8,8,8,10]{3,2,1,0:T(8,128)S(1)} %reshape.118) | copy-start | bytes 61444
  51.3 32.5 %all-to-all-start.2 = ((bf16[64,64,128]{2,1,0:T(8,128)(2,1)}), bf16[64,64,128]{2,1,0:T(8,128)(2,1)S(1)}, u32[]{:S(2)}, u32[]{:S(2)}) async-start(bf16[64,64,128]{2,1,0:T(8,128)(2,1)} %split_pages.1), calls=%async_computation.2 | async-start | bytes 2097152 | tf_op jit(solution)/shard_map/all_to_all | solution.py:20
  55.7 52.5 %copy-start.4 = (bf16[16,1024]{1,0:T(8,128)(2,1)S(1)}, bf16[16,1024]{1,0:T(8,128)(2,1)}, u32[]{:S(2)}) copy-start(bf16[16,1024]{1,0:T(8,128)(2,1)} %param.10) | copy-start | bytes 98308
  61.3 46.9 %copy-start.5 = (f32[1024]{0:T(1024)S(1)}, f32[1024]{0:T(1024)}, u32[]{:S(2)}) copy-start(f32[1024]{0:T(1024)} %param.16) | copy-start | bytes 12292
  86.3 0.7 copy-start.1
  87.0 20.8 %all-to-all-start.3 = ((bf16[64,16,128]{2,1,0:T(8,128)(2,1)}), bf16[64,16,128]{2,1,0:T(8,128)(2,1)S(1)}, u32[]{:S(2)}, u32[]{:S(2)}) async-start(bf16[64,16,128]{2,1,0:T(8,128)(2,1)} %bitcast.58), calls=%async_computation.3 | async-start | bytes 524288 | tf_op jit(solution)/shard_map/all_to_all | solution.py:20

commit v2 on v1

v2 whole, which is shorter than its diff:
```python
import functools

import jax
import jax.numpy as jnp
from jax import lax
from jax.experimental import pallas as pl
from jax.experimental.pallas import tpu as pltpu
from jax.sharding import Mesh
from jax.sharding import PartitionSpec as P

HEADS = 8
PAGE = 32
eps = 1e-05

PLANE = ("y", "x", "c")
SPREAD = ("z", "x", "c")

FIELDS = 16
LIVE, SLOT = 8, 9

VMEM = pl.BlockSpec(memory_space=pltpu.VMEM)
SMEM = pl.BlockSpec(memory_space=pltpu.SMEM)
HBM = pl.BlockSpec(memory_space=pl.ANY)


def exchange(array, axes):
    return lax.all_to_all(array, axes, split_axis=0, concat_axis=0, tiled=True)


def shift(array, axis, step):
    n = lax.axis_size(axis)
    return lax.ppermute(array, axis, [(i, (i + step) % n) for i in range(n)])


def silu(value):
    half = value * 0.5
    return half + half * jnp.tanh(half)


def announce_kernel(place_ref, owner_ref, slot_ref, length_ref, seen_ref, q_ref, out_ref):
    rows = q_ref.shape[0]
    pages = owner_ref.shape[0]
    tiles, blocks = seen_ref.shape
    hd = out_ref.shape[2]
    lane = lax.broadcasted_iota(jnp.int32, (8, hd), 1)
    owner, field = lane // FIELDS, lane % FIELDS
    seen = []
    for b in range(blocks):
        row = jnp.zeros((8, hd), jnp.int32)
        for t in range(tiles):
            row = jnp.where(field == t, seen_ref[t, b], row)
        seen.append(row)
    info = jnp.zeros((8, hd), jnp.int32)
    for j in range(pages):
        live = jnp.clip(length_ref[0] - (place_ref[0] * pages + j) * PAGE, 0, PAGE)
        row = jnp.where(field == LIVE, live, seen[j * blocks // pages])
        row = jnp.where(field == SLOT, slot_ref[j], row)
        info = jnp.where(owner == owner_ref[j], row, info)
    info = info.astype(jnp.float32).astype(jnp.bfloat16)
    query = silu(q_ref[...].astype(jnp.float32)).astype(jnp.bfloat16)
    for h in range(HEADS):
        chunk = jnp.concatenate([query[:, h * hd : (h + 1) * hd], info], axis=0)
        for z in range(out_ref.shape[0] // HEADS):
            out_ref[z * HEADS + h] = chunk


def announce(place, owners, slots, lengths, seen, cand_proj, users):
    rows, width = cand_proj.shape[0], cand_proj.shape[1] // 4
    hd = width // HEADS
    return pl.pallas_call(
        announce_kernel,
        grid=(1,),
        in_specs=[SMEM] * 5 + [pl.BlockSpec((rows, width), lambda i: (0, 2))],
        out_specs=VMEM,
        out_shape=jax.ShapeDtypeStruct((users * HEADS, rows + 8, hd), jnp.bfloat16),
        name="announce",
    )(place, owners, slots, lengths, seen, cand_proj)


def split_pages_kernel(slot_ref, pool_ref, out_ref, sems):
    hd = out_ref.shape[3]
    copies = []
    for u in range(slot_ref.shape[0]):
        for h in range(HEADS):
            copies.append(
                pltpu.make_async_copy(
                    pool_ref.at[slot_ref[u], :, :, pl.ds(h * hd, hd)],
                    out_ref.at[u * HEADS + h],
                    sems.at[u * HEADS + h],
                )
            )
    for copy in copies:
        copy.start()
    for copy in copies:
        copy.wait()


def split_pages(slots, kv_pool):
    _, _, page, width = kv_pool.shape
    users = slots.shape[0]
    return pl.pallas_call(
        split_pages_kernel,
        in_specs=[SMEM, HBM],
        out_specs=HBM,
        out_shape=jax.ShapeDtypeStruct((users * HEADS, 2, page, width // HEADS), kv_pool.dtype),
        scratch_shapes=[pltpu.SemaphoreType.DMA((users * HEADS,))],
        name="split_pages",
    )(slots, kv_pool)


STEPS = (0, -1, 1, -3, -4, -2, 3, 2)


def gather_queries(row):
    below, above = shift(row, "y", 1), shift(row, "y", -1)
    below3 = shift(jnp.concatenate([row, below, above]), "y", 3)
    above3 = shift(jnp.concatenate([row, below]), "y", -3)
    return row, below, above, below3, above3


def attend_kernel(scale, y_ref, info_ref, kv_ref, *rest):
    pieces, (out_ref, q_ref, acc_ref) = rest[:-3], rest[-3:]
    hd = out_ref.shape[1]
    sources, tiles = info_ref.shape[0], len(STEPS)
    span = sources * PAGE
    height = out_ref.shape[0] // tiles
    y = y_ref[0]
    place = 0
    for piece in pieces:
        for b in range(piece.shape[0] // height):
            to = lax.rem(y + (STEPS[place] + tiles), tiles)
            q_ref[pl.ds(to * height, height), :] = piece[b * height : (b + 1) * height, :]
            place += 1
    place = lax.broadcasted_iota(jnp.int32, (sources, span), 1)
    which = lax.broadcasted_iota(jnp.int32, (sources, span), 0)
    spread = (place // PAGE == which).astype(jnp.bfloat16)
    fields = lax.dot_general(
        info_ref[...], spread, (((0,), (0,)), ((), ())), preferred_element_type=jnp.float32
    )
    within = lax.rem(lax.broadcasted_iota(jnp.int32, (1, span), 1), PAGE).astype(jnp.float32)
    q = q_ref[...]
    for o in range(kv_ref.shape[0] // sources):
        keys = kv_ref[o * sources : (o + 1) * sources, 0].reshape(span, hd)
        values = kv_ref[o * sources : (o + 1) * sources, 1].reshape(span, hd)
        seen = fields[o * FIELDS : o * FIELDS + tiles]
        live = fields[o * FIELDS + LIVE : o * FIELDS + LIVE + 1]
        allowed = jnp.where(within < live, seen, 0.0).astype(jnp.bfloat16)
        score = lax.dot_general(q, keys, (((1,), (1,)), ((), ())), preferred_element_type=jnp.float32)
        weight = silu(score * scale).astype(jnp.bfloat16)
        weight = weight.reshape(tiles, height, span) * allowed[:, None, :]
        part = jnp.dot(weight.reshape(tiles * height, span), values, preferred_element_type=jnp.float32)
        if o == 0:
            acc_ref[...] = part
        else:
            acc_ref[...] += part
    out_ref[...] = acc_ref[...].astype(out_ref.dtype)


def attend(y, info, pages, pieces, scale):
    rows, hd = sum(piece.shape[0] for piece in pieces), pages.shape[-1]
    return pl.pallas_call(
        functools.partial(attend_kernel, scale),
        in_specs=[SMEM] + [VMEM] * (2 + len(pieces)),
        out_specs=VMEM,
        out_shape=jax.ShapeDtypeStruct((rows, hd), jnp.bfloat16),
        scratch_shapes=[pltpu.VMEM((rows, hd), jnp.bfloat16), pltpu.VMEM((rows, hd), jnp.float32)],
        compiler_params=pltpu.CompilerParams(vmem_limit_bytes=40 * 1024 * 1024),
        name="attend",
    )(y, info, pages, *pieces)


def finish_kernel(scale, back_ref, proj_ref, input_ref, gain_ref, weight_ref, out_ref):
    rows, width = input_ref.shape
    hd = width // HEADS

    def act(block, h):
        start = block * width + h * hd
        value = silu(proj_ref[:, start : start + hd].astype(jnp.float32))
        return value.astype(jnp.bfloat16).astype(jnp.float32)

    attn = []
    for h in range(HEADS):
        total = jnp.zeros((rows, hd), jnp.float32)
        for g in range(back_ref.shape[0] // HEADS):
            total += back_ref[g * HEADS + h].astype(jnp.float32)
        own = silu(jnp.sum(act(2, h) * act(3, h), axis=1, keepdims=True) * scale)
        own = own.astype(jnp.bfloat16).astype(jnp.float32)
        attn.append(total + own * act(1, h))
    attn = jnp.concatenate(attn, axis=1)
    mean = jnp.mean(attn, axis=1, keepdims=True)
    centered = attn - mean
    var = jnp.mean(centered * centered, axis=1, keepdims=True)
    u_act = jnp.concatenate([act(0, h) for h in range(HEADS)], axis=1)
    normed = (centered * lax.rsqrt(var + eps) * gain_ref[...] * u_act).astype(jnp.bfloat16)
    out = jnp.dot(normed, weight_ref[...], preferred_element_type=jnp.float32)
    out_ref[...] = (input_ref[...].astype(jnp.float32) + out).astype(out_ref.dtype)


def finish(back, cand_proj, cand_input, out_gain, out_weight, scale):
    return pl.pallas_call(
        functools.partial(finish_kernel, scale),
        in_specs=[VMEM] * 5,
        out_specs=VMEM,
        out_shape=jax.ShapeDtypeStruct(cand_input.shape, cand_input.dtype),
        compiler_params=pltpu.CompilerParams(vmem_limit_bytes=40 * 1024 * 1024),
        name="finish",
    )(back, cand_proj, cand_input, out_gain.reshape(1, -1), out_weight)


def on_device(
    cand_proj, cand_input, kv_pool, page_owner, page_slot, lengths, block_mask, out_gain, out_weight
):
    rows, width = cand_input.shape
    hd = width // HEADS
    scale = hd ** (-0.5)
    n_z = lax.axis_size("z")
    z, y, h = lax.axis_index("z"), lax.axis_index("y"), lax.axis_index(("x", "c"))
    place = lax.axis_index(PLANE)

    sent = announce(
        place.reshape(1), page_owner.reshape(-1), page_slot.reshape(-1), lengths, block_mask[0], cand_proj, n_z
    )
    told = exchange(sent, SPREAD).reshape(n_z, HEADS, rows + 8, hd)
    to_me = lax.dynamic_slice(told, (0, h, rows, z * FIELDS + SLOT), (n_z, 1, 1, 1)).reshape(-1)
    slots = jnp.clip(to_me.astype(jnp.int32), 0, kv_pool.shape[0] - 1)
    pages = split_pages(slots, kv_pool)
    pages, told = lax.optimization_barrier((pages, told))
    got = exchange(pages, SPREAD)
    mine = lax.dynamic_index_in_dim(told, z, 0, keepdims=False)
    pieces = gather_queries(mine[:, :rows].reshape(-1, hd))
    part = attend(y.reshape(1), mine[:, rows], got, pieces, scale)
    back = exchange(part.reshape(-1, rows, hd), PLANE)
    return finish(back, cand_proj, cand_input, out_gain, out_weight, scale)


def solution(mesh):
    n_z, n_p = mesh.shape["batch"], mesh.shape["pos"]
    cores, n_x = 2, HEADS // 2
    grid = Mesh(mesh.devices.reshape(n_z, n_p // HEADS, n_x, cores), ("z", "y", "x", "c"))
    rows = P(("z", "y", "x", "c"), None)
    placed = (
        rows,
        rows,
        P("z", None, PLANE, None),
        P("z", PLANE, None),
        P("z", PLANE, None),
        P("z"),
        P("z", None, PLANE),
        P(),
        P(),
    )
    return jax.shard_map(on_device, mesh=grid, in_specs=placed, out_specs=rows, check_vma=False)
```

time: 111 us -> 131 us (1.18)
  Pallas kernels: 8.37 us -> 39.4 us
  blocking collectives: 0 us -> 24.4 us
  waiting for transfers between devices: 48.6 us -> 25.9 us
  local copies, waits for them, and re-layouts: 8.83 us -> 2.78 us
  other arithmetic: 5.62 us -> 0.54 us
  matrix products: 1.81 us -> 0 us
    pallas_call x2 -> x4, Pallas kernels: 8.37 us -> 39.4 us  [the longest x1 34.1 us: split_pages(): pl.pallas_call(split_pages_kernel, in_specs=[SMEM, HBM], out_specs=HBM, o...]
    all_to_all x4 -> x2, waiting for transfers between devices: 48.6 us -> 20.9 us  [exchange(): return lax.all_to_all(array, axes, split_axis=0, concat_axis=0, tiled=True)]
    all_to_all x0 -> x1, blocking collectives: none -> 24.4 us  [exchange(): return lax.all_to_all(array, axes, split_axis=0, concat_axis=0, tiled=True)]
    ppermute x0 -> x4, starting transfers between devices: none -> 15.8 us  [shift(): return lax.ppermute(array, axis, [(i, (i + step) % n) for i in range(n)])]
    all_to_all x4 -> x2, starting transfers between devices: 35.8 us -> 20.4 us  [exchange(): return lax.all_to_all(array, axes, split_axis=0, concat_axis=0, tiled=True)]
    ppermute x0 -> x4, waiting for transfers between devices: none -> 4.98 us  [shift(): return lax.ppermute(array, axis, [(i, (i + step) % n) for i in range(n)])]
    convert_element_type x4 -> x0, other arithmetic: 2.35 us -> none  [the longest x1 0.99 us: on_device(): act = jax.nn.silu(cand_proj.astype(jnp.float32)).astype(jnp.bfloat16)]
    broadcast_in_dim x5 -> x0, local copies, waits for them, and re-layouts: 2.24 us -> none  [the longest x1 0.75 us: on_device(): jnp.broadcast_to(by_head[None], (n_y, HEADS, rows, hd))]
  transfers between devices with their start and end apart: 4 -> 6, of which waited for: 4 -> 3; matrix products, arithmetic and copies ran while one was open for 8% -> 1% of each run, Pallas kernels for 5% -> 0%
where the time goes in v2:
time: 131 us; the launch traced here: 130 us
  Pallas kernels  39.4 us (30%)
  starting transfers between devices  36.2 us (28%)
  waiting for transfers between devices  25.9 us (20%)
  blocking collectives  24.4 us (19%)
  local copies, waits for them, and re-layouts  2.78 us (2%)
    pallas_call x1, Pallas kernels, split_pages(): pl.pallas_call(split_pages_kernel, in_specs=[SMEM, HBM], out_specs=HBM, o...  34.1 us
    all_to_all x1, blocking collectives, exchange(): return lax.all_to_all(array, axes, split_axis=0, concat_axis=0, tiled=True)  24.4 us
    all_to_all x2, waiting for transfers between devices, exchange(): return lax.all_to_all(array, axes, split_axis=0, concat_axis=0, tiled=True)  20.9 us
    all_to_all x2, starting transfers between devices, exchange(): return lax.all_to_all(array, axes, split_axis=0, concat_axis=0, tiled=True)  20.4 us
    ppermute x4, starting transfers between devices, shift(): return lax.ppermute(array, axis, [(i, (i + step) % n) for i in range(n)])  15.8 us
    ppermute x4, waiting for transfers between devices, shift(): return lax.ppermute(array, axis, [(i, (i + step) % n) for i in range(n)])  4.98 us
  transfers between devices with their start and end apart: 6, of which 3 were waited for; matrix products, arithmetic and copies ran while one was open for 1% of the time, Pallas kernels for 0%

profile of v2, /device:TPU:1, one launch (start us, length us, event | category | flops | bytes accessed | tf_op | source)
XLA Modules:
  0.0 130.1 jit_solution(175210808939297073)
XLA Ops:
  0.7 1.3 %copy.10.seen_ref = s32[8,2]{1,0:T(8,128)} copy(s32[8,2]{0,1:T(2,128)} %bitcast.24) | data formatting | bytes 128 | tf_op jit(solution)/shard_map/squeeze | solution.py:221
  2.0 1.6 %announce.1 = bf16[64,24,128]{2,1,0:T(8,128)(2,1)} custom-call(s32[1]{0:T(128)} %bitcast.1.place_ref, s32[8]{0:T(128)} %bitcast.25, s32[8]{0:T(128)} %bitcast.26, s32[1]{0:T(128)S(6)} %copy.15.length_ref, s32[8,2]{1,0:T(8,128)} %copy.10.seen_ref, bf16[16,4096]{1,0:T(8,128)(2,1)} %proj_ref.1), custom_call_target="tpu_custom_call" | custom-call | tf_op jit(solution)/shard_map/announce/pallas_call | solution.py:70
  3.6 14.8 %all-to-all-start = ((bf16[64,24,128]{2,1,0:T(8,128)(2,1)}), bf16[64,24,128]{2,1,0:T(8,128)(2,1)S(1)}, u32[]{:S(2)}, u32[]{:S(2)}) async-start(bf16[64,24,128]{2,1,0:T(8,128)(2,1)} %announce.1), calls=%async_computation | async-start | bytes 786432 | tf_op jit(solution)/shard_map/all_to_all | solution.py:27
  18.4 15.1 %all-to-all-done = bf16[64,24,128]{2,1,0:T(8,128)(2,1)S(1)} async-done(((bf16[64,24,128]{2,1,0:T(8,128)(2,1)}), bf16[64,24,128]{2,1,0:T(8,128)(2,1)S(1)}, u32[]{:S(2)}, u32[]{:S(2)}) %all-to-all-start) | async-done | bytes 393248 | tf_op jit(solution)/shard_map/all_to_all | solution.py:27
  33.5 0.0 copy-start.4
  33.5 0.1 constant_dynamic-slice_fusion
  33.6 0.1 copy.14
  33.6 0.5 clamp_bitcast_fusion.slot_ref
  34.2 34.1 %split_pages.1 = bf16[64,2,32,128]{3,2,1,0:T(8,128)(2,1)} custom-call(s32[8]{0:T(128)} %clamp_bitcast_fusion.slot_ref, bf16[8,2,32,1024]{3,2,1,0:T(8,128)(2,1)} %pool_ref.1), custom_call_target="tpu_custom_call" | custom-call | tf_op jit(solution)/shard_map/split_pages/pallas_call | solution.py:101
  68.3 0.0 copy-done.4
  68.3 5.6 %all-to-all-start.1 = ((bf16[64,2,32,128]{3,2,1,0:T(8,128)(2,1)}), bf16[64,2,32,128]{3,2,1,0:T(8,128)(2,1)S(1)}, u32[]{:S(2)}, u32[]{:S(2)}) async-start(bf16[64,2,32,128]{3,2,1,0:T(8,128)(2,1)} %split_pages.1), calls=%async_computation.1 | async-start | bytes 2097152 | tf_op jit(solution)/shard_map/all_to_all | solution.py:27
  73.9 0.0 copy-start
  73.9 0.0 copy-start.1
  73.9 0.0 copy-start.3
  73.9 1.2 copy.12
  75.2 3.2 %collective-permute-start = (bf16[128,128]{1,0:T(8,128)(2,1)S(1)}, bf16[128,128]{1,0:T(8,128)(2,1)S(1)}, u32[]{:S(2)}, u32[]{:S(2)}) collective-permute-start(bf16[128,128]{1,0:T(8,128)(2,1)S(1)} %bitcast.16), channel_id=1, source_target_pairs={{0,8},{8,16},{16,24},{24,32},{32,40},{40,48},{48,56},{56,0},{1,9},... | collective-permute-start | bytes 98312 | tf_op jit(solution)/shard_map/ppermute | solution.py:32
  78.4 3.8 %collective-permute-start.1 = (bf16[128,128]{1,0:T(8,128)(2,1)S(1)}, bf16[128,128]{1,0:T(8,128)(2,1)S(1)}, u32[]{:S(2)}, u32[]{:S(2)}) collective-permute-start(bf16[128,128]{1,0:T(8,128)(2,1)S(1)} %bitcast.17), channel_id=1, source_target_pairs={{0,56},{8,0},{16,8},{24,16},{32,24},{40,32},{48,40},{56,48},{1,57}... | collective-permute-start | bytes 98312 | tf_op jit(solution)/shard_map/ppermute | solution.py:32
  82.2 0.0 collective-permute-done.rest_1_
  82.3 4.9 %collective-permute-start.3 = (bf16[256,128]{1,0:T(8,128)(2,1)S(1)}, bf16[256,128]{1,0:T(8,128)(2,1)S(1)}, u32[]{:S(2)}, u32[]{:S(2)}) collective-permute-start(bf16[256,128]{1,0:T(8,128)(2,1)S(1)} %pad_maximum_fusion.1), channel_id=1, source_target_pairs={{0,40},{8,48},{16,56},{24,0},{32,8},{40,16},{48,24},{56,32},{1,41}... | collective-permute-start | bytes 196616 | tf_op jit(solution)/shard_map/ppermute | solution.py:32
  87.2 0.0 collective-permute-done.1.rest_2_
  87.2 3.8 %collective-permute-start.2 = (bf16[384,128]{1,0:T(8,128)(2,1)S(1)}, bf16[384,128]{1,0:T(8,128)(2,1)S(1)}, u32[]{:S(2)}, u32[]{:S(2)}) collective-permute-start(bf16[384,128]{1,0:T(8,128)(2,1)S(1)} %pad_maximum_fusion), channel_id=1, source_target_pairs={{0,24},{8,32},{16,40},{24,48},{32,56},{40,0},{48,8},{56,16},{1,25}... | collective-permute-start | bytes 294920 | tf_op jit(solution)/shard_map/ppermute | solution.py:32
  91.0 0.0 collective-permute-done.3.rest_4_
  91.1 5.0 %collective-permute-done.2.rest_3_ = bf16[384,128]{1,0:T(8,128)(2,1)S(1)} collective-permute-done((bf16[384,128]{1,0:T(8,128)(2,1)S(1)}, bf16[384,128]{1,0:T(8,128)(2,1)S(1)}, u32[]{:S(2)}, u32[]{:S(2)}) %collective-permute-start.2) | collective-permute-done | bytes 98336 | tf_op jit(solution)/shard_map/ppermute | solution.py:32
  96.0 5.9 %all-to-all-done.1.kv_ref = bf16[64,2,32,128]{3,2,1,0:T(8,128)(2,1)S(1)} async-done(((bf16[64,2,32,128]{3,2,1,0:T(8,128)(2,1)}), bf16[64,2,32,128]{3,2,1,0:T(8,128)(2,1)S(1)}, u32[]{:S(2)}, u32[]{:S(2)}) %all-to-all-start.1) | async-done | bytes 1048608 | tf_op jit(solution)/shard_map/all_to_all | solution.py:27
  101.9 0.0 copy-start.2
  101.9 2.5 %attend.1 = bf16[1024,128]{1,0:T(8,128)(2,1)S(1)} custom-call(s32[1]{0:T(128)} %bitcast.y_ref, bf16[8,128]{1,0:T(8,128)(2,1)S(1)} %slice_bitcast_fusion.info_ref, bf16[64,2,32,128]{3,2,1,0:T(8,128)(2,1)S(1)} %all-to-all-done.1.kv_ref, bf16[128,128]{1,0:T(8,128)(2,1)S(1)} %bitcast.20, bf16[128,128]{1,0:T(8,128)(2,1)S(1)} %collective-permute-done.rest_1_, ...), custom_call_target="tpu_custom_call" | custom-call | tf_op jit(solution)/shard_map/attend/pallas_call | solution.py:161
  104.4 24.4 %all_to_all.15.back_ref = bf16[64,16,128]{2,1,0:T(8,128)(2,1)S(1)} all-to-all(bf16[64,16,128]{2,1,0:T(8,128)(2,1)S(1)} %bitcast.15), channel_id=1, replica_groups=mesh['z'=8,'y'=8,'x'=4,'c'=2] {'y','x','c'}, dimensions={0} | all-to-all | bytes 524288 | tf_op jit(solution)/shard_map/all_to_all | solution.py:27
  128.8 0.0 copy-done
  128.8 0.0 copy-done.1
  128.8 0.0 copy-done.3
  128.8 0.0 copy-done.2
  128.8 1.3 finish.1
  (6 shorter events, 0.0 us)
Async XLA Ops:
  3.6 29.9 %all-to-all-start = ((bf16[64,24,128]{2,1,0:T(8,128)(2,1)}), bf16[64,24,128]{2,1,0:T(8,128)(2,1)S(1)}, u32[]{:S(2)}, u32[]{:S(2)}) async-start(bf16[64,24,128]{2,1,0:T(8,128)(2,1)} %announce.1), calls=%async_computation | async-start | bytes 786432 | tf_op jit(solution)/shard_map/all_to_all | solution.py:27
  33.5 34.8 %copy-start.4 = (bf16[64,24,128]{2,1,0:T(8,128)(2,1)}, bf16[64,24,128]{2,1,0:T(8,128)(2,1)S(1)}, u32[]{:S(2)}) copy-start(bf16[64,24,128]{2,1,0:T(8,128)(2,1)S(1)} %all-to-all-done) | copy-start | bytes 1179652
  68.3 33.6 %all-to-all-start.1 = ((bf16[64,2,32,128]{3,2,1,0:T(8,128)(2,1)}), bf16[64,2,32,128]{3,2,1,0:T(8,128)(2,1)S(1)}, u32[]{:S(2)}, u32[]{:S(2)}) async-start(bf16[64,2,32,128]{3,2,1,0:T(8,128)(2,1)} %split_pages.1), calls=%async_computation.1 | async-start | bytes 2097152 | tf_op jit(solution)/shard_map/all_to_all | solution.py:27
  73.9 54.9 %copy-start = (bf16[1024,1024]{1,0:T(8,128)(2,1)S(1)}, bf16[1024,1024]{1,0:T(8,128)(2,1)}, u32[]{:S(2)}) copy-start(bf16[1024,1024]{1,0:T(8,128)(2,1)} %weight_ref.1) | copy-start | bytes 6291460
  73.9 54.9 %copy-start.1 = (bf16[16,4096]{1,0:T(8,128)(2,1)S(1)}, bf16[16,4096]{1,0:T(8,128)(2,1)}, u32[]{:S(2)}) copy-start(bf16[16,4096]{1,0:T(8,128)(2,1)} %proj_ref.1) | copy-start | bytes 393220
  73.9 54.9 %copy-start.3 = (f32[1024]{0:T(1024)S(1)}, f32[1024]{0:T(1024)}, u32[]{:S(2)}) copy-start(f32[1024]{0:T(1024)} %param.16) | copy-start | bytes 12292
  75.2 7.0 %collective-permute-start = (bf16[128,128]{1,0:T(8,128)(2,1)S(1)}, bf16[128,128]{1,0:T(8,128)(2,1)S(1)}, u32[]{:S(2)}, u32[]{:S(2)}) collective-permute-start(bf16[128,128]{1,0:T(8,128)(2,1)S(1)} %bitcast.16), channel_id=1, source_target_pairs={{0,8},{8,16},{16,24},{24,32},{32,40},{40,48},{48,56},{56,0},{1,9},... | collective-permute-start | bytes 98312 | tf_op jit(solution)/shard_map/ppermute | solution.py:32
  78.4 8.8 %collective-permute-start.1 = (bf16[128,128]{1,0:T(8,128)(2,1)S(1)}, bf16[128,128]{1,0:T(8,128)(2,1)S(1)}, u32[]{:S(2)}, u32[]{:S(2)}) collective-permute-start(bf16[128,128]{1,0:T(8,128)(2,1)S(1)} %bitcast.17), channel_id=1, source_target_pairs={{0,56},{8,0},{16,8},{24,16},{32,24},{40,32},{48,40},{56,48},{1,57}... | collective-permute-start | bytes 98312 | tf_op jit(solution)/shard_map/ppermute | solution.py:32
  82.3 8.8 %collective-permute-start.3 = (bf16[256,128]{1,0:T(8,128)(2,1)S(1)}, bf16[256,128]{1,0:T(8,128)(2,1)S(1)}, u32[]{:S(2)}, u32[]{:S(2)}) collective-permute-start(bf16[256,128]{1,0:T(8,128)(2,1)S(1)} %pad_maximum_fusion.1), channel_id=1, source_target_pairs={{0,40},{8,48},{16,56},{24,0},{32,8},{40,16},{48,24},{56,32},{1,41}... | collective-permute-start | bytes 196616 | tf_op jit(solution)/shard_map/ppermute | solution.py:32
  87.2 8.8 %collective-permute-start.2 = (bf16[384,128]{1,0:T(8,128)(2,1)S(1)}, bf16[384,128]{1,0:T(8,128)(2,1)S(1)}, u32[]{:S(2)}, u32[]{:S(2)}) collective-permute-start(bf16[384,128]{1,0:T(8,128)(2,1)S(1)} %pad_maximum_fusion), channel_id=1, source_target_pairs={{0,24},{8,32},{16,40},{24,48},{32,56},{40,0},{48,8},{56,16},{1,25}... | collective-permute-start | bytes 294920 | tf_op jit(solution)/shard_map/ppermute | solution.py:32
  101.9 26.9 %copy-start.2 = (bf16[16,1024]{1,0:T(8,128)(2,1)S(1)}, bf16[16,1024]{1,0:T(8,128)(2,1)}, u32[]{:S(2)}) copy-start(bf16[16,1024]{1,0:T(8,128)(2,1)} %input_ref.1) | copy-start | bytes 98308

commit v3 on v2

--- a/solution.py
+++ b/solution.py
@@ -38,30 +38,29 @@
 
 
 def announce_kernel(place_ref, owner_ref, slot_ref, length_ref, seen_ref, q_ref, out_ref):
-    rows = q_ref.shape[0]
+    rows, hd = out_ref.shape[1:]
     pages = owner_ref.shape[0]
     tiles, blocks = seen_ref.shape
-    hd = out_ref.shape[2]
-    lane = lax.broadcasted_iota(jnp.int32, (8, hd), 1)
+    lane = lax.broadcasted_iota(jnp.int32, (rows, hd), 1)
     owner, field = lane // FIELDS, lane % FIELDS
     seen = []
     for b in range(blocks):
-        row = jnp.zeros((8, hd), jnp.int32)
+        row = jnp.zeros((rows, hd), jnp.int32)
         for t in range(tiles):
-            row = jnp.where(field == t, seen_ref[t, b], row)
+            row = jnp.where(field == t, seen_ref[t : t + 1, b : b + 1], row)
         seen.append(row)
-    info = jnp.zeros((8, hd), jnp.int32)
+    info = jnp.zeros((rows, hd), jnp.int32)
     for j in range(pages):
-        live = jnp.clip(length_ref[0] - (place_ref[0] * pages + j) * PAGE, 0, PAGE)
+        live = jnp.clip(length_ref[0] - (place_ref[1] * pages + j) * PAGE, 0, PAGE)
         row = jnp.where(field == LIVE, live, seen[j * blocks // pages])
         row = jnp.where(field == SLOT, slot_ref[j], row)
         info = jnp.where(owner == owner_ref[j], row, info)
     info = info.astype(jnp.float32).astype(jnp.bfloat16)
+    for i in range(out_ref.shape[0]):
+        out_ref[i] = info
     query = silu(q_ref[...].astype(jnp.float32)).astype(jnp.bfloat16)
     for h in range(HEADS):
-        chunk = jnp.concatenate([query[:, h * hd : (h + 1) * hd], info], axis=0)
-        for z in range(out_ref.shape[0] // HEADS):
-            out_ref[z * HEADS + h] = chunk
+        out_ref[place_ref[0] * HEADS + h] = query[:, h * hd : (h + 1) * hd]
 
 
 def announce(place, owners, slots, lengths, seen, cand_proj, users):
@@ -70,27 +69,22 @@
     return pl.pallas_call(
         announce_kernel,
         grid=(1,),
-        in_specs=[SMEM] * 5 + [pl.BlockSpec((rows, width), lambda i: (0, 2))],
+        in_specs=[SMEM] * 4 + [VMEM, pl.BlockSpec((rows, width), lambda i: (0, 2))],
         out_specs=VMEM,
-        out_shape=jax.ShapeDtypeStruct((users * HEADS, rows + 8, hd), jnp.bfloat16),
+        out_shape=jax.ShapeDtypeStruct((users * HEADS, rows, hd), jnp.bfloat16),
         name="announce",
     )(place, owners, slots, lengths, seen, cand_proj)
 
 
-def split_pages_kernel(slot_ref, pool_ref, out_ref, sems):
+def split_pages_kernel(slot_ref, pool_ref, out_ref, split_ref, sems):
     hd = out_ref.shape[3]
     copies = []
     for u in range(slot_ref.shape[0]):
         for h in range(HEADS):
-            copies.append(
-                pltpu.make_async_copy(
-                    pool_ref.at[slot_ref[u], :, :, pl.ds(h * hd, hd)],
-                    out_ref.at[u * HEADS + h],
-                    sems.at[u * HEADS + h],
-                )
-            )
-    for copy in copies:
-        copy.start()
+            split_ref[u * HEADS + h] = pool_ref[slot_ref[u], :, :, h * hd : (h + 1) * hd]
+        part = pl.ds(u * HEADS, HEADS)
+        copies.append(pltpu.make_async_copy(split_ref.at[part], out_ref.at[part], sems.at[u]))
+        copies[-1].start()
     for copy in copies:
         copy.wait()
 
@@ -98,12 +92,13 @@
 def split_pages(slots, kv_pool):
     _, _, page, width = kv_pool.shape
     users = slots.shape[0]
+    out = jax.ShapeDtypeStruct((users * HEADS, 2, page, width // HEADS), kv_pool.dtype)
     return pl.pallas_call(
         split_pages_kernel,
-        in_specs=[SMEM, HBM],
+        in_specs=[SMEM, VMEM],
         out_specs=HBM,
-        out_shape=jax.ShapeDtypeStruct((users * HEADS, 2, page, width // HEADS), kv_pool.dtype),
-        scratch_shapes=[pltpu.SemaphoreType.DMA((users * HEADS,))],
+        out_shape=out,
+        scratch_shapes=[pltpu.VMEM(out.shape, out.dtype), pltpu.SemaphoreType.DMA((users,))],
         name="split_pages",
     )(slots, kv_pool)
 
@@ -215,20 +210,21 @@
     scale = hd ** (-0.5)
     n_z = lax.axis_size("z")
     z, y, h = lax.axis_index("z"), lax.axis_index("y"), lax.axis_index(("x", "c"))
-    place = lax.axis_index(PLANE)
-
-    sent = announce(
-        place.reshape(1), page_owner.reshape(-1), page_slot.reshape(-1), lengths, block_mask[0], cand_proj, n_z
-    )
-    told = exchange(sent, SPREAD).reshape(n_z, HEADS, rows + 8, hd)
-    to_me = lax.dynamic_slice(told, (0, h, rows, z * FIELDS + SLOT), (n_z, 1, 1, 1)).reshape(-1)
-    slots = jnp.clip(to_me.astype(jnp.int32), 0, kv_pool.shape[0] - 1)
-    pages = split_pages(slots, kv_pool)
+    place = jnp.stack([z, lax.axis_index(PLANE)])
+    owners, own_slots = page_owner.reshape(-1), page_slot.reshape(-1)
+
+    sent = announce(place, owners, own_slots, lengths, block_mask[0], cand_proj, n_z)
+    told = exchange(sent, SPREAD).reshape(n_z, HEADS, rows, hd)
+    to_me = lax.dynamic_slice(told, (0, h, 0, z * FIELDS + SLOT), (n_z, 1, 1, 1)).reshape(-1)
+    at_home = jnp.sum(jnp.where(owners == z, own_slots, 0))
+    slots = jnp.where(jnp.arange(n_z) == z, at_home, to_me.astype(jnp.int32))
+    pages = split_pages(jnp.clip(slots, 0, kv_pool.shape[0] - 1), kv_pool)
     pages, told = lax.optimization_barrier((pages, told))
     got = exchange(pages, SPREAD)
-    mine = lax.dynamic_index_in_dim(told, z, 0, keepdims=False)
-    pieces = gather_queries(mine[:, :rows].reshape(-1, hd))
-    part = attend(y.reshape(1), mine[:, rows], got, pieces, scale)
+    below = lax.dynamic_slice(told, ((z + n_z - 1) % n_z, 0, 0, 0), (1, HEADS, 1, hd)).reshape(HEADS, hd)
+    info = shift(below, "z", -1)
+    pieces = gather_queries(lax.dynamic_index_in_dim(told, z, 0, keepdims=False).reshape(-1, hd))
+    part = attend(y.reshape(1), info, got, pieces, scale)
     back = exchange(part.reshape(-1, rows, hd), PLANE)
     return finish(back, cand_proj, cand_input, out_gain, out_weight, scale)
 

time: 131 us -> 97.7 us (0.75)
  Pallas kernels: 39.4 us -> 7.68 us
  waiting for transfers between devices: 25.9 us -> 17.4 us
  starting transfers between devices: 36.2 us -> 40.2 us
  other arithmetic: 0.54 us -> 3.14 us
    pallas_call x2, Pallas kernels: 35.7 us -> 3.92 us  [the longest x1 2.3 us: split_pages(): pl.pallas_call(split_pages_kernel, in_specs=[SMEM, VMEM], out_specs=HBM,...]
    all_to_all x2, waiting for transfers between devices: 20.9 us -> 15.4 us  [exchange(): return lax.all_to_all(array, axes, split_axis=0, concat_axis=0, tiled=True)]
    ppermute x4 -> x5, starting transfers between devices: 15.8 us -> 20.5 us  [shift(): return lax.ppermute(array, axis, [(i, (i + step) % n) for i in range(n)])]
    ppermute x4 -> x5, waiting for transfers between devices: 4.98 us -> 2.04 us  [shift(): return lax.ppermute(array, axis, [(i, (i + step) % n) for i in range(n)])]
    reduce_sum x0 -> x1, other arithmetic: none -> 1.31 us  [on_device(): at_home = jnp.sum(jnp.where(owners == z, own_slots, 0))]
  transfers between devices with their start and end apart: 6 -> 7, of which waited for: 3 -> 3; matrix products, arithmetic and copies ran while one was open for 1% -> 3% of each run, Pallas kernels for 0% -> 0%
where the time goes in v3:
time: 97.7 us; the launch traced here: 97 us
  starting transfers between devices  40.2 us (41%)
  blocking collectives  24.4 us (25%)
  waiting for transfers between devices  17.4 us (18%)
  Pallas kernels  7.68 us (8%)
  local copies, waits for them, and re-layouts  3.35 us (3%)
  other arithmetic  3.14 us (3%)
    all_to_all x1, blocking collectives, exchange(): return lax.all_to_all(array, axes, split_axis=0, concat_axis=0, tiled=True)  24.4 us
    ppermute x5, starting transfers between devices, shift(): return lax.ppermute(array, axis, [(i, (i + step) % n) for i in range(n)])  20.5 us
    all_to_all x2, starting transfers between devices, exchange(): return lax.all_to_all(array, axes, split_axis=0, concat_axis=0, tiled=True)  19.7 us
    all_to_all x2, waiting for transfers between devices, exchange(): return lax.all_to_all(array, axes, split_axis=0, concat_axis=0, tiled=True)  15.4 us
    pallas_call x1, Pallas kernels, attend(): pl.pallas_call(functools.partial(attend_kernel, scale), in_specs=[SMEM] +...  2.49 us
    pallas_call x1, Pallas kernels, split_pages(): pl.pallas_call(split_pages_kernel, in_specs=[SMEM, VMEM], out_specs=HBM,...  2.3 us
    ppermute x5, waiting for transfers between devices, shift(): return lax.ppermute(array, axis, [(i, (i + step) % n) for i in range(n)])  2.04 us
  transfers between devices with their start and end apart: 7, of which 3 were waited for; matrix products, arithmetic and copies ran while one was open for 3% of the time, Pallas kernels for 0%

profile of v3, /device:TPU:1, one launch (start us, length us, event | category | flops | bytes accessed | tf_op | source)
XLA Modules:
  0.0 97.0 jit_solution(8179520860217540513)
XLA Ops:
  0.7 1.3 %copy.12.seen_ref = s32[8,2]{1,0:T(8,128)} copy(s32[8,2]{0,1:T(2,128)} %bitcast.29) | data formatting | bytes 128 | tf_op jit(solution)/shard_map/squeeze | solution.py:216
  2.0 0.6 pad_add_fusion.place_ref
  2.6 1.6 %announce.1 = bf16[64,16,128]{2,1,0:T(8,128)(2,1)} custom-call(s32[2]{0:T(128)} %pad_add_fusion.place_ref, s32[8]{0:T(128)} %bitcast.27, s32[8]{0:T(128)} %bitcast.28, s32[1]{0:T(128)S(6)} %copy.16.length_ref, s32[8,2]{1,0:T(8,128)} %copy.12.seen_ref, bf16[16,4096]{1,0:T(8,128)(2,1)} %proj_ref.1), custom_call_target="tpu_custom_call" | custom-call | tf_op jit(solution)/shard_map/announce/pallas_call | solution.py:69
  4.3 14.8 %all-to-all-start = ((bf16[64,16,128]{2,1,0:T(8,128)(2,1)}), bf16[64,16,128]{2,1,0:T(8,128)(2,1)S(1)}, u32[]{:S(2)}, u32[]{:S(2)}) async-start(bf16[64,16,128]{2,1,0:T(8,128)(2,1)} %announce.1), calls=%async_computation | async-start | bytes 524288 | tf_op jit(solution)/shard_map/all_to_all | solution.py:27
  19.1 1.3 %fusion.1 = s32[]{:T(128)} fusion(s32[]{:T(128)} %axis_index.58, s32[1,1,8]{2,1,0:T(1,128)} %param.13, s32[1,1,8]{2,1,0:T(1,128)} %param.12), kind=kLoop, calls=%fused_computation.8 | loop fusion | flops 23 | bytes 72 | tf_op jit(solution)/shard_map/reduce_sum | solution.py:219
  20.4 11.8 %all-to-all-done = bf16[64,16,128]{2,1,0:T(8,128)(2,1)S(1)} async-done(((bf16[64,16,128]{2,1,0:T(8,128)(2,1)}), bf16[64,16,128]{2,1,0:T(8,128)(2,1)S(1)}, u32[]{:S(2)}, u32[]{:S(2)}) %all-to-all-start) | async-done | bytes 262176 | tf_op jit(solution)/shard_map/all_to_all | solution.py:27
  32.3 0.1 constant_dynamic-slice_fusion.1
  32.4 0.1 copy.15
  32.5 1.2 %fusion.slot_ref = s32[8]{0:T(128)} fusion(bf16[8,1,1,1]{0,3,2,1:T(2,128)(2,1)S(1)} %copy.15, s32[]{:T(128)} %fusion.1, s32[]{:T(128)} %axis_index.58), kind=kLoop, calls=%fused_computation.7 | loop fusion | flops 32 | bytes 56 | tf_op jit(solution)/shard_map/jit(clip)/min | solution.py:221
  33.6 0.0 copy-done.4
  33.6 2.3 %split_pages.1 = bf16[64,2,32,128]{3,2,1,0:T(8,128)(2,1)} custom-call(s32[8]{0:T(128)} %fusion.slot_ref, bf16[8,2,32,1024]{3,2,1,0:T(8,128)(2,1)} %pool_ref.1), custom_call_target="tpu_custom_call" | custom-call | tf_op jit(solution)/shard_map/split_pages/pallas_call | solution.py:96
  35.9 0.0 copy-start
  35.9 0.0 copy-start.1
  36.0 0.0 copy-start.3
  36.0 4.9 %all-to-all-start.1 = ((bf16[64,2,32,128]{3,2,1,0:T(8,128)(2,1)}), bf16[64,2,32,128]{3,2,1,0:T(8,128)(2,1)S(1)}, u32[]{:S(2)}, u32[]{:S(2)}) async-start(bf16[64,2,32,128]{3,2,1,0:T(8,128)(2,1)} %split_pages.1), calls=%async_computation.1 | async-start | bytes 2097152 | tf_op jit(solution)/shard_map/all_to_all | solution.py:27
  40.8 0.8 constant_dynamic-slice_fusion
  41.6 3.2 %collective-permute-start.1 = (bf16[128,128]{1,0:T(8,128)(2,1)S(1)}, bf16[128,128]{1,0:T(8,128)(2,1)S(1)}, u32[]{:S(2)}, u32[]{:S(2)}) collective-permute-start(bf16[128,128]{1,0:T(8,128)(2,1)S(1)} %bitcast.18), channel_id=1, source_target_pairs={{0,8},{8,16},{16,24},{24,32},{32,40},{40,48},{48,56},{56,0},{1,9},... | collective-permute-start | bytes 98312 | tf_op jit(solution)/shard_map/ppermute | solution.py:32
  44.8 1.0 %copy.14 = bf16[8,8,16,128]{3,1,2,0:T(8,128)(2,1)S(1)} copy(bf16[8,8,16,128]{3,2,1,0:T(8,128)(2,1)} %bitcast.26) | data formatting | bytes 524288 | tf_op jit(solution)/shard_map/optimization_barrier | solution.py:222
  45.8 3.8 %collective-permute-start.2 = (bf16[128,128]{1,0:T(8,128)(2,1)S(1)}, bf16[128,128]{1,0:T(8,128)(2,1)S(1)}, u32[]{:S(2)}, u32[]{:S(2)}) collective-permute-start(bf16[128,128]{1,0:T(8,128)(2,1)S(1)} %bitcast.19), channel_id=1, source_target_pairs={{0,56},{8,0},{16,8},{24,16},{32,24},{40,32},{48,40},{56,48},{1,57}... | collective-permute-start | bytes 98312 | tf_op jit(solution)/shard_map/ppermute | solution.py:32
  49.7 0.0 collective-permute-done.1.rest_1_
  49.7 4.9 %collective-permute-start.4 = (bf16[256,128]{1,0:T(8,128)(2,1)S(1)}, bf16[256,128]{1,0:T(8,128)(2,1)S(1)}, u32[]{:S(2)}, u32[]{:S(2)}) collective-permute-start(bf16[256,128]{1,0:T(8,128)(2,1)S(1)} %pad_maximum_fusion.1), channel_id=1, source_target_pairs={{0,40},{8,48},{16,56},{24,0},{32,8},{40,16},{48,24},{56,32},{1,41}... | collective-permute-start | bytes 196616 | tf_op jit(solution)/shard_map/ppermute | solution.py:32
  54.6 0.0 collective-permute-done.2.rest_2_
  54.7 3.8 %collective-permute-start.3 = (bf16[384,128]{1,0:T(8,128)(2,1)S(1)}, bf16[384,128]{1,0:T(8,128)(2,1)S(1)}, u32[]{:S(2)}, u32[]{:S(2)}) collective-permute-start(bf16[384,128]{1,0:T(8,128)(2,1)S(1)} %pad_maximum_fusion), channel_id=1, source_target_pairs={{0,24},{8,32},{16,40},{24,48},{32,56},{40,0},{48,8},{56,16},{1,25}... | collective-permute-start | bytes 294920 | tf_op jit(solution)/shard_map/ppermute | solution.py:32
  58.5 4.8 %collective-permute-start = (bf16[8,128]{1,0:T(8,128)(2,1)S(1)}, bf16[8,128]{1,0:T(8,128)(2,1)S(1)}, u32[]{:S(2)}, u32[]{:S(2)}) collective-permute-start(bf16[8,128]{1,0:T(8,128)(2,1)S(1)} %dynamic-slice_bitcast_fusion), channel_id=1, source_target_pairs={{0,448},{64,0},{128,64},{192,128},{256,192},{320,256},{384,320},{4... | collective-permute-start | bytes 6152 | tf_op jit(solution)/shard_map/ppermute | solution.py:32
  63.3 2.0 %collective-permute-done.info_ref = bf16[8,128]{1,0:T(8,128)(2,1)S(1)} collective-permute-done((bf16[8,128]{1,0:T(8,128)(2,1)S(1)}, bf16[8,128]{1,0:T(8,128)(2,1)S(1)}, u32[]{:S(2)}, u32[]{:S(2)}) %collective-permute-start) | collective-permute-done | bytes 2080 | tf_op jit(solution)/shard_map/ppermute | solution.py:32
  65.3 0.0 collective-permute-done.4.rest_4_
  65.3 0.0 collective-permute-done.3.rest_3_
  65.3 3.5 %all-to-all-done.1.kv_ref = bf16[64,2,32,128]{3,2,1,0:T(8,128)(2,1)S(1)} async-done(((bf16[64,2,32,128]{3,2,1,0:T(8,128)(2,1)}), bf16[64,2,32,128]{3,2,1,0:T(8,128)(2,1)S(1)}, u32[]{:S(2)}, u32[]{:S(2)}) %all-to-all-start.1) | async-done | bytes 1048608 | tf_op jit(solution)/shard_map/all_to_all | solution.py:27
  68.8 2.5 %attend.1 = bf16[1024,128]{1,0:T(8,128)(2,1)S(1)} custom-call(s32[1]{0:T(128)} %bitcast.y_ref, bf16[8,128]{1,0:T(8,128)(2,1)S(1)} %collective-permute-done.info_ref, bf16[64,2,32,128]{3,2,1,0:T(8,128)(2,1)S(1)} %all-to-all-done.1.kv_ref, bf16[128,128]{1,0:T(8,128)(2,1)S(1)} %bitcast.22, bf16[128,128]{1,0:T(8,128)(2,1)S(1)} %collective-permute-done.1.rest_1_, ...), custom_call_target="tpu_custom_call" | custom-call | tf_op jit(solution)/shard_map/attend/pallas_call | solution.py:156
  71.3 24.4 %all_to_all.15.back_ref = bf16[64,16,128]{2,1,0:T(8,128)(2,1)S(1)} all-to-all(bf16[64,16,128]{2,1,0:T(8,128)(2,1)S(1)} %bitcast.17), channel_id=1, replica_groups=mesh['z'=8,'y'=8,'x'=4,'c'=2] {'y','x','c'}, dimensions={0} | all-to-all | bytes 524288 | tf_op jit(solution)/shard_map/all_to_all | solution.py:27
  95.7 0.0 copy-done.1
  95.7 1.3 %finish.1 = bf16[16,1024]{1,0:T(8,128)(2,1)} custom-call(bf16[64,16,128]{2,1,0:T(8,128)(2,1)S(1)} %all_to_all.15.back_ref, bf16[16,4096]{1,0:T(8,128)(2,1)S(1)} %copy-done.1, bf16[16,1024]{1,0:T(8,128)(2,1)S(1)} %copy-done.2, f32[1,1024]{1,0:T(1,128)S(1)} %bitcast.23, bf16[1024,1024]{1,0:T(8,128)(2,1)S(1)} %copy-done), custom_call_target="tpu_custom_call" | custom-call | tf_op jit(solution)/shard_map/finish/pallas_call | solution.py:195
  (8 shorter events, 0.0 us)
Async XLA Ops:
  4.3 28.0 %all-to-all-start = ((bf16[64,16,128]{2,1,0:T(8,128)(2,1)}), bf16[64,16,128]{2,1,0:T(8,128)(2,1)S(1)}, u32[]{:S(2)}, u32[]{:S(2)}) async-start(bf16[64,16,128]{2,1,0:T(8,128)(2,1)} %announce.1), calls=%async_computation | async-start | bytes 524288 | tf_op jit(solution)/shard_map/all_to_all | solution.py:27
  32.3 1.3 %copy-start.4 = (bf16[64,16,128]{2,1,0:T(8,128)(2,1)}, bf16[64,16,128]{2,1,0:T(8,128)(2,1)S(1)}, u32[]{:S(2)}) copy-start(bf16[64,16,128]{2,1,0:T(8,128)(2,1)S(1)} %all-to-all-done) | copy-start | bytes 786436
  35.9 59.8 %copy-start = (bf16[1024,1024]{1,0:T(8,128)(2,1)S(1)}, bf16[1024,1024]{1,0:T(8,128)(2,1)}, u32[]{:S(2)}) copy-start(bf16[1024,1024]{1,0:T(8,128)(2,1)} %weight_ref.1) | copy-start | bytes 6291460
  35.9 59.8 %copy-start.1 = (bf16[16,4096]{1,0:T(8,128)(2,1)S(1)}, bf16[16,4096]{1,0:T(8,128)(2,1)}, u32[]{:S(2)}) copy-start(bf16[16,4096]{1,0:T(8,128)(2,1)} %proj_ref.1) | copy-start | bytes 393220
  36.0 59.8 %copy-start.3 = (f32[1024]{0:T(1024)S(1)}, f32[1024]{0:T(1024)}, u32[]{:S(2)}) copy-start(f32[1024]{0:T(1024)} %param.16) | copy-start | bytes 12292
  36.0 32.9 %all-to-all-start.1 = ((bf16[64,2,32,128]{3,2,1,0:T(8,128)(2,1)}), bf16[64,2,32,128]{3,2,1,0:T(8,128)(2,1)S(1)}, u32[]{:S(2)}, u32[]{:S(2)}) async-start(bf16[64,2,32,128]{3,2,1,0:T(8,128)(2,1)} %split_pages.1), calls=%async_computation.1 | async-start | bytes 2097152 | tf_op jit(solution)/shard_map/all_to_all | solution.py:27
  41.6 8.1 %collective-permute-start.1 = (bf16[128,128]{1,0:T(8,128)(2,1)S(1)}, bf16[128,128]{1,0:T(8,128)(2,1)S(1)}, u32[]{:S(2)}, u32[]{:S(2)}) collective-permute-start(bf16[128,128]{1,0:T(8,128)(2,1)S(1)} %bitcast.18), channel_id=1, source_target_pairs={{0,8},{8,16},{16,24},{24,32},{32,40},{40,48},{48,56},{56,0},{1,9},... | collective-permute-start | bytes 98312 | tf_op jit(solution)/shard_map/ppermute | solution.py:32
  45.8 8.8 %collective-permute-start.2 = (bf16[128,128]{1,0:T(8,128)(2,1)S(1)}, bf16[128,128]{1,0:T(8,128)(2,1)S(1)}, u32[]{:S(2)}, u32[]{:S(2)}) collective-permute-start(bf16[128,128]{1,0:T(8,128)(2,1)S(1)} %bitcast.19), channel_id=1, source_target_pairs={{0,56},{8,0},{16,8},{24,16},{32,24},{40,32},{48,40},{56,48},{1,57}... | collective-permute-start | bytes 98312 | tf_op jit(solution)/shard_map/ppermute | solution.py:32
  49.7 15.6 %collective-permute-start.4 = (bf16[256,128]{1,0:T(8,128)(2,1)S(1)}, bf16[256,128]{1,0:T(8,128)(2,1)S(1)}, u32[]{:S(2)}, u32[]{:S(2)}) collective-permute-start(bf16[256,128]{1,0:T(8,128)(2,1)S(1)} %pad_maximum_fusion.1), channel_id=1, source_target_pairs={{0,40},{8,48},{16,56},{24,0},{32,8},{40,16},{48,24},{56,32},{1,41}... | collective-permute-start | bytes 196616 | tf_op jit(solution)/shard_map/ppermute | solution.py:32
  54.7 10.6 %collective-permute-start.3 = (bf16[384,128]{1,0:T(8,128)(2,1)S(1)}, bf16[384,128]{1,0:T(8,128)(2,1)S(1)}, u32[]{:S(2)}, u32[]{:S(2)}) collective-permute-start(bf16[384,128]{1,0:T(8,128)(2,1)S(1)} %pad_maximum_fusion), channel_id=1, source_target_pairs={{0,24},{8,32},{16,40},{24,48},{32,56},{40,0},{48,8},{56,16},{1,25}... | collective-permute-start | bytes 294920 | tf_op jit(solution)/shard_map/ppermute | solution.py:32
  58.5 6.8 %collective-permute-start = (bf16[8,128]{1,0:T(8,128)(2,1)S(1)}, bf16[8,128]{1,0:T(8,128)(2,1)S(1)}, u32[]{:S(2)}, u32[]{:S(2)}) collective-permute-start(bf16[8,128]{1,0:T(8,128)(2,1)S(1)} %dynamic-slice_bitcast_fusion), channel_id=1, source_target_pairs={{0,448},{64,0},{128,64},{192,128},{256,192},{320,256},{384,320},{4... | collective-permute-start | bytes 6152 | tf_op jit(solution)/shard_map/ppermute | solution.py:32
  68.8 26.9 %copy-start.2 = (bf16[16,1024]{1,0:T(8,128)(2,1)S(1)}, bf16[16,1024]{1,0:T(8,128)(2,1)}, u32[]{:S(2)}) copy-start(bf16[16,1024]{1,0:T(8,128)(2,1)} %input_ref.1) | copy-start | bytes 98308

commit v4 on v3

--- a/solution.py
+++ b/solution.py
@@ -14,6 +14,9 @@
 
 PLANE = ("y", "x", "c")
 SPREAD = ("z", "x", "c")
+PAGES = ("x", "z", "c")
+SUMS = ("x", "y", "c")
+CORES = 2
 
 FIELDS = 16
 LIVE, SLOT = 8, 9
@@ -37,21 +40,22 @@
     return half + half * jnp.tanh(half)
 
 
-def announce_kernel(place_ref, owner_ref, slot_ref, length_ref, seen_ref, q_ref, out_ref):
+def announce_kernel(owner_ref, slot_ref, length_ref, seen_ref, q_ref, out_ref):
     rows, hd = out_ref.shape[1:]
     pages = owner_ref.shape[0]
-    tiles, blocks = seen_ref.shape
+    blocks, tiles = seen_ref.shape
+    place = lax.axis_index(PLANE)
     lane = lax.broadcasted_iota(jnp.int32, (rows, hd), 1)
     owner, field = lane // FIELDS, lane % FIELDS
     seen = []
     for b in range(blocks):
         row = jnp.zeros((rows, hd), jnp.int32)
         for t in range(tiles):
-            row = jnp.where(field == t, seen_ref[t : t + 1, b : b + 1], row)
+            row = jnp.where(field == t, seen_ref[b : b + 1, t : t + 1], row)
         seen.append(row)
     info = jnp.zeros((rows, hd), jnp.int32)
     for j in range(pages):
-        live = jnp.clip(length_ref[0] - (place_ref[1] * pages + j) * PAGE, 0, PAGE)
+        live = jnp.clip(length_ref[0] - (place * pages + j) * PAGE, 0, PAGE)
         row = jnp.where(field == LIVE, live, seen[j * blocks // pages])
         row = jnp.where(field == SLOT, slot_ref[j], row)
         info = jnp.where(owner == owner_ref[j], row, info)
@@ -60,47 +64,59 @@
         out_ref[i] = info
     query = silu(q_ref[...].astype(jnp.float32)).astype(jnp.bfloat16)
     for h in range(HEADS):
-        out_ref[place_ref[0] * HEADS + h] = query[:, h * hd : (h + 1) * hd]
-
-
-def announce(place, owners, slots, lengths, seen, cand_proj, users):
+        out_ref[lax.axis_index("z") * HEADS + h] = query[:, h * hd : (h + 1) * hd]
+
+
+def announce(owners, slots, lengths, seen, cand_proj, users):
     rows, width = cand_proj.shape[0], cand_proj.shape[1] // 4
     hd = width // HEADS
     return pl.pallas_call(
         announce_kernel,
         grid=(1,),
-        in_specs=[SMEM] * 4 + [VMEM, pl.BlockSpec((rows, width), lambda i: (0, 2))],
+        in_specs=[SMEM] * 3 + [VMEM, pl.BlockSpec((rows, width), lambda i: (0, 2))],
         out_specs=VMEM,
         out_shape=jax.ShapeDtypeStruct((users * HEADS, rows, hd), jnp.bfloat16),
         name="announce",
-    )(place, owners, slots, lengths, seen, cand_proj)
-
-
-def split_pages_kernel(slot_ref, pool_ref, out_ref, split_ref, sems):
-    hd = out_ref.shape[3]
+    )(owners, slots, lengths, seen, cand_proj)
+
+
+def split_pages_kernel(owner_ref, slot_ref, told_ref, pool_ref, out_ref, split_ref, sems):
+    n_x, users = out_ref.shape[:2]
+    rows, hd = told_ref.shape[1:]
+    z, h = lax.axis_index("z"), lax.axis_index(("x", "c"))
+    at_home = jnp.int32(0)
+    for j in range(owner_ref.shape[0]):
+        at_home = jnp.where(owner_ref[j] == z, slot_ref[j], at_home)
+    lane = lax.broadcasted_iota(jnp.int32, (rows, hd), 1)
+    row = lax.broadcasted_iota(jnp.int32, (rows, hd), 0)
+    here = (row == 0) & (lane == z * FIELDS + SLOT)
+    slots = []
+    for u in range(users):
+        told = told_ref[u * HEADS + h].astype(jnp.float32)
+        slot = jnp.sum(jnp.where(here, told, 0.0)).astype(jnp.int32)
+        slots.append(jnp.clip(jnp.where(z == u, at_home, slot), 0, pool_ref.shape[0] - 1))
     copies = []
-    for u in range(slot_ref.shape[0]):
-        for h in range(HEADS):
-            split_ref[u * HEADS + h] = pool_ref[slot_ref[u], :, :, h * hd : (h + 1) * hd]
-        part = pl.ds(u * HEADS, HEADS)
-        copies.append(pltpu.make_async_copy(split_ref.at[part], out_ref.at[part], sems.at[u]))
+    for u in range(users):
+        for k in range(HEADS):
+            split_ref[k // CORES, u, k % CORES] = pool_ref[slots[u], :, :, k * hd : (k + 1) * hd]
+        copies.append(pltpu.make_async_copy(split_ref.at[:, u], out_ref.at[:, u], sems.at[u]))
         copies[-1].start()
     for copy in copies:
         copy.wait()
 
 
-def split_pages(slots, kv_pool):
+def split_pages(owners, own_slots, told, kv_pool):
     _, _, page, width = kv_pool.shape
-    users = slots.shape[0]
-    out = jax.ShapeDtypeStruct((users * HEADS, 2, page, width // HEADS), kv_pool.dtype)
+    users = told.shape[0] // HEADS
+    shape = (HEADS // CORES, users, CORES, 2, page, width // HEADS)
     return pl.pallas_call(
         split_pages_kernel,
-        in_specs=[SMEM, VMEM],
+        in_specs=[SMEM, SMEM, VMEM, VMEM],
         out_specs=HBM,
-        out_shape=out,
-        scratch_shapes=[pltpu.VMEM(out.shape, out.dtype), pltpu.SemaphoreType.DMA((users,))],
+        out_shape=jax.ShapeDtypeStruct(shape, kv_pool.dtype),
+        scratch_shapes=[pltpu.VMEM(shape, kv_pool.dtype), pltpu.SemaphoreType.DMA((users,))],
         name="split_pages",
-    )(slots, kv_pool)
+    )(owners, own_slots, told, kv_pool)
 
 
 STEPS = (0, -1, 1, -3, -4, -2, 3, 2)
@@ -113,13 +129,13 @@
     return row, below, above, below3, above3
 
 
-def attend_kernel(scale, y_ref, info_ref, kv_ref, *rest):
+def attend_kernel(scale, info_ref, kv_ref, *rest):
     pieces, (out_ref, q_ref, acc_ref) = rest[:-3], rest[-3:]
-    hd = out_ref.shape[1]
+    n_x, n_y, cores, rows, hd = out_ref.shape
     sources, tiles = info_ref.shape[0], len(STEPS)
     span = sources * PAGE
-    height = out_ref.shape[0] // tiles
-    y = y_ref[0]
+    height = n_x * cores * rows
+    y = lax.axis_index("y")
     place = 0
     for piece in pieces:
         for b in range(piece.shape[0] // height):
@@ -134,9 +150,9 @@
     )
     within = lax.rem(lax.broadcasted_iota(jnp.int32, (1, span), 1), PAGE).astype(jnp.float32)
     q = q_ref[...]
-    for o in range(kv_ref.shape[0] // sources):
-        keys = kv_ref[o * sources : (o + 1) * sources, 0].reshape(span, hd)
-        values = kv_ref[o * sources : (o + 1) * sources, 1].reshape(span, hd)
+    for o in range(kv_ref.shape[1]):
+        keys = kv_ref[:, o, :, 0].reshape(span, hd)
+        values = kv_ref[:, o, :, 1].reshape(span, hd)
         seen = fields[o * FIELDS : o * FIELDS + tiles]
         live = fields[o * FIELDS + LIVE : o * FIELDS + LIVE + 1]
         allowed = jnp.where(within < live, seen, 0.0).astype(jnp.bfloat16)
@@ -148,20 +164,23 @@
             acc_ref[...] = part
         else:
             acc_ref[...] += part
-    out_ref[...] = acc_ref[...].astype(out_ref.dtype)
-
-
-def attend(y, info, pages, pieces, scale):
-    rows, hd = sum(piece.shape[0] for piece in pieces), pages.shape[-1]
+    total = acc_ref[...].astype(out_ref.dtype).reshape(n_y, n_x, cores, rows, hd)
+    for t in range(n_y):
+        out_ref[:, t] = total[t]
+
+
+def attend(info, pages, pieces, scale, rows):
+    n_x, _, cores, _, _, hd = pages.shape
+    height = sum(piece.shape[0] for piece in pieces)
     return pl.pallas_call(
         functools.partial(attend_kernel, scale),
-        in_specs=[SMEM] + [VMEM] * (2 + len(pieces)),
+        in_specs=[VMEM] * (2 + len(pieces)),
         out_specs=VMEM,
-        out_shape=jax.ShapeDtypeStruct((rows, hd), jnp.bfloat16),
-        scratch_shapes=[pltpu.VMEM((rows, hd), jnp.bfloat16), pltpu.VMEM((rows, hd), jnp.float32)],
+        out_shape=jax.ShapeDtypeStruct((n_x, len(STEPS), cores, rows, hd), jnp.bfloat16),
+        scratch_shapes=[pltpu.VMEM((height, hd), jnp.bfloat16), pltpu.VMEM((height, hd), jnp.float32)],
         compiler_params=pltpu.CompilerParams(vmem_limit_bytes=40 * 1024 * 1024),
         name="attend",
-    )(y, info, pages, *pieces)
+    )(info, pages, *pieces)
 
 
 def finish_kernel(scale, back_ref, proj_ref, input_ref, gain_ref, weight_ref, out_ref):
@@ -176,8 +195,8 @@
     attn = []
     for h in range(HEADS):
         total = jnp.zeros((rows, hd), jnp.float32)
-        for g in range(back_ref.shape[0] // HEADS):
-            total += back_ref[g * HEADS + h].astype(jnp.float32)
+        for y in range(back_ref.shape[1]):
+            total += back_ref[h // CORES, y, h % CORES].astype(jnp.float32)
         own = silu(jnp.sum(act(2, h) * act(3, h), axis=1, keepdims=True) * scale)
         own = own.astype(jnp.bfloat16).astype(jnp.float32)
         attn.append(total + own * act(1, h))
@@ -209,30 +228,27 @@
     hd = width // HEADS
     scale = hd ** (-0.5)
     n_z = lax.axis_size("z")
-    z, y, h = lax.axis_index("z"), lax.axis_index("y"), lax.axis_index(("x", "c"))
-    place = jnp.stack([z, lax.axis_index(PLANE)])
+    z = lax.axis_index("z")
     owners, own_slots = page_owner.reshape(-1), page_slot.reshape(-1)
 
-    sent = announce(place, owners, own_slots, lengths, block_mask[0], cand_proj, n_z)
-    told = exchange(sent, SPREAD).reshape(n_z, HEADS, rows, hd)
-    to_me = lax.dynamic_slice(told, (0, h, 0, z * FIELDS + SLOT), (n_z, 1, 1, 1)).reshape(-1)
-    at_home = jnp.sum(jnp.where(owners == z, own_slots, 0))
-    slots = jnp.where(jnp.arange(n_z) == z, at_home, to_me.astype(jnp.int32))
-    pages = split_pages(jnp.clip(slots, 0, kv_pool.shape[0] - 1), kv_pool)
+    sent = announce(owners, own_slots, lengths, block_mask[0].T, cand_proj, n_z)
+    told = exchange(sent, SPREAD)
+    pages = split_pages(owners, own_slots, told, kv_pool)
     pages, told = lax.optimization_barrier((pages, told))
-    got = exchange(pages, SPREAD)
+    got = exchange(pages.reshape((-1,) + pages.shape[3:]), PAGES).reshape(pages.shape)
+    told = told.reshape(n_z, HEADS, rows, hd)
     below = lax.dynamic_slice(told, ((z + n_z - 1) % n_z, 0, 0, 0), (1, HEADS, 1, hd)).reshape(HEADS, hd)
     info = shift(below, "z", -1)
     pieces = gather_queries(lax.dynamic_index_in_dim(told, z, 0, keepdims=False).reshape(-1, hd))
-    part = attend(y.reshape(1), info, got, pieces, scale)
-    back = exchange(part.reshape(-1, rows, hd), PLANE)
+    part = attend(info, got, pieces, scale, rows)
+    back = exchange(part.reshape(-1, rows, hd), SUMS).reshape(part.shape)
     return finish(back, cand_proj, cand_input, out_gain, out_weight, scale)
 
 
 def solution(mesh):
     n_z, n_p = mesh.shape["batch"], mesh.shape["pos"]
-    cores, n_x = 2, HEADS // 2
-    grid = Mesh(mesh.devices.reshape(n_z, n_p // HEADS, n_x, cores), ("z", "y", "x", "c"))
+    n_x = HEADS // CORES
+    grid = Mesh(mesh.devices.reshape(n_z, n_p // HEADS, n_x, CORES), ("z", "y", "x", "c"))
     rows = P(("z", "y", "x", "c"), None)
     placed = (
         rows,

time: 97.7 us -> 93 us (0.952)
  blocking collectives: 24.4 us -> 50.2 us
  starting transfers between devices: 40.2 us -> 25.1 us
  waiting for transfers between devices: 17.4 us -> 6.71 us
  other arithmetic: 3.14 us -> 0.02 us
  local copies, waits for them, and re-layouts: 3.35 us -> 1.52 us
    all_to_all x1 -> x2, blocking collectives: 24.4 us -> 50.2 us  [exchange(): return lax.all_to_all(array, axes, split_axis=0, concat_axis=0, tiled=True)]
    all_to_all x2 -> x1, starting transfers between devices: 19.7 us -> 4.86 us  [exchange(): return lax.all_to_all(array, axes, split_axis=0, concat_axis=0, tiled=True)]
    all_to_all x2 -> x1, waiting for transfers between devices: 15.4 us -> 4.39 us  [exchange(): return lax.all_to_all(array, axes, split_axis=0, concat_axis=0, tiled=True)]
    squeeze x1 -> x0, local copies, waits for them, and re-layouts: 1.35 us -> none  [on_device(): block_mask[0]]
    reduce_sum x1 -> x0, other arithmetic: 1.31 us -> none  [on_device(): at_home = jnp.sum(jnp.where(owners == z, own_slots, 0))]
    min x1 -> x0, other arithmetic: 1.16 us -> none  [on_device(): pages = split_pages(jnp.clip(slots, 0, kv_pool.shape[0] - 1), kv_pool)]
    optimization_barrier x1 -> x0, local copies, waits for them, and re-layouts: 1.02 us -> none  [on_device(): pages, told = lax.optimization_barrier((pages, told))]
  transfers between devices with their start and end apart: 7 -> 6, of which waited for: 3 -> 2; matrix products, arithmetic and copies ran while one was open for 3% -> 2% of each run, Pallas kernels for 0% -> 0%
where the time goes in v4:
time: 93 us; the launch traced here: 92.3 us
  blocking collectives  50.2 us (54%)
  starting transfers between devices  25.1 us (27%)
  Pallas kernels  7.96 us (9%)
  waiting for transfers between devices  6.71 us (7%)
  local copies, waits for them, and re-layouts  1.52 us (2%)
    all_to_all x2, blocking collectives, exchange(): return lax.all_to_all(array, axes, split_axis=0, concat_axis=0, tiled=True)  50.2 us
    ppermute x5, starting transfers between devices, shift(): return lax.ppermute(array, axis, [(i, (i + step) % n) for i in range(n)])  20.2 us
    all_to_all x1, starting transfers between devices, exchange(): return lax.all_to_all(array, axes, split_axis=0, concat_axis=0, tiled=True)  4.86 us
    all_to_all x1, waiting for transfers between devices, exchange(): return lax.all_to_all(array, axes, split_axis=0, concat_axis=0, tiled=True)  4.39 us
    pallas_call x1, Pallas kernels, split_pages(): pl.pallas_call(split_pages_kernel, in_specs=[SMEM, SMEM, VMEM, VMEM], out...  2.56 us
    pallas_call x1, Pallas kernels, attend(): pl.pallas_call(functools.partial(attend_kernel, scale), in_specs=[VMEM] *...  2.49 us
    ppermute x5, waiting for transfers between devices, shift(): return lax.ppermute(array, axis, [(i, (i + step) % n) for i in range(n)])  2.31 us
  transfers between devices with their start and end apart: 6, of which 2 were waited for; matrix products, arithmetic and copies ran while one was open for 2% of the time, Pallas kernels for 0%

profile of v4, /device:TPU:1, one launch (start us, length us, event | category | flops | bytes accessed | tf_op | source)
XLA Modules:
  0.0 92.3 jit_solution(10742710226745623436)
XLA Ops:
  0.7 1.6 %announce.1 = bf16[64,16,128]{2,1,0:T(8,128)(2,1)} custom-call(s32[8]{0:T(128)} %bitcast.28, s32[8]{0:T(128)} %bitcast.30, s32[1]{0:T(128)S(6)} %copy.14.length_ref, s32[2,8]{1,0:T(2,128)} %bitcast.32, bf16[16,4096]{1,0:T(8,128)(2,1)} %proj_ref.1), custom_call_target="tpu_custom_call" | custom-call | tf_op jit(solution)/shard_map/announce/pallas_call | solution.py:73
  2.3 28.1 %all_to_all.15.told_ref = bf16[64,16,128]{2,1,0:T(8,128)(2,1)} all-to-all(bf16[64,16,128]{2,1,0:T(8,128)(2,1)} %announce.1), channel_id=1, replica_groups=mesh['z'=8,'y'=8,'x'=4,'c'=2] {'z','x','c'}, dimensions={0} | all-to-all | bytes 524288 | tf_op jit(solution)/shard_map/all_to_all | solution.py:30
  30.4 2.6 %split_pages.1 = bf16[4,8,2,2,32,128]{5,4,3,2,1,0:T(8,128)(2,1)} custom-call(s32[8]{0:T(128)} %bitcast.29, s32[8]{0:T(128)} %bitcast.31, bf16[64,16,128]{2,1,0:T(8,128)(2,1)} %all_to_all.15.told_ref, bf16[8,2,32,1024]{3,2,1,0:T(8,128)(2,1)} %pool_ref.1), custom_call_target="tpu_custom_call" | custom-call | tf_op jit(solution)/shard_map/split_pages/pallas_call | solution.py:112
  33.0 0.0 copy-start
  33.0 0.0 copy-start.1
  33.0 0.0 copy-start.3
  33.0 4.9 %all-to-all-start.1 = ((bf16[64,2,32,128]{3,2,1,0:T(8,128)(2,1)}), bf16[64,2,32,128]{3,2,1,0:T(8,128)(2,1)S(1)}, u32[]{:S(2)}, u32[]{:S(2)}) async-start(bf16[64,2,32,128]{3,2,1,0:T(8,128)(2,1)} %bitcast.24), calls=%async_computation.1 | async-start | bytes 2097152 | tf_op jit(solution)/shard_map/all_to_all | solution.py:30
  37.9 0.8 constant_dynamic-slice_fusion
  38.6 3.2 %collective-permute-start.1 = (bf16[128,128]{1,0:T(8,128)(2,1)S(1)}, bf16[128,128]{1,0:T(8,128)(2,1)S(1)}, u32[]{:S(2)}, u32[]{:S(2)}) collective-permute-start(bf16[128,128]{1,0:T(8,128)(2,1)S(1)} %bitcast.18), channel_id=1, source_target_pairs={{0,8},{8,16},{16,24},{24,32},{32,40},{40,48},{48,56},{56,0},{1,9},... | collective-permute-start | bytes 98312 | tf_op jit(solution)/shard_map/ppermute | solution.py:35
  41.9 3.8 %collective-permute-start.2 = (bf16[128,128]{1,0:T(8,128)(2,1)S(1)}, bf16[128,128]{1,0:T(8,128)(2,1)S(1)}, u32[]{:S(2)}, u32[]{:S(2)}) collective-permute-start(bf16[128,128]{1,0:T(8,128)(2,1)S(1)} %bitcast.19), channel_id=1, source_target_pairs={{0,56},{8,0},{16,8},{24,16},{32,24},{40,32},{48,40},{56,48},{1,57}... | collective-permute-start | bytes 98312 | tf_op jit(solution)/shard_map/ppermute | solution.py:35
  45.7 0.0 collective-permute-done.1.rest_1_
  45.7 4.9 %collective-permute-start.4 = (bf16[256,128]{1,0:T(8,128)(2,1)S(1)}, bf16[256,128]{1,0:T(8,128)(2,1)S(1)}, u32[]{:S(2)}, u32[]{:S(2)}) collective-permute-start(bf16[256,128]{1,0:T(8,128)(2,1)S(1)} %pad_maximum_fusion.1), channel_id=1, source_target_pairs={{0,40},{8,48},{16,56},{24,0},{32,8},{40,16},{48,24},{56,32},{1,41}... | collective-permute-start | bytes 196616 | tf_op jit(solution)/shard_map/ppermute | solution.py:35
  50.6 0.0 collective-permute-done.2.rest_2_
  50.7 3.8 %collective-permute-start.3 = (bf16[384,128]{1,0:T(8,128)(2,1)S(1)}, bf16[384,128]{1,0:T(8,128)(2,1)S(1)}, u32[]{:S(2)}, u32[]{:S(2)}) collective-permute-start(bf16[384,128]{1,0:T(8,128)(2,1)S(1)} %pad_maximum_fusion), channel_id=1, source_target_pairs={{0,24},{8,32},{16,40},{24,48},{32,56},{40,0},{48,8},{56,16},{1,25}... | collective-permute-start | bytes 294920 | tf_op jit(solution)/shard_map/ppermute | solution.py:35
  54.5 0.7 constant_dynamic-slice_fusion.1
  55.2 4.5 %collective-permute-start = (bf16[8,128]{1,0:T(8,128)(2,1)S(1)}, bf16[8,128]{1,0:T(8,128)(2,1)S(1)}, u32[]{:S(2)}, u32[]{:S(2)}) collective-permute-start(bf16[8,128]{1,0:T(8,128)(2,1)S(1)} %bitcast.27), channel_id=1, source_target_pairs={{0,448},{64,0},{128,64},{192,128},{256,192},{320,256},{384,320},{4... | collective-permute-start | bytes 6152 | tf_op jit(solution)/shard_map/ppermute | solution.py:35
  59.7 2.3 %collective-permute-done.info_ref = bf16[8,128]{1,0:T(8,128)(2,1)S(1)} collective-permute-done((bf16[8,128]{1,0:T(8,128)(2,1)S(1)}, bf16[8,128]{1,0:T(8,128)(2,1)S(1)}, u32[]{:S(2)}, u32[]{:S(2)}) %collective-permute-start) | collective-permute-done | bytes 2080 | tf_op jit(solution)/shard_map/ppermute | solution.py:35
  62.0 0.0 collective-permute-done.4.rest_4_
  62.0 0.0 collective-permute-done.3.rest_3_
  62.0 4.4 %all-to-all-done.1 = bf16[64,2,32,128]{3,2,1,0:T(8,128)(2,1)S(1)} async-done(((bf16[64,2,32,128]{3,2,1,0:T(8,128)(2,1)}), bf16[64,2,32,128]{3,2,1,0:T(8,128)(2,1)S(1)}, u32[]{:S(2)}, u32[]{:S(2)}) %all-to-all-start.1) | async-done | bytes 1048608 | tf_op jit(solution)/shard_map/all_to_all | solution.py:30
  66.4 0.0 copy-start.2
  66.4 2.5 %attend.1 = bf16[4,8,2,16,128]{4,3,2,1,0:T(8,128)(2,1)S(1)} custom-call(bf16[8,128]{1,0:T(8,128)(2,1)S(1)} %collective-permute-done.info_ref, bf16[4,8,2,2,32,128]{5,4,3,2,1,0:T(8,128)(2,1)S(1)} %bitcast.15, bf16[128,128]{1,0:T(8,128)(2,1)S(1)} %bitcast.22, bf16[128,128]{1,0:T(8,128)(2,1)S(1)} %collective-permute-done.1.rest_1_, ...), custom_call_target="tpu_custom_call" | custom-call | tf_op jit(solution)/shard_map/attend/pallas_call | solution.py:175
  68.9 22.1 %all_to_all.16 = bf16[64,16,128]{2,1,0:T(8,128)(2,1)S(1)} all-to-all(bf16[64,16,128]{2,1,0:T(8,128)(2,1)S(1)} %bitcast.17), channel_id=1, replica_groups=mesh['z'=8,'y'=8,'x'=4,'c'=2] {'x','y','c'}, dimensions={0} | all-to-all | bytes 524288 | tf_op jit(solution)/shard_map/all_to_all | solution.py:30
  91.0 0.0 copy-done
  91.0 0.0 copy-done.1
  91.0 0.0 copy-done.3
  91.1 0.0 copy-done.2
  91.1 1.3 %finish.1 = bf16[16,1024]{1,0:T(8,128)(2,1)} custom-call(bf16[4,8,2,16,128]{4,3,2,1,0:T(8,128)(2,1)S(1)} %bitcast.16, bf16[16,4096]{1,0:T(8,128)(2,1)S(1)} %copy-done.1, bf16[16,1024]{1,0:T(8,128)(2,1)S(1)} %copy-done.2, f32[1,1024]{1,0:T(1,128)S(1)} %bitcast.23, bf16[1024,1024]{1,0:T(8,128)(2,1)S(1)} %copy-done), custom_call_target="tpu_custom_call" | custom-call | tf_op jit(solution)/shard_map/finish/pallas_call | solution.py:214
  (3 shorter events, 0.0 us)
Async XLA Ops:
  33.0 58.1 %copy-start = (bf16[1024,1024]{1,0:T(8,128)(2,1)S(1)}, bf16[1024,1024]{1,0:T(8,128)(2,1)}, u32[]{:S(2)}) copy-start(bf16[1024,1024]{1,0:T(8,128)(2,1)} %weight_ref.1) | copy-start | bytes 6291460
  33.0 58.1 %copy-start.1 = (bf16[16,4096]{1,0:T(8,128)(2,1)S(1)}, bf16[16,4096]{1,0:T(8,128)(2,1)}, u32[]{:S(2)}) copy-start(bf16[16,4096]{1,0:T(8,128)(2,1)} %proj_ref.1) | copy-start | bytes 393220
  33.0 58.1 %copy-start.3 = (f32[1024]{0:T(1024)S(1)}, f32[1024]{0:T(1024)}, u32[]{:S(2)}) copy-start(f32[1024]{0:T(1024)} %param.16) | copy-start | bytes 12292
  33.0 33.4 %all-to-all-start.1 = ((bf16[64,2,32,128]{3,2,1,0:T(8,128)(2,1)}), bf16[64,2,32,128]{3,2,1,0:T(8,128)(2,1)S(1)}, u32[]{:S(2)}, u32[]{:S(2)}) async-start(bf16[64,2,32,128]{3,2,1,0:T(8,128)(2,1)} %bitcast.24), calls=%async_computation.1 | async-start | bytes 2097152 | tf_op jit(solution)/shard_map/all_to_all | solution.py:30
  38.6 7.0 %collective-permute-start.1 = (bf16[128,128]{1,0:T(8,128)(2,1)S(1)}, bf16[128,128]{1,0:T(8,128)(2,1)S(1)}, u32[]{:S(2)}, u32[]{:S(2)}) collective-permute-start(bf16[128,128]{1,0:T(8,128)(2,1)S(1)} %bitcast.18), channel_id=1, source_target_pairs={{0,8},{8,16},{16,24},{24,32},{32,40},{40,48},{48,56},{56,0},{1,9},... | collective-permute-start | bytes 98312 | tf_op jit(solution)/shard_map/ppermute | solution.py:35
  41.9 8.8 %collective-permute-start.2 = (bf16[128,128]{1,0:T(8,128)(2,1)S(1)}, bf16[128,128]{1,0:T(8,128)(2,1)S(1)}, u32[]{:S(2)}, u32[]{:S(2)}) collective-permute-start(bf16[128,128]{1,0:T(8,128)(2,1)S(1)} %bitcast.19), channel_id=1, source_target_pairs={{0,56},{8,0},{16,8},{24,16},{32,24},{40,32},{48,40},{56,48},{1,57}... | collective-permute-start | bytes 98312 | tf_op jit(solution)/shard_map/ppermute | solution.py:35
  45.7 16.3 %collective-permute-start.4 = (bf16[256,128]{1,0:T(8,128)(2,1)S(1)}, bf16[256,128]{1,0:T(8,128)(2,1)S(1)}, u32[]{:S(2)}, u32[]{:S(2)}) collective-permute-start(bf16[256,128]{1,0:T(8,128)(2,1)S(1)} %pad_maximum_fusion.1), channel_id=1, source_target_pairs={{0,40},{8,48},{16,56},{24,0},{32,8},{40,16},{48,24},{56,32},{1,41}... | collective-permute-start | bytes 196616 | tf_op jit(solution)/shard_map/ppermute | solution.py:35
  50.7 11.4 %collective-permute-start.3 = (bf16[384,128]{1,0:T(8,128)(2,1)S(1)}, bf16[384,128]{1,0:T(8,128)(2,1)S(1)}, u32[]{:S(2)}, u32[]{:S(2)}) collective-permute-start(bf16[384,128]{1,0:T(8,128)(2,1)S(1)} %pad_maximum_fusion), channel_id=1, source_target_pairs={{0,24},{8,32},{16,40},{24,48},{32,56},{40,0},{48,8},{56,16},{1,25}... | collective-permute-start | bytes 294920 | tf_op jit(solution)/shard_map/ppermute | solution.py:35
  55.2 6.8 %collective-permute-start = (bf16[8,128]{1,0:T(8,128)(2,1)S(1)}, bf16[8,128]{1,0:T(8,128)(2,1)S(1)}, u32[]{:S(2)}, u32[]{:S(2)}) collective-permute-start(bf16[8,128]{1,0:T(8,128)(2,1)S(1)} %bitcast.27), channel_id=1, source_target_pairs={{0,448},{64,0},{128,64},{192,128},{256,192},{320,256},{384,320},{4... | collective-permute-start | bytes 6152 | tf_op jit(solution)/shard_map/ppermute | solution.py:35
  66.4 24.6 %copy-start.2 = (bf16[16,1024]{1,0:T(8,128)(2,1)S(1)}, bf16[16,1024]{1,0:T(8,128)(2,1)}, u32[]{:S(2)}) copy-start(bf16[16,1024]{1,0:T(8,128)(2,1)} %input_ref.1) | copy-start | bytes 98308

commit v5 on v4

--- a/solution.py
+++ b/solution.py
@@ -40,7 +40,7 @@
     return half + half * jnp.tanh(half)
 
 
-def announce_kernel(owner_ref, slot_ref, length_ref, seen_ref, q_ref, out_ref):
+def announce_kernel(owner_ref, slot_ref, length_ref, seen_ref, out_ref):
     rows, hd = out_ref.shape[1:]
     pages = owner_ref.shape[0]
     blocks, tiles = seen_ref.shape
@@ -62,39 +62,49 @@
     info = info.astype(jnp.float32).astype(jnp.bfloat16)
     for i in range(out_ref.shape[0]):
         out_ref[i] = info
+
+
+def announce(owners, slots, lengths, seen, users, rows, hd):
+    return pl.pallas_call(
+        announce_kernel,
+        in_specs=[SMEM] * 3 + [VMEM],
+        out_specs=VMEM,
+        out_shape=jax.ShapeDtypeStruct((users, rows, hd), jnp.bfloat16),
+        name="announce",
+    )(owners, slots, lengths, seen)
+
+
+def ask_kernel(q_ref, info_ref, out_ref):
+    rows, hd = info_ref.shape[1:]
     query = silu(q_ref[...].astype(jnp.float32)).astype(jnp.bfloat16)
     for h in range(HEADS):
-        out_ref[lax.axis_index("z") * HEADS + h] = query[:, h * hd : (h + 1) * hd]
-
-
-def announce(owners, slots, lengths, seen, cand_proj, users):
+        out_ref[h, :rows] = query[:, h * hd : (h + 1) * hd]
+        out_ref[h, rows:] = info_ref[0]
+
+
+def ask(cand_proj, info):
     rows, width = cand_proj.shape[0], cand_proj.shape[1] // 4
     hd = width // HEADS
     return pl.pallas_call(
-        announce_kernel,
+        ask_kernel,
         grid=(1,),
-        in_specs=[SMEM] * 3 + [VMEM, pl.BlockSpec((rows, width), lambda i: (0, 2))],
-        out_specs=VMEM,
-        out_shape=jax.ShapeDtypeStruct((users * HEADS, rows, hd), jnp.bfloat16),
-        name="announce",
-    )(owners, slots, lengths, seen, cand_proj)
-
-
-def split_pages_kernel(owner_ref, slot_ref, told_ref, pool_ref, out_ref, split_ref, sems):
+        in_specs=[pl.BlockSpec((rows, width), lambda i: (0, 2)), VMEM],
+        out_specs=VMEM,
+        out_shape=jax.ShapeDtypeStruct((HEADS, 2 * rows, hd), jnp.bfloat16),
+        name="ask",
+    )(cand_proj, info)
+
+
+def split_pages_kernel(told_ref, pool_ref, out_ref, split_ref, sems):
     n_x, users = out_ref.shape[:2]
     rows, hd = told_ref.shape[1:]
-    z, h = lax.axis_index("z"), lax.axis_index(("x", "c"))
-    at_home = jnp.int32(0)
-    for j in range(owner_ref.shape[0]):
-        at_home = jnp.where(owner_ref[j] == z, slot_ref[j], at_home)
     lane = lax.broadcasted_iota(jnp.int32, (rows, hd), 1)
     row = lax.broadcasted_iota(jnp.int32, (rows, hd), 0)
-    here = (row == 0) & (lane == z * FIELDS + SLOT)
+    here = (row == 0) & (lane == lax.axis_index("z") * FIELDS + SLOT)
     slots = []
     for u in range(users):
-        told = told_ref[u * HEADS + h].astype(jnp.float32)
-        slot = jnp.sum(jnp.where(here, told, 0.0)).astype(jnp.int32)
-        slots.append(jnp.clip(jnp.where(z == u, at_home, slot), 0, pool_ref.shape[0] - 1))
+        slot = jnp.sum(jnp.where(here, told_ref[u].astype(jnp.float32), 0.0)).astype(jnp.int32)
+        slots.append(jnp.clip(slot, 0, pool_ref.shape[0] - 1))
     copies = []
     for u in range(users):
         for k in range(HEADS):
@@ -105,48 +115,46 @@
         copy.wait()
 
 
-def split_pages(owners, own_slots, told, kv_pool):
+def split_pages(told, kv_pool):
     _, _, page, width = kv_pool.shape
-    users = told.shape[0] // HEADS
-    shape = (HEADS // CORES, users, CORES, 2, page, width // HEADS)
+    shape = (HEADS // CORES, told.shape[0], CORES, 2, page, width // HEADS)
     return pl.pallas_call(
         split_pages_kernel,
-        in_specs=[SMEM, SMEM, VMEM, VMEM],
+        in_specs=[VMEM, VMEM],
         out_specs=HBM,
         out_shape=jax.ShapeDtypeStruct(shape, kv_pool.dtype),
-        scratch_shapes=[pltpu.VMEM(shape, kv_pool.dtype), pltpu.SemaphoreType.DMA((users,))],
+        scratch_shapes=[pltpu.VMEM(shape, kv_pool.dtype), pltpu.SemaphoreType.DMA((told.shape[0],))],
         name="split_pages",
-    )(owners, own_slots, told, kv_pool)
-
-
-STEPS = (0, -1, 1, -3, -4, -2, 3, 2)
+    )(told, kv_pool)
+
+
+STEPS = (0, -3, 3, -1, -4, 2, 1, -2)
 
 
 def gather_queries(row):
-    below, above = shift(row, "y", 1), shift(row, "y", -1)
-    below3 = shift(jnp.concatenate([row, below, above]), "y", 3)
-    above3 = shift(jnp.concatenate([row, below]), "y", -3)
-    return row, below, above, below3, above3
-
-
-def attend_kernel(scale, info_ref, kv_ref, *rest):
+    below3, above3 = shift(row, "y", 3), shift(row, "y", -3)
+    below = shift(jnp.concatenate([row, below3, above3]), "y", 1)
+    above = shift(jnp.concatenate([row, below3]), "y", -1)
+    return below3, above3, below, above
+
+
+def attend_kernel(scale, asked_ref, kv_ref, *rest):
     pieces, (out_ref, q_ref, acc_ref) = rest[:-3], rest[-3:]
     n_x, n_y, cores, rows, hd = out_ref.shape
-    sources, tiles = info_ref.shape[0], len(STEPS)
+    sources, tiles = n_x * cores, len(STEPS)
     span = sources * PAGE
     height = n_x * cores * rows
     y = lax.axis_index("y")
-    place = 0
+    blocks = [asked_ref[:, :rows].reshape(height, hd)]
     for piece in pieces:
-        for b in range(piece.shape[0] // height):
-            to = lax.rem(y + (STEPS[place] + tiles), tiles)
-            q_ref[pl.ds(to * height, height), :] = piece[b * height : (b + 1) * height, :]
-            place += 1
-    place = lax.broadcasted_iota(jnp.int32, (sources, span), 1)
-    which = lax.broadcasted_iota(jnp.int32, (sources, span), 0)
-    spread = (place // PAGE == which).astype(jnp.bfloat16)
+        blocks += [piece[b * height : (b + 1) * height, :] for b in range(piece.shape[0] // height)]
+    for step, block in zip(STEPS, blocks):
+        q_ref[pl.ds(lax.rem(y + (step + tiles), tiles) * height, height), :] = block
+    place = lax.broadcasted_iota(jnp.int32, (height, span), 1)
+    which = lax.broadcasted_iota(jnp.int32, (height, span), 0)
+    spread = (place // PAGE * rows == which).astype(jnp.bfloat16)
     fields = lax.dot_general(
-        info_ref[...], spread, (((0,), (0,)), ((), ())), preferred_element_type=jnp.float32
+        asked_ref[:, rows:].reshape(height, hd), spread, (((0,), (0,)), ((), ())), preferred_element_type=jnp.float32
     )
     within = lax.rem(lax.broadcasted_iota(jnp.int32, (1, span), 1), PAGE).astype(jnp.float32)
     q = q_ref[...]
@@ -169,18 +177,20 @@
         out_ref[:, t] = total[t]
 
 
-def attend(info, pages, pieces, scale, rows):
+def attend(asked, pages, pieces, scale):
     n_x, _, cores, _, _, hd = pages.shape
-    height = sum(piece.shape[0] for piece in pieces)
+    rows = asked.shape[1] // 2
+    out = jax.ShapeDtypeStruct((n_x, len(STEPS), cores, rows, hd), jnp.bfloat16)
+    height = out.size // hd
     return pl.pallas_call(
         functools.partial(attend_kernel, scale),
         in_specs=[VMEM] * (2 + len(pieces)),
         out_specs=VMEM,
-        out_shape=jax.ShapeDtypeStruct((n_x, len(STEPS), cores, rows, hd), jnp.bfloat16),
+        out_shape=out,
         scratch_shapes=[pltpu.VMEM((height, hd), jnp.bfloat16), pltpu.VMEM((height, hd), jnp.float32)],
-        compiler_params=pltpu.CompilerParams(vmem_limit_bytes=40 * 1024 * 1024),
+        compiler_params=pltpu.CompilerParams(vmem_limit_bytes=16 * 1024 * 1024),
         name="attend",
-    )(info, pages, *pieces)
+    )(asked, pages, *pieces)
 
 
 def finish_kernel(scale, back_ref, proj_ref, input_ref, gain_ref, weight_ref, out_ref):
@@ -216,7 +226,7 @@
         in_specs=[VMEM] * 5,
         out_specs=VMEM,
         out_shape=jax.ShapeDtypeStruct(cand_input.shape, cand_input.dtype),
-        compiler_params=pltpu.CompilerParams(vmem_limit_bytes=40 * 1024 * 1024),
+        compiler_params=pltpu.CompilerParams(vmem_limit_bytes=16 * 1024 * 1024),
         name="finish",
     )(back, cand_proj, cand_input, out_gain.reshape(1, -1), out_weight)
 
@@ -228,19 +238,17 @@
     hd = width // HEADS
     scale = hd ** (-0.5)
     n_z = lax.axis_size("z")
-    z = lax.axis_index("z")
     owners, own_slots = page_owner.reshape(-1), page_slot.reshape(-1)
 
-    sent = announce(owners, own_slots, lengths, block_mask[0].T, cand_proj, n_z)
-    told = exchange(sent, SPREAD)
-    pages = split_pages(owners, own_slots, told, kv_pool)
-    pages, told = lax.optimization_barrier((pages, told))
+    sent = announce(owners, own_slots, lengths, block_mask[0].T, n_z, rows, hd)
+    told = exchange(sent, ("z",))
+    told, asked = lax.optimization_barrier((told, ask(cand_proj, sent)))
+    asked = exchange(asked, ("x", "c"))
+    pages = split_pages(told, kv_pool)
+    pages, asked = lax.optimization_barrier((pages, asked))
     got = exchange(pages.reshape((-1,) + pages.shape[3:]), PAGES).reshape(pages.shape)
-    told = told.reshape(n_z, HEADS, rows, hd)
-    below = lax.dynamic_slice(told, ((z + n_z - 1) % n_z, 0, 0, 0), (1, HEADS, 1, hd)).reshape(HEADS, hd)
-    info = shift(below, "z", -1)
-    pieces = gather_queries(lax.dynamic_index_in_dim(told, z, 0, keepdims=False).reshape(-1, hd))
-    part = attend(info, got, pieces, scale, rows)
+    pieces = gather_queries(asked[:, :rows].reshape(-1, hd))
+    part = attend(asked, got, pieces, scale)
     back = exchange(part.reshape(-1, rows, hd), SUMS).reshape(part.shape)
     return finish(back, cand_proj, cand_input, out_gain, out_weight, scale)
 

time: 93 us -> 92.2 us (level)
  blocking collectives: 50.2 us -> 22.2 us
  waiting for transfers between devices: 6.71 us -> 20.6 us
  starting transfers between devices: 25.1 us -> 37.4 us
  Pallas kernels: 7.96 us -> 9.06 us
    all_to_all x2 -> x1, blocking collectives: 50.2 us -> 22.2 us  [exchange(): return lax.all_to_all(array, axes, split_axis=0, concat_axis=0, tiled=True)]
    all_to_all x1 -> x3, starting transfers between devices: 4.86 us -> 22.3 us  [exchange(): return lax.all_to_all(array, axes, split_axis=0, concat_axis=0, tiled=True)]
    all_to_all x1 -> x3, waiting for transfers between devices: 4.39 us -> 13.3 us  [exchange(): return lax.all_to_all(array, axes, split_axis=0, concat_axis=0, tiled=True)]
    ppermute x5 -> x4, starting transfers between devices: 20.2 us -> 15.1 us  [shift(): return lax.ppermute(array, axis, [(i, (i + step) % n) for i in range(n)])]
    ppermute x5 -> x4, waiting for transfers between devices: 2.31 us -> 7.34 us  [shift(): return lax.ppermute(array, axis, [(i, (i + step) % n) for i in range(n)])]
    dynamic_slice x2 -> x0, local copies, waits for them, and re-layouts: 1.49 us -> none  [the longest x1 0.77 us: on_device(): lax.dynamic_index_in_dim(told, z, 0, keepdims=False).reshape(-1, hd)]
    unnamed x9 -> x14, local copies, waits for them, and re-layouts: 0.03 us -> 1.48 us
    pallas_call x2 -> x3, Pallas kernels: 4.2 us -> 5.31 us  [the longest x1 2.45 us: split_pages(): pl.pallas_call(split_pages_kernel, in_specs=[VMEM, VMEM], out_specs=HBM,...]
  transfers between devices with their start and end apart: 6 -> 7, of which waited for: 2 -> 5; matrix products, arithmetic and copies ran while one was open for 2% -> 0% of each run, Pallas kernels for 0% -> 4%
where the time goes in v5:
time: 92.2 us; the launch traced here: 91.5 us
  starting transfers between devices  37.4 us (41%)
  blocking collectives  22.2 us (24%)
  waiting for transfers between devices  20.6 us (22%)
  Pallas kernels  9.06 us (10%)
  local copies, waits for them, and re-layouts  1.48 us (2%)
    all_to_all x3, starting transfers between devices, exchange(): return lax.all_to_all(array, axes, split_axis=0, concat_axis=0, tiled=True)  22.3 us
    all_to_all x1, blocking collectives, exchange(): return lax.all_to_all(array, axes, split_axis=0, concat_axis=0, tiled=True)  22.2 us
    ppermute x4, starting transfers between devices, shift(): return lax.ppermute(array, axis, [(i, (i + step) % n) for i in range(n)])  15.1 us
    all_to_all x3, waiting for transfers between devices, exchange(): return lax.all_to_all(array, axes, split_axis=0, concat_axis=0, tiled=True)  13.3 us
    ppermute x4, waiting for transfers between devices, shift(): return lax.ppermute(array, axis, [(i, (i + step) % n) for i in range(n)])  7.34 us
    pallas_call x1, Pallas kernels, attend(): pl.pallas_call(functools.partial(attend_kernel, scale), in_specs=[VMEM] *...  2.48 us
    pallas_call x1, Pallas kernels, split_pages(): pl.pallas_call(split_pages_kernel, in_specs=[VMEM, VMEM], out_specs=HBM,...  2.45 us
  transfers between devices with their start and end apart: 7, of which 5 were waited for; matrix products, arithmetic and copies ran while one was open for 0% of the time, Pallas kernels for 4%

profile of v5, /device:TPU:1, one launch (start us, length us, event | category | flops | bytes accessed | tf_op | source)
XLA Modules:
  0.0 91.5 jit_solution(2760852699083400205)
XLA Ops:
  0.7 1.4 %announce.1.info_ref = bf16[8,16,128]{2,1,0:T(8,128)(2,1)} custom-call(s32[8]{0:T(128)} %bitcast.21, s32[8]{0:T(128)} %bitcast.22, s32[1]{0:T(128)S(6)} %copy.10.length_ref, s32[2,8]{1,0:T(2,128)} %bitcast.20), custom_call_target="tpu_custom_call" | custom-call | tf_op jit(solution)/shard_map/announce/pallas_call | solution.py:68
  2.1 10.9 %all-to-all-start = ((bf16[8,16,128]{2,1,0:T(8,128)(2,1)}), bf16[8,16,128]{2,1,0:T(8,128)(2,1)S(1)}, u32[]{:S(2)}, u32[]{:S(2)}) async-start(bf16[8,16,128]{2,1,0:T(8,128)(2,1)} %announce.1.info_ref), calls=%async_computation | async-start | bytes 65536 | tf_op jit(solution)/shard_map/all_to_all | solution.py:30
  12.9 1.4 %ask.1 = bf16[8,32,128]{2,1,0:T(8,128)(2,1)} custom-call(bf16[16,4096]{1,0:T(8,128)(2,1)} %proj_ref.1, bf16[8,16,128]{2,1,0:T(8,128)(2,1)} %announce.1.info_ref), custom_call_target="tpu_custom_call" | custom-call | tf_op jit(solution)/shard_map/ask/pallas_call | solution.py:88
  14.4 5.4 %all-to-all-done.told_ref = bf16[8,16,128]{2,1,0:T(8,128)(2,1)S(1)} async-done(((bf16[8,16,128]{2,1,0:T(8,128)(2,1)}), bf16[8,16,128]{2,1,0:T(8,128)(2,1)S(1)}, u32[]{:S(2)}, u32[]{:S(2)}) %all-to-all-start) | async-done | bytes 32800 | tf_op jit(solution)/shard_map/all_to_all | solution.py:30
  19.8 0.0 copy-start.6
  19.8 6.4 %all-to-all-start.1 = ((bf16[8,32,128]{2,1,0:T(8,128)(2,1)}), bf16[8,32,128]{2,1,0:T(8,128)(2,1)S(1)}, u32[]{:S(2)}, u32[]{:S(2)}) async-start(bf16[8,32,128]{2,1,0:T(8,128)(2,1)} %ask.1), calls=%async_computation.1 | async-start | bytes 131072 | tf_op jit(solution)/shard_map/all_to_all | solution.py:30
  26.2 0.0 copy-done.6
  26.2 2.4 %split_pages.1 = bf16[4,8,2,2,32,128]{5,4,3,2,1,0:T(8,128)(2,1)} custom-call(bf16[8,16,128]{2,1,0:T(8,128)(2,1)} %copy-done.6, bf16[8,2,32,1024]{3,2,1,0:T(8,128)(2,1)} %pool_ref.1), custom_call_target="tpu_custom_call" | custom-call | tf_op jit(solution)/shard_map/split_pages/pallas_call | solution.py:121
  28.7 2.4 %all-to-all-done.1.asked_ref = bf16[8,32,128]{2,1,0:T(8,128)(2,1)S(1)} async-done(((bf16[8,32,128]{2,1,0:T(8,128)(2,1)}), bf16[8,32,128]{2,1,0:T(8,128)(2,1)S(1)}, u32[]{:S(2)}, u32[]{:S(2)}) %all-to-all-start.1) | async-done | bytes 65568 | tf_op jit(solution)/shard_map/all_to_all | solution.py:30
  31.1 0.0 copy-start
  31.1 0.0 copy-start.1
  31.1 0.0 copy-start.4
  31.1 0.0 copy-start.5
  31.1 5.0 %all-to-all-start.2 = ((bf16[64,2,32,128]{3,2,1,0:T(8,128)(2,1)}), bf16[64,2,32,128]{3,2,1,0:T(8,128)(2,1)S(1)}, u32[]{:S(2)}, u32[]{:S(2)}) async-start(bf16[64,2,32,128]{3,2,1,0:T(8,128)(2,1)} %bitcast.15), calls=%async_computation.2 | async-start | bytes 2097152 | tf_op jit(solution)/shard_map/all_to_all | solution.py:30
  36.1 6.7 %collective-permute-start.1 = (bf16[128,128]{1,0:T(8,128)(2,1)S(1)}, bf16[128,128]{1,0:T(8,128)(2,1)S(1)}, u32[]{:S(2)}, u32[]{:S(2)}) collective-permute-start(bf16[128,128]{1,0:T(8,128)(2,1)S(1)} %bitcast.16), channel_id=1, source_target_pairs={{0,40},{8,48},{16,56},{24,0},{32,8},{40,16},{48,24},{56,32},{1,41}... | collective-permute-start | bytes 98312 | tf_op jit(solution)/shard_map/ppermute | solution.py:35
  42.8 1.9 %collective-permute-start = (bf16[128,128]{1,0:T(8,128)(2,1)S(1)}, bf16[128,128]{1,0:T(8,128)(2,1)S(1)}, u32[]{:S(2)}, u32[]{:S(2)}) collective-permute-start(bf16[128,128]{1,0:T(8,128)(2,1)S(1)} %bitcast.17), channel_id=1, source_target_pairs={{0,24},{8,32},{16,40},{24,48},{32,56},{40,0},{48,8},{56,16},{1,25}... | collective-permute-start | bytes 98312 | tf_op jit(solution)/shard_map/ppermute | solution.py:35
  44.7 0.0 collective-permute-done.1.rest_1_
  44.7 6.0 %collective-permute-done.rest_0_ = bf16[128,128]{1,0:T(8,128)(2,1)S(1)} collective-permute-done((bf16[128,128]{1,0:T(8,128)(2,1)S(1)}, bf16[128,128]{1,0:T(8,128)(2,1)S(1)}, u32[]{:S(2)}, u32[]{:S(2)}) %collective-permute-start) | collective-permute-done | bytes 32800 | tf_op jit(solution)/shard_map/ppermute | solution.py:35
  50.8 2.3 %collective-permute-start.2 = (bf16[384,128]{1,0:T(8,128)(2,1)S(1)}, bf16[384,128]{1,0:T(8,128)(2,1)S(1)}, u32[]{:S(2)}, u32[]{:S(2)}) collective-permute-start(bf16[384,128]{1,0:T(8,128)(2,1)S(1)} %pad_maximum_fusion), channel_id=1, source_target_pairs={{0,8},{8,16},{16,24},{24,32},{32,40},{40,48},{48,56},{56,0},{1,9},... | collective-permute-start | bytes 294920 | tf_op jit(solution)/shard_map/ppermute | solution.py:35
  53.1 4.2 %collective-permute-start.3 = (bf16[256,128]{1,0:T(8,128)(2,1)S(1)}, bf16[256,128]{1,0:T(8,128)(2,1)S(1)}, u32[]{:S(2)}, u32[]{:S(2)}) collective-permute-start(bf16[256,128]{1,0:T(8,128)(2,1)S(1)} %pad_maximum_fusion.1), channel_id=1, source_target_pairs={{0,56},{8,0},{16,8},{24,16},{32,24},{40,32},{48,40},{56,48},{1,57}... | collective-permute-start | bytes 196616 | tf_op jit(solution)/shard_map/ppermute | solution.py:35
  57.3 1.3 %collective-permute-done.3.rest_3_ = bf16[256,128]{1,0:T(8,128)(2,1)S(1)} collective-permute-done((bf16[256,128]{1,0:T(8,128)(2,1)S(1)}, bf16[256,128]{1,0:T(8,128)(2,1)S(1)}, u32[]{:S(2)}, u32[]{:S(2)}) %collective-permute-start.3) | collective-permute-done | bytes 65568 | tf_op jit(solution)/shard_map/ppermute | solution.py:35
  58.6 0.6 copy-done.2
  59.2 0.0 collective-permute-done.2.rest_2_
  59.2 5.5 %all-to-all-done.2 = bf16[64,2,32,128]{3,2,1,0:T(8,128)(2,1)S(1)} async-done(((bf16[64,2,32,128]{3,2,1,0:T(8,128)(2,1)}), bf16[64,2,32,128]{3,2,1,0:T(8,128)(2,1)S(1)}, u32[]{:S(2)}, u32[]{:S(2)}) %all-to-all-start.2) | async-done | bytes 1048608 | tf_op jit(solution)/shard_map/all_to_all | solution.py:30
  64.7 0.8 copy-done.3
  65.5 2.5 %attend.1 = bf16[4,8,2,16,128]{4,3,2,1,0:T(8,128)(2,1)S(1)} custom-call(bf16[8,32,128]{2,1,0:T(8,128)(2,1)S(1)} %all-to-all-done.1.asked_ref, bf16[4,8,2,2,32,128]{5,4,3,2,1,0:T(8,128)(2,1)S(1)} %bitcast.11, bf16[128,128]{1,0:T(8,128)(2,1)S(1)} %collective-permute-done.rest_0_, bf16[128,128]{1,0:T(8,128)(2,1)S(1)} %collective-permute-done.1.rest_1_, ...), custom_call_target="tpu_custom_call" | custom-call | tf_op jit(solution)/shard_map/attend/pallas_call | solution.py:185
  68.0 22.2 %all_to_all.20 = bf16[64,16,128]{2,1,0:T(8,128)(2,1)S(1)} all-to-all(bf16[64,16,128]{2,1,0:T(8,128)(2,1)S(1)} %bitcast.12), channel_id=1, replica_groups=mesh['z'=8,'y'=8,'x'=4,'c'=2] {'x','y','c'}, dimensions={0} | all-to-all | bytes 524288 | tf_op jit(solution)/shard_map/all_to_all | solution.py:30
  90.2 0.0 copy-done
  90.2 0.0 copy-done.1
  90.2 0.0 copy-done.4
  90.2 0.0 copy-done.5
  90.2 1.3 %finish.1 = bf16[16,1024]{1,0:T(8,128)(2,1)} custom-call(bf16[4,8,2,16,128]{4,3,2,1,0:T(8,128)(2,1)S(1)} %bitcast.13, bf16[16,4096]{1,0:T(8,128)(2,1)S(1)} %copy-done.1, bf16[16,1024]{1,0:T(8,128)(2,1)S(1)} %copy-done.4, f32[1,1024]{1,0:T(1,128)S(1)} %bitcast.14, bf16[1024,1024]{1,0:T(8,128)(2,1)S(1)} %copy-done), custom_call_target="tpu_custom_call" | custom-call | tf_op jit(solution)/shard_map/finish/pallas_call | solution.py:224
  (5 shorter events, 0.0 us)
Async XLA Ops:
  2.1 17.7 %all-to-all-start = ((bf16[8,16,128]{2,1,0:T(8,128)(2,1)}), bf16[8,16,128]{2,1,0:T(8,128)(2,1)S(1)}, u32[]{:S(2)}, u32[]{:S(2)}) async-start(bf16[8,16,128]{2,1,0:T(8,128)(2,1)} %announce.1.info_ref), calls=%async_computation | async-start | bytes 65536 | tf_op jit(solution)/shard_map/all_to_all | solution.py:30
  19.8 6.4 %copy-start.6 = (bf16[8,16,128]{2,1,0:T(8,128)(2,1)}, bf16[8,16,128]{2,1,0:T(8,128)(2,1)S(1)}, u32[]{:S(2)}) copy-start(bf16[8,16,128]{2,1,0:T(8,128)(2,1)S(1)} %all-to-all-done.told_ref) | copy-start | bytes 98308
  19.8 11.3 %all-to-all-start.1 = ((bf16[8,32,128]{2,1,0:T(8,128)(2,1)}), bf16[8,32,128]{2,1,0:T(8,128)(2,1)S(1)}, u32[]{:S(2)}, u32[]{:S(2)}) async-start(bf16[8,32,128]{2,1,0:T(8,128)(2,1)} %ask.1), calls=%async_computation.1 | async-start | bytes 131072 | tf_op jit(solution)/shard_map/all_to_all | solution.py:30
  31.1 59.1 %copy-start = (bf16[1024,1024]{1,0:T(8,128)(2,1)S(1)}, bf16[1024,1024]{1,0:T(8,128)(2,1)}, u32[]{:S(2)}) copy-start(bf16[1024,1024]{1,0:T(8,128)(2,1)} %weight_ref.1) | copy-start | bytes 6291460
  31.1 59.1 %copy-start.1 = (bf16[16,4096]{1,0:T(8,128)(2,1)S(1)}, bf16[16,4096]{1,0:T(8,128)(2,1)}, u32[]{:S(2)}) copy-start(bf16[16,4096]{1,0:T(8,128)(2,1)} %proj_ref.1) | copy-start | bytes 393220
  31.1 59.1 %copy-start.4 = (bf16[16,1024]{1,0:T(8,128)(2,1)S(1)}, bf16[16,1024]{1,0:T(8,128)(2,1)}, u32[]{:S(2)}) copy-start(bf16[16,1024]{1,0:T(8,128)(2,1)} %input_ref.1) | copy-start | bytes 98308
  31.1 59.1 %copy-start.5 = (f32[1024]{0:T(1024)S(1)}, f32[1024]{0:T(1024)}, u32[]{:S(2)}) copy-start(f32[1024]{0:T(1024)} %param.16) | copy-start | bytes 12292
  31.1 33.6 %all-to-all-start.2 = ((bf16[64,2,32,128]{3,2,1,0:T(8,128)(2,1)}), bf16[64,2,32,128]{3,2,1,0:T(8,128)(2,1)S(1)}, u32[]{:S(2)}, u32[]{:S(2)}) async-start(bf16[64,2,32,128]{3,2,1,0:T(8,128)(2,1)} %bitcast.15), calls=%async_computation.2 | async-start | bytes 2097152 | tf_op jit(solution)/shard_map/all_to_all | solution.py:30
  36.1 8.6 %collective-permute-start.1 = (bf16[128,128]{1,0:T(8,128)(2,1)S(1)}, bf16[128,128]{1,0:T(8,128)(2,1)S(1)}, u32[]{:S(2)}, u32[]{:S(2)}) collective-permute-start(bf16[128,128]{1,0:T(8,128)(2,1)S(1)} %bitcast.16), channel_id=1, source_target_pairs={{0,40},{8,48},{16,56},{24,0},{32,8},{40,16},{48,24},{56,32},{1,41}... | collective-permute-start | bytes 98312 | tf_op jit(solution)/shard_map/ppermute | solution.py:35
  42.8 8.0 %collective-permute-start = (bf16[128,128]{1,0:T(8,128)(2,1)S(1)}, bf16[128,128]{1,0:T(8,128)(2,1)S(1)}, u32[]{:S(2)}, u32[]{:S(2)}) collective-permute-start(bf16[128,128]{1,0:T(8,128)(2,1)S(1)} %bitcast.17), channel_id=1, source_target_pairs={{0,24},{8,32},{16,40},{24,48},{32,56},{40,0},{48,8},{56,16},{1,25}... | collective-permute-start | bytes 98312 | tf_op jit(solution)/shard_map/ppermute | solution.py:35
  50.8 8.5 %collective-permute-start.2 = (bf16[384,128]{1,0:T(8,128)(2,1)S(1)}, bf16[384,128]{1,0:T(8,128)(2,1)S(1)}, u32[]{:S(2)}, u32[]{:S(2)}) collective-permute-start(bf16[384,128]{1,0:T(8,128)(2,1)S(1)} %pad_maximum_fusion), channel_id=1, source_target_pairs={{0,8},{8,16},{16,24},{24,32},{32,40},{40,48},{48,56},{56,0},{1,9},... | collective-permute-start | bytes 294920 | tf_op jit(solution)/shard_map/ppermute | solution.py:35
  53.1 5.5 %collective-permute-start.3 = (bf16[256,128]{1,0:T(8,128)(2,1)S(1)}, bf16[256,128]{1,0:T(8,128)(2,1)S(1)}, u32[]{:S(2)}, u32[]{:S(2)}) collective-permute-start(bf16[256,128]{1,0:T(8,128)(2,1)S(1)} %pad_maximum_fusion.1), channel_id=1, source_target_pairs={{0,56},{8,0},{16,8},{24,16},{32,24},{40,32},{48,40},{56,48},{1,57}... | collective-permute-start | bytes 196616 | tf_op jit(solution)/shard_map/ppermute | solution.py:35
  58.6 0.6 copy-start.2
  64.7 0.8 copy-start.3

commit v6 on v5

--- a/solution.py
+++ b/solution.py
@@ -74,23 +74,36 @@
     )(owners, slots, lengths, seen)
 
 
-def ask_kernel(q_ref, info_ref, out_ref):
+def ask_kernel(scale, proj_ref, info_ref, out_ref, own_ref, u_ref):
     rows, hd = info_ref.shape[1:]
-    query = silu(q_ref[...].astype(jnp.float32)).astype(jnp.bfloat16)
+
+    def act(block, h):
+        start = (block * HEADS + h) * hd
+        return silu(proj_ref[:, start : start + hd].astype(jnp.float32)).astype(jnp.bfloat16)
+
     for h in range(HEADS):
-        out_ref[h, :rows] = query[:, h * hd : (h + 1) * hd]
+        part = slice(h * hd, (h + 1) * hd)
+        query = act(2, h)
+        out_ref[h, :rows] = query
         out_ref[h, rows:] = info_ref[0]
-
-
-def ask(cand_proj, info):
-    rows, width = cand_proj.shape[0], cand_proj.shape[1] // 4
-    hd = width // HEADS
-    return pl.pallas_call(
-        ask_kernel,
-        grid=(1,),
-        in_specs=[pl.BlockSpec((rows, width), lambda i: (0, 2)), VMEM],
-        out_specs=VMEM,
-        out_shape=jax.ShapeDtypeStruct((HEADS, 2 * rows, hd), jnp.bfloat16),
+        score = query.astype(jnp.float32) * act(3, h).astype(jnp.float32)
+        own = silu(jnp.sum(score, axis=1, keepdims=True) * scale).astype(jnp.bfloat16)
+        own_ref[:, part] = own.astype(jnp.float32) * act(1, h).astype(jnp.float32)
+        u_ref[:, part] = act(0, h)
+
+
+def ask(cand_proj, info, scale):
+    rows, hd = info.shape[1:]
+    width = cand_proj.shape[1] // 4
+    return pl.pallas_call(
+        functools.partial(ask_kernel, scale),
+        in_specs=[VMEM] * 2,
+        out_specs=[VMEM] * 3,
+        out_shape=[
+            jax.ShapeDtypeStruct((HEADS, 2 * rows, hd), jnp.bfloat16),
+            jax.ShapeDtypeStruct((rows, width), jnp.float32),
+            jax.ShapeDtypeStruct((rows, width), jnp.bfloat16),
+        ],
         name="ask",
     )(cand_proj, info)
 
@@ -128,33 +141,33 @@
     )(told, kv_pool)
 
 
-STEPS = (0, -3, 3, -1, -4, 2, 1, -2)
+STEPS = (0, -1, 1, -3, -2, 3, 4, 2)
 
 
 def gather_queries(row):
-    below3, above3 = shift(row, "y", 3), shift(row, "y", -3)
-    below = shift(jnp.concatenate([row, below3, above3]), "y", 1)
-    above = shift(jnp.concatenate([row, below3]), "y", -1)
-    return below3, above3, below, above
-
-
-def attend_kernel(scale, asked_ref, kv_ref, *rest):
+    below, above = shift(row, "y", 1), shift(row, "y", -1)
+    below3 = shift(jnp.concatenate([row, above]), "y", 3)
+    above3 = shift(jnp.concatenate([row, above, below]), "y", -3)
+    return below, above, below3, above3
+
+
+def attend_kernel(scale, info_ref, row_ref, kv_ref, *rest):
     pieces, (out_ref, q_ref, acc_ref) = rest[:-3], rest[-3:]
     n_x, n_y, cores, rows, hd = out_ref.shape
     sources, tiles = n_x * cores, len(STEPS)
     span = sources * PAGE
     height = n_x * cores * rows
     y = lax.axis_index("y")
-    blocks = [asked_ref[:, :rows].reshape(height, hd)]
+    blocks = [row_ref[...]]
     for piece in pieces:
         blocks += [piece[b * height : (b + 1) * height, :] for b in range(piece.shape[0] // height)]
     for step, block in zip(STEPS, blocks):
         q_ref[pl.ds(lax.rem(y + (step + tiles), tiles) * height, height), :] = block
-    place = lax.broadcasted_iota(jnp.int32, (height, span), 1)
-    which = lax.broadcasted_iota(jnp.int32, (height, span), 0)
-    spread = (place // PAGE * rows == which).astype(jnp.bfloat16)
+    place = lax.broadcasted_iota(jnp.int32, (sources, span), 1)
+    which = lax.broadcasted_iota(jnp.int32, (sources, span), 0)
+    spread = (place // PAGE == which).astype(jnp.bfloat16)
     fields = lax.dot_general(
-        asked_ref[:, rows:].reshape(height, hd), spread, (((0,), (0,)), ((), ())), preferred_element_type=jnp.float32
+        info_ref[...], spread, (((0,), (0,)), ((), ())), preferred_element_type=jnp.float32
     )
     within = lax.rem(lax.broadcasted_iota(jnp.int32, (1, span), 1), PAGE).astype(jnp.float32)
     q = q_ref[...]
@@ -177,58 +190,48 @@
         out_ref[:, t] = total[t]
 
 
-def attend(asked, pages, pieces, scale):
+def attend(info, row, pages, pieces, scale):
     n_x, _, cores, _, _, hd = pages.shape
-    rows = asked.shape[1] // 2
+    rows = row.shape[0] // (n_x * cores)
     out = jax.ShapeDtypeStruct((n_x, len(STEPS), cores, rows, hd), jnp.bfloat16)
     height = out.size // hd
     return pl.pallas_call(
         functools.partial(attend_kernel, scale),
-        in_specs=[VMEM] * (2 + len(pieces)),
+        in_specs=[VMEM] * (3 + len(pieces)),
         out_specs=VMEM,
         out_shape=out,
         scratch_shapes=[pltpu.VMEM((height, hd), jnp.bfloat16), pltpu.VMEM((height, hd), jnp.float32)],
         compiler_params=pltpu.CompilerParams(vmem_limit_bytes=16 * 1024 * 1024),
         name="attend",
-    )(asked, pages, *pieces)
-
-
-def finish_kernel(scale, back_ref, proj_ref, input_ref, gain_ref, weight_ref, out_ref):
-    rows, width = input_ref.shape
-    hd = width // HEADS
-
-    def act(block, h):
-        start = block * width + h * hd
-        value = silu(proj_ref[:, start : start + hd].astype(jnp.float32))
-        return value.astype(jnp.bfloat16).astype(jnp.float32)
-
+    )(info, row, pages, *pieces)
+
+
+def finish_kernel(back_ref, own_ref, u_ref, gain_ref, input_ref, weight_ref, out_ref):
     attn = []
     for h in range(HEADS):
-        total = jnp.zeros((rows, hd), jnp.float32)
-        for y in range(back_ref.shape[1]):
+        total = back_ref[h // CORES, 0, h % CORES].astype(jnp.float32)
+        for y in range(1, back_ref.shape[1]):
             total += back_ref[h // CORES, y, h % CORES].astype(jnp.float32)
-        own = silu(jnp.sum(act(2, h) * act(3, h), axis=1, keepdims=True) * scale)
-        own = own.astype(jnp.bfloat16).astype(jnp.float32)
-        attn.append(total + own * act(1, h))
-    attn = jnp.concatenate(attn, axis=1)
+        attn.append(total)
+    attn = jnp.concatenate(attn, axis=1) + own_ref[...]
     mean = jnp.mean(attn, axis=1, keepdims=True)
     centered = attn - mean
     var = jnp.mean(centered * centered, axis=1, keepdims=True)
-    u_act = jnp.concatenate([act(0, h) for h in range(HEADS)], axis=1)
-    normed = (centered * lax.rsqrt(var + eps) * gain_ref[...] * u_act).astype(jnp.bfloat16)
+    gate = gain_ref[...] * u_ref[...].astype(jnp.float32)
+    normed = (centered * lax.rsqrt(var + eps) * gate).astype(jnp.bfloat16)
     out = jnp.dot(normed, weight_ref[...], preferred_element_type=jnp.float32)
     out_ref[...] = (input_ref[...].astype(jnp.float32) + out).astype(out_ref.dtype)
 
 
-def finish(back, cand_proj, cand_input, out_gain, out_weight, scale):
-    return pl.pallas_call(
-        functools.partial(finish_kernel, scale),
-        in_specs=[VMEM] * 5,
+def finish(back, own, u_act, out_gain, cand_input, out_weight):
+    return pl.pallas_call(
+        finish_kernel,
+        in_specs=[VMEM] * 6,
         out_specs=VMEM,
         out_shape=jax.ShapeDtypeStruct(cand_input.shape, cand_input.dtype),
         compiler_params=pltpu.CompilerParams(vmem_limit_bytes=16 * 1024 * 1024),
         name="finish",
-    )(back, cand_proj, cand_input, out_gain.reshape(1, -1), out_weight)
+    )(back, own, u_act, out_gain.reshape(1, -1), cand_input, out_weight)
 
 
 def on_device(
@@ -242,15 +245,16 @@
 
     sent = announce(owners, own_slots, lengths, block_mask[0].T, n_z, rows, hd)
     told = exchange(sent, ("z",))
-    told, asked = lax.optimization_barrier((told, ask(cand_proj, sent)))
+    asked, own, u_act = ask(cand_proj, sent, scale)
+    told, asked = lax.optimization_barrier((told, asked))
     asked = exchange(asked, ("x", "c"))
     pages = split_pages(told, kv_pool)
     pages, asked = lax.optimization_barrier((pages, asked))
     got = exchange(pages.reshape((-1,) + pages.shape[3:]), PAGES).reshape(pages.shape)
-    pieces = gather_queries(asked[:, :rows].reshape(-1, hd))
-    part = attend(asked, got, pieces, scale)
+    row, info = asked[:, :rows].reshape(-1, hd), asked[:, rows]
+    part = attend(info, row, got, gather_queries(row), scale)
     back = exchange(part.reshape(-1, rows, hd), SUMS).reshape(part.shape)
-    return finish(back, cand_proj, cand_input, out_gain, out_weight, scale)
+    return finish(back, own, u_act, out_gain, cand_input, out_weight)
 
 
 def solution(mesh):

time: 92.2 us -> 91.2 us (0.989)
  local copies, waits for them, and re-layouts: 1.48 us -> 0.06 us
    all_to_all x3, waiting for transfers between devices: 13.3 us -> 15.9 us  [exchange(): return lax.all_to_all(array, axes, split_axis=0, concat_axis=0, tiled=True)]
    ppermute x4, waiting for transfers between devices: 7.34 us -> 4.83 us  [shift(): return lax.ppermute(array, axis, [(i, (i + step) % n) for i in range(n)])]
    unnamed x14 -> x12, local copies, waits for them, and re-layouts: 1.48 us -> 0.02 us
  transfers between devices with their start and end apart: 7 -> 7, of which waited for: 5 -> 4; matrix products, arithmetic and copies ran while one was open for 0% -> 0% of each run, Pallas kernels for 4% -> 5%
where the time goes in v6:
time: 91.2 us; the launch traced here: 90.6 us
  starting transfers between devices  37.6 us (41%)
  blocking collectives  22.2 us (24%)
  waiting for transfers between devices  20.7 us (23%)
  Pallas kernels  9.23 us (10%)
    all_to_all x3, starting transfers between devices, exchange(): return lax.all_to_all(array, axes, split_axis=0, concat_axis=0, tiled=True)  22.3 us
    all_to_all x1, blocking collectives, exchange(): return lax.all_to_all(array, axes, split_axis=0, concat_axis=0, tiled=True)  22.2 us
    all_to_all x3, waiting for transfers between devices, exchange(): return lax.all_to_all(array, axes, split_axis=0, concat_axis=0, tiled=True)  15.9 us
    ppermute x4, starting transfers between devices, shift(): return lax.ppermute(array, axis, [(i, (i + step) % n) for i in range(n)])  15.3 us
    ppermute x4, waiting for transfers between devices, shift(): return lax.ppermute(array, axis, [(i, (i + step) % n) for i in range(n)])  4.83 us
    pallas_call x1, Pallas kernels, attend(): pl.pallas_call(functools.partial(attend_kernel, scale), in_specs=[VMEM] *...  2.48 us
    pallas_call x1, Pallas kernels, split_pages(): pl.pallas_call(split_pages_kernel, in_specs=[VMEM, VMEM], out_specs=HBM,...  2.45 us
  transfers between devices with their start and end apart: 7, of which 4 were waited for; matrix products, arithmetic and copies ran while one was open for 0% of the time, Pallas kernels for 5%

profile of v6, /device:TPU:1, one launch (start us, length us, event | category | flops | bytes accessed | tf_op | source)
XLA Modules:
  0.0 90.6 jit_solution(7972143185505560218)
XLA Ops:
  0.7 1.4 %announce.1.info_ref = bf16[8,16,128]{2,1,0:T(8,128)(2,1)} custom-call(s32[8]{0:T(128)} %bitcast.24, s32[8]{0:T(128)} %bitcast.25, s32[1]{0:T(128)S(6)} %copy.13.length_ref, s32[2,8]{1,0:T(2,128)} %bitcast.23), custom_call_target="tpu_custom_call" | custom-call | tf_op jit(solution)/shard_map/announce/pallas_call | solution.py:68
  2.1 10.9 %all-to-all-start = ((bf16[8,16,128]{2,1,0:T(8,128)(2,1)}), bf16[8,16,128]{2,1,0:T(8,128)(2,1)S(1)}, u32[]{:S(2)}, u32[]{:S(2)}) async-start(bf16[8,16,128]{2,1,0:T(8,128)(2,1)} %announce.1.info_ref), calls=%async_computation | async-start | bytes 65536 | tf_op jit(solution)/shard_map/all_to_all | solution.py:30
  12.9 1.7 %ask.1 = (bf16[8,32,128]{2,1,0:T(8,128)(2,1)}, f32[16,1024]{1,0:T(8,128)}, bf16[16,1024]{1,0:T(8,128)(2,1)}) custom-call(bf16[16,4096]{1,0:T(8,128)(2,1)} %proj_ref.1, bf16[8,16,128]{2,1,0:T(8,128)(2,1)} %announce.1.info_ref), custom_call_target="tpu_custom_call" | custom-call | tf_op jit(solution)/shard_map/ask/pallas_call | solution.py:98
  14.6 5.2 %all-to-all-done.told_ref = bf16[8,16,128]{2,1,0:T(8,128)(2,1)S(1)} async-done(((bf16[8,16,128]{2,1,0:T(8,128)(2,1)}), bf16[8,16,128]{2,1,0:T(8,128)(2,1)S(1)}, u32[]{:S(2)}, u32[]{:S(2)}) %all-to-all-start) | async-done | bytes 32800 | tf_op jit(solution)/shard_map/all_to_all | solution.py:30
  19.8 0.0 copy-start.5
  19.8 6.4 %all-to-all-start.1 = ((bf16[8,32,128]{2,1,0:T(8,128)(2,1)}), bf16[8,32,128]{2,1,0:T(8,128)(2,1)S(1)}, u32[]{:S(2)}, u32[]{:S(2)}) async-start(bf16[8,32,128]{2,1,0:T(8,128)(2,1)} %get-tuple-element.14), calls=%async_computation.1 | async-start | bytes 131072 | tf_op jit(solution)/shard_map/all_to_all | solution.py:30
  26.2 0.0 copy-done.5
  26.2 2.4 %split_pages.1 = bf16[4,8,2,2,32,128]{5,4,3,2,1,0:T(8,128)(2,1)} custom-call(bf16[8,16,128]{2,1,0:T(8,128)(2,1)} %copy-done.5, bf16[8,2,32,1024]{3,2,1,0:T(8,128)(2,1)} %pool_ref.1), custom_call_target="tpu_custom_call" | custom-call | tf_op jit(solution)/shard_map/split_pages/pallas_call | solution.py:134
  28.7 2.4 %all-to-all-done.1 = bf16[8,32,128]{2,1,0:T(8,128)(2,1)S(1)} async-done(((bf16[8,32,128]{2,1,0:T(8,128)(2,1)}), bf16[8,32,128]{2,1,0:T(8,128)(2,1)S(1)}, u32[]{:S(2)}, u32[]{:S(2)}) %all-to-all-start.1) | async-done | bytes 65568 | tf_op jit(solution)/shard_map/all_to_all | solution.py:30
  31.1 0.0 copy-start
  31.1 0.0 copy-start.1
  31.1 0.0 copy-start.2
  31.1 0.0 copy-start.3
  31.1 0.0 copy-start.4
  31.1 5.0 %all-to-all-start.2 = ((bf16[64,2,32,128]{3,2,1,0:T(8,128)(2,1)}), bf16[64,2,32,128]{3,2,1,0:T(8,128)(2,1)S(1)}, u32[]{:S(2)}, u32[]{:S(2)}) async-start(bf16[64,2,32,128]{3,2,1,0:T(8,128)(2,1)} %bitcast.22), calls=%async_computation.2 | async-start | bytes 2097152 | tf_op jit(solution)/shard_map/all_to_all | solution.py:30
  36.1 5.1 %collective-permute-start.1 = (bf16[128,128]{1,0:T(8,128)(2,1)S(1)}, bf16[128,128]{1,0:T(8,128)(2,1)S(1)}, u32[]{:S(2)}, u32[]{:S(2)}) collective-permute-start(bf16[128,128]{1,0:T(8,128)(2,1)S(1)} %bitcast.16), channel_id=1, source_target_pairs={{0,56},{8,0},{16,8},{24,16},{32,24},{40,32},{48,40},{56,48},{1,57}... | collective-permute-start | bytes 98312 | tf_op jit(solution)/shard_map/ppermute | solution.py:35
  41.3 1.9 %collective-permute-start = (bf16[128,128]{1,0:T(8,128)(2,1)S(1)}, bf16[128,128]{1,0:T(8,128)(2,1)S(1)}, u32[]{:S(2)}, u32[]{:S(2)}) collective-permute-start(bf16[128,128]{1,0:T(8,128)(2,1)S(1)} %bitcast.17), channel_id=1, source_target_pairs={{0,8},{8,16},{16,24},{24,32},{32,40},{40,48},{48,56},{56,0},{1,9},... | collective-permute-start | bytes 98312 | tf_op jit(solution)/shard_map/ppermute | solution.py:35
  43.2 0.0 collective-permute-done.1.rest_1_
  43.2 4.7 %collective-permute-start.2 = (bf16[256,128]{1,0:T(8,128)(2,1)S(1)}, bf16[256,128]{1,0:T(8,128)(2,1)S(1)}, u32[]{:S(2)}, u32[]{:S(2)}) collective-permute-start(bf16[256,128]{1,0:T(8,128)(2,1)S(1)} %pad_maximum_fusion.1), channel_id=1, source_target_pairs={{0,24},{8,32},{16,40},{24,48},{32,56},{40,0},{48,8},{56,16},{1,25}... | collective-permute-start | bytes 196616 | tf_op jit(solution)/shard_map/ppermute | solution.py:35
  47.9 0.0 collective-permute-done.rest_0_
  48.0 3.6 %collective-permute-start.3 = (bf16[384,128]{1,0:T(8,128)(2,1)S(1)}, bf16[384,128]{1,0:T(8,128)(2,1)S(1)}, u32[]{:S(2)}, u32[]{:S(2)}) collective-permute-start(bf16[384,128]{1,0:T(8,128)(2,1)S(1)} %pad_maximum_fusion), channel_id=1, source_target_pairs={{0,40},{8,48},{16,56},{24,0},{32,8},{40,16},{48,24},{56,32},{1,41}... | collective-permute-start | bytes 294920 | tf_op jit(solution)/shard_map/ppermute | solution.py:35
  51.6 0.0 collective-permute-done.2.rest_2_
  51.6 4.8 %collective-permute-done.3.rest_3_ = bf16[384,128]{1,0:T(8,128)(2,1)S(1)} collective-permute-done((bf16[384,128]{1,0:T(8,128)(2,1)S(1)}, bf16[384,128]{1,0:T(8,128)(2,1)S(1)}, u32[]{:S(2)}, u32[]{:S(2)}) %collective-permute-start.3) | collective-permute-done | bytes 98336 | tf_op jit(solution)/shard_map/ppermute | solution.py:35
  56.4 8.3 %all-to-all-done.2 = bf16[64,2,32,128]{3,2,1,0:T(8,128)(2,1)S(1)} async-done(((bf16[64,2,32,128]{3,2,1,0:T(8,128)(2,1)}), bf16[64,2,32,128]{3,2,1,0:T(8,128)(2,1)S(1)}, u32[]{:S(2)}, u32[]{:S(2)}) %all-to-all-start.2) | async-done | bytes 1048608 | tf_op jit(solution)/shard_map/all_to_all | solution.py:30
  64.7 2.5 %attend.1 = bf16[4,8,2,16,128]{4,3,2,1,0:T(8,128)(2,1)S(1)} custom-call(bf16[8,128]{1,0:T(8,128)(2,1)S(1)} %slice_bitcast_fusion.info_ref, bf16[128,128]{1,0:T(8,128)(2,1)S(1)} %bitcast.20, bf16[4,8,2,2,32,128]{5,4,3,2,1,0:T(8,128)(2,1)S(1)} %bitcast.13, bf16[128,128]{1,0:T(8,128)(2,1)S(1)} %collective-permute-done.rest_0_, ...), custom_call_target="tpu_custom_call" | custom-call | tf_op jit(solution)/shard_map/attend/pallas_call | solution.py:198
  67.2 22.2 %all_to_all.20 = bf16[64,16,128]{2,1,0:T(8,128)(2,1)S(1)} all-to-all(bf16[64,16,128]{2,1,0:T(8,128)(2,1)S(1)} %bitcast.15), channel_id=1, replica_groups=mesh['z'=8,'y'=8,'x'=4,'c'=2] {'x','y','c'}, dimensions={0} | all-to-all | bytes 524288 | tf_op jit(solution)/shard_map/all_to_all | solution.py:30
  89.4 0.0 copy-done
  89.4 0.0 copy-done.1
  89.4 0.0 copy-done.2
  89.4 0.0 copy-done.3
  89.4 0.0 copy-done.4
  89.4 1.2 %finish.1 = bf16[16,1024]{1,0:T(8,128)(2,1)} custom-call(bf16[4,8,2,16,128]{4,3,2,1,0:T(8,128)(2,1)S(1)} %bitcast.14, f32[16,1024]{1,0:T(8,128)S(1)} %copy-done.1, bf16[16,1024]{1,0:T(8,128)(2,1)S(1)} %copy-done.3, f32[1,1024]{1,0:T(1,128)S(1)} %bitcast.21, bf16[16,1024]{1,0:T(8,128)(2,1)S(1)} %copy-done.2, bf16[1024,1024]{1,0:T(8,128)(2,1)S(1)} %copy-done), custom_call_target="tpu_custom_call" | custom-call | tf_op jit(solution)/shard_map/finish/pallas_call | solution.py:227
  (5 shorter events, 0.1 us)
Async XLA Ops:
  2.1 17.7 %all-to-all-start = ((bf16[8,16,128]{2,1,0:T(8,128)(2,1)}), bf16[8,16,128]{2,1,0:T(8,128)(2,1)S(1)}, u32[]{:S(2)}, u32[]{:S(2)}) async-start(bf16[8,16,128]{2,1,0:T(8,128)(2,1)} %announce.1.info_ref), calls=%async_computation | async-start | bytes 65536 | tf_op jit(solution)/shard_map/all_to_all | solution.py:30
  19.8 6.4 %copy-start.5 = (bf16[8,16,128]{2,1,0:T(8,128)(2,1)}, bf16[8,16,128]{2,1,0:T(8,128)(2,1)S(1)}, u32[]{:S(2)}) copy-start(bf16[8,16,128]{2,1,0:T(8,128)(2,1)S(1)} %all-to-all-done.told_ref) | copy-start | bytes 98308
  19.8 11.3 %all-to-all-start.1 = ((bf16[8,32,128]{2,1,0:T(8,128)(2,1)}), bf16[8,32,128]{2,1,0:T(8,128)(2,1)S(1)}, u32[]{:S(2)}, u32[]{:S(2)}) async-start(bf16[8,32,128]{2,1,0:T(8,128)(2,1)} %get-tuple-element.14), calls=%async_computation.1 | async-start | bytes 131072 | tf_op jit(solution)/shard_map/all_to_all | solution.py:30
  31.1 58.3 %copy-start = (bf16[1024,1024]{1,0:T(8,128)(2,1)S(1)}, bf16[1024,1024]{1,0:T(8,128)(2,1)}, u32[]{:S(2)}) copy-start(bf16[1024,1024]{1,0:T(8,128)(2,1)} %weight_ref.1) | copy-start | bytes 6291460
  31.1 58.3 %copy-start.1 = (f32[16,1024]{1,0:T(8,128)S(1)}, f32[16,1024]{1,0:T(8,128)}, u32[]{:S(2)}) copy-start(f32[16,1024]{1,0:T(8,128)} %get-tuple-element.17.own_ref) | copy-start | bytes 196612
  31.1 58.3 %copy-start.2 = (bf16[16,1024]{1,0:T(8,128)(2,1)S(1)}, bf16[16,1024]{1,0:T(8,128)(2,1)}, u32[]{:S(2)}) copy-start(bf16[16,1024]{1,0:T(8,128)(2,1)} %input_ref.1) | copy-start | bytes 98308
  31.1 58.3 %copy-start.3 = (bf16[16,1024]{1,0:T(8,128)(2,1)S(1)}, bf16[16,1024]{1,0:T(8,128)(2,1)}, u32[]{:S(2)}) copy-start(bf16[16,1024]{1,0:T(8,128)(2,1)} %get-tuple-element.18.u_ref) | copy-start | bytes 98308
  31.1 58.3 %copy-start.4 = (f32[1024]{0:T(1024)S(1)}, f32[1024]{0:T(1024)}, u32[]{:S(2)}) copy-start(f32[1024]{0:T(1024)} %param.16) | copy-start | bytes 12292
  31.1 33.6 %all-to-all-start.2 = ((bf16[64,2,32,128]{3,2,1,0:T(8,128)(2,1)}), bf16[64,2,32,128]{3,2,1,0:T(8,128)(2,1)S(1)}, u32[]{:S(2)}, u32[]{:S(2)}) async-start(bf16[64,2,32,128]{3,2,1,0:T(8,128)(2,1)} %bitcast.22), calls=%async_computation.2 | async-start | bytes 2097152 | tf_op jit(solution)/shard_map/all_to_all | solution.py:30
  36.1 7.1 %collective-permute-start.1 = (bf16[128,128]{1,0:T(8,128)(2,1)S(1)}, bf16[128,128]{1,0:T(8,128)(2,1)S(1)}, u32[]{:S(2)}, u32[]{:S(2)}) collective-permute-start(bf16[128,128]{1,0:T(8,128)(2,1)S(1)} %bitcast.16), channel_id=1, source_target_pairs={{0,56},{8,0},{16,8},{24,16},{32,24},{40,32},{48,40},{56,48},{1,57}... | collective-permute-start | bytes 98312 | tf_op jit(solution)/shard_map/ppermute | solution.py:35
  41.3 6.7 %collective-permute-start = (bf16[128,128]{1,0:T(8,128)(2,1)S(1)}, bf16[128,128]{1,0:T(8,128)(2,1)S(1)}, u32[]{:S(2)}, u32[]{:S(2)}) collective-permute-start(bf16[128,128]{1,0:T(8,128)(2,1)S(1)} %bitcast.17), channel_id=1, source_target_pairs={{0,8},{8,16},{16,24},{24,32},{32,40},{40,48},{48,56},{56,0},{1,9},... | collective-permute-start | bytes 98312 | tf_op jit(solution)/shard_map/ppermute | solution.py:35
  43.2 8.3 %collective-permute-start.2 = (bf16[256,128]{1,0:T(8,128)(2,1)S(1)}, bf16[256,128]{1,0:T(8,128)(2,1)S(1)}, u32[]{:S(2)}, u32[]{:S(2)}) collective-permute-start(bf16[256,128]{1,0:T(8,128)(2,1)S(1)} %pad_maximum_fusion.1), channel_id=1, source_target_pairs={{0,24},{8,32},{16,40},{24,48},{32,56},{40,0},{48,8},{56,16},{1,25}... | collective-permute-start | bytes 196616 | tf_op jit(solution)/shard_map/ppermute | solution.py:35
  48.0 8.4 %collective-permute-start.3 = (bf16[384,128]{1,0:T(8,128)(2,1)S(1)}, bf16[384,128]{1,0:T(8,128)(2,1)S(1)}, u32[]{:S(2)}, u32[]{:S(2)}) collective-permute-start(bf16[384,128]{1,0:T(8,128)(2,1)S(1)} %pad_maximum_fusion), channel_id=1, source_target_pairs={{0,40},{8,48},{16,56},{24,0},{32,8},{40,16},{48,24},{56,32},{1,41}... | collective-permute-start | bytes 294920 | tf_op jit(solution)/shard_map/ppermute | solution.py:35

commit v7 on v6

--- a/solution.py
+++ b/solution.py
@@ -19,7 +19,7 @@
 CORES = 2
 
 FIELDS = 16
-LIVE, SLOT = 8, 9
+LIVE = 8
 
 VMEM = pl.BlockSpec(memory_space=pltpu.VMEM)
 SMEM = pl.BlockSpec(memory_space=pltpu.SMEM)
@@ -40,10 +40,10 @@
     return half + half * jnp.tanh(half)
 
 
-def announce_kernel(owner_ref, slot_ref, length_ref, seen_ref, out_ref):
-    rows, hd = out_ref.shape[1:]
+def ask_kernel(scale, owner_ref, length_ref, seen_ref, proj_ref, out_ref, own_ref, u_ref):
     pages = owner_ref.shape[0]
     blocks, tiles = seen_ref.shape
+    rows, hd = out_ref.shape[1] // 2, out_ref.shape[2]
     place = lax.axis_index(PLANE)
     lane = lax.broadcasted_iota(jnp.int32, (rows, hd), 1)
     owner, field = lane // FIELDS, lane % FIELDS
@@ -57,25 +57,8 @@
     for j in range(pages):
         live = jnp.clip(length_ref[0] - (place * pages + j) * PAGE, 0, PAGE)
         row = jnp.where(field == LIVE, live, seen[j * blocks // pages])
-        row = jnp.where(field == SLOT, slot_ref[j], row)
         info = jnp.where(owner == owner_ref[j], row, info)
     info = info.astype(jnp.float32).astype(jnp.bfloat16)
-    for i in range(out_ref.shape[0]):
-        out_ref[i] = info
-
-
-def announce(owners, slots, lengths, seen, users, rows, hd):
-    return pl.pallas_call(
-        announce_kernel,
-        in_specs=[SMEM] * 3 + [VMEM],
-        out_specs=VMEM,
-        out_shape=jax.ShapeDtypeStruct((users, rows, hd), jnp.bfloat16),
-        name="announce",
-    )(owners, slots, lengths, seen)
-
-
-def ask_kernel(scale, proj_ref, info_ref, out_ref, own_ref, u_ref):
-    rows, hd = info_ref.shape[1:]
 
     def act(block, h):
         start = (block * HEADS + h) * hd
@@ -85,19 +68,19 @@
         part = slice(h * hd, (h + 1) * hd)
         query = act(2, h)
         out_ref[h, :rows] = query
-        out_ref[h, rows:] = info_ref[0]
+        out_ref[h, rows:] = info
         score = query.astype(jnp.float32) * act(3, h).astype(jnp.float32)
         own = silu(jnp.sum(score, axis=1, keepdims=True) * scale).astype(jnp.bfloat16)
         own_ref[:, part] = own.astype(jnp.float32) * act(1, h).astype(jnp.float32)
         u_ref[:, part] = act(0, h)
 
 
-def ask(cand_proj, info, scale):
-    rows, hd = info.shape[1:]
-    width = cand_proj.shape[1] // 4
+def ask(owners, lengths, seen, cand_proj, scale):
+    rows, width = cand_proj.shape[0], cand_proj.shape[1] // 4
+    hd = width // HEADS
     return pl.pallas_call(
         functools.partial(ask_kernel, scale),
-        in_specs=[VMEM] * 2,
+        in_specs=[SMEM] * 2 + [VMEM] * 2,
         out_specs=[VMEM] * 3,
         out_shape=[
             jax.ShapeDtypeStruct((HEADS, 2 * rows, hd), jnp.bfloat16),
@@ -105,19 +88,21 @@
             jax.ShapeDtypeStruct((rows, width), jnp.bfloat16),
         ],
         name="ask",
-    )(cand_proj, info)
+    )(owners, lengths, seen, cand_proj)
 
 
 def split_pages_kernel(told_ref, pool_ref, out_ref, split_ref, sems):
     n_x, users = out_ref.shape[:2]
-    rows, hd = told_ref.shape[1:]
-    lane = lax.broadcasted_iota(jnp.int32, (rows, hd), 1)
-    row = lax.broadcasted_iota(jnp.int32, (rows, hd), 0)
-    here = (row == 0) & (lane == lax.axis_index("z") * FIELDS + SLOT)
+    hd = out_ref.shape[5]
+    count = pool_ref.shape[0]
+    first = lax.axis_index("z") * count
     slots = []
     for u in range(users):
-        slot = jnp.sum(jnp.where(here, told_ref[u].astype(jnp.float32), 0.0)).astype(jnp.int32)
-        slots.append(jnp.clip(slot, 0, pool_ref.shape[0] - 1))
+        slot = jnp.int32(0)
+        for j in range(told_ref.shape[1]):
+            at = told_ref[u, j] - first
+            slot = jnp.where((at >= 0) & (at < count), at, slot)
+        slots.append(slot)
     copies = []
     for u in range(users):
         for k in range(HEADS):
@@ -133,7 +118,7 @@
     shape = (HEADS // CORES, told.shape[0], CORES, 2, page, width // HEADS)
     return pl.pallas_call(
         split_pages_kernel,
-        in_specs=[VMEM, VMEM],
+        in_specs=[SMEM, VMEM],
         out_specs=HBM,
         out_shape=jax.ShapeDtypeStruct(shape, kv_pool.dtype),
         scratch_shapes=[pltpu.VMEM(shape, kv_pool.dtype), pltpu.SemaphoreType.DMA((told.shape[0],))],
@@ -241,14 +226,14 @@
     hd = width // HEADS
     scale = hd ** (-0.5)
     n_z = lax.axis_size("z")
-    owners, own_slots = page_owner.reshape(-1), page_slot.reshape(-1)
-
-    sent = announce(owners, own_slots, lengths, block_mask[0].T, n_z, rows, hd)
-    told = exchange(sent, ("z",))
-    asked, own, u_act = ask(cand_proj, sent, scale)
+    owners = page_owner.reshape(-1)
+
+    places = page_owner * kv_pool.shape[0] + page_slot
+    told = exchange(jnp.broadcast_to(places, (n_z,) + places.shape[1:]), ("z",))
+    asked, own, u_act = ask(owners, lengths, block_mask[0].T, cand_proj, scale)
     told, asked = lax.optimization_barrier((told, asked))
     asked = exchange(asked, ("x", "c"))
-    pages = split_pages(told, kv_pool)
+    pages = split_pages(told.reshape(n_z, -1), kv_pool)
     pages, asked = lax.optimization_barrier((pages, asked))
     got = exchange(pages.reshape((-1,) + pages.shape[3:]), PAGES).reshape(pages.shape)
     row, info = asked[:, :rows].reshape(-1, hd), asked[:, rows]

time: 91.2 us -> 90 us (0.987)
  Pallas kernels: 9.23 us -> 7.7 us
    pallas_call x3 -> x2, Pallas kernels: 5.56 us -> 4.04 us  [the longest x1 2.32 us: split_pages(): pl.pallas_call(split_pages_kernel, in_specs=[SMEM, VMEM], out_specs=HBM,...]
    all_to_all x3, waiting for transfers between devices: 15.9 us -> 15 us  [exchange(): return lax.all_to_all(array, axes, split_axis=0, concat_axis=0, tiled=True)]
where the time goes in v7:
time: 90 us; the launch traced here: 89.5 us
  starting transfers between devices  37.6 us (42%)
  blocking collectives  22.2 us (25%)
  waiting for transfers between devices  19.8 us (22%)
  Pallas kernels  7.7 us (9%)
    all_to_all x3, starting transfers between devices, exchange(): return lax.all_to_all(array, axes, split_axis=0, concat_axis=0, tiled=True)  22.3 us
    all_to_all x1, blocking collectives, exchange(): return lax.all_to_all(array, axes, split_axis=0, concat_axis=0, tiled=True)  22.2 us
    ppermute x4, starting transfers between devices, shift(): return lax.ppermute(array, axis, [(i, (i + step) % n) for i in range(n)])  15.3 us
    all_to_all x3, waiting for transfers between devices, exchange(): return lax.all_to_all(array, axes, split_axis=0, concat_axis=0, tiled=True)  15 us
    ppermute x4, waiting for transfers between devices, shift(): return lax.ppermute(array, axis, [(i, (i + step) % n) for i in range(n)])  4.83 us
    pallas_call x1, Pallas kernels, attend(): pl.pallas_call(functools.partial(attend_kernel, scale), in_specs=[VMEM] *...  2.48 us
    pallas_call x1, Pallas kernels, split_pages(): pl.pallas_call(split_pages_kernel, in_specs=[SMEM, VMEM], out_specs=HBM,...  2.32 us
  transfers between devices with their start and end apart: 7, of which 4 were waited for; matrix products, arithmetic and copies ran while one was open for 0% of the time, Pallas kernels for 5%

profile of v7, /device:TPU:1, one launch (start us, length us, event | category | flops | bytes accessed | tf_op | source)
XLA Modules:
  0.0 89.5 jit_solution(8403054784947500793)
XLA Ops:
  0.0 0.7 add_bitcast_fusion
  0.7 0.6 broadcast_in_dim.8
  1.3 10.9 %all-to-all-start = ((s32[8,1,8]{2,1,0:T(1,128)}), s32[8,1,8]{2,1,0:T(1,128)S(1)}, u32[]{:S(2)}, u32[]{:S(2)}) async-start(s32[8,1,8]{2,1,0:T(1,128)} %broadcast_in_dim.8), calls=%async_computation | async-start | bytes 8192 | tf_op jit(solution)/shard_map/all_to_all | solution.py:30
  12.8 1.7 %ask.1 = (bf16[8,32,128]{2,1,0:T(8,128)(2,1)}, f32[16,1024]{1,0:T(8,128)}, bf16[16,1024]{1,0:T(8,128)(2,1)}) custom-call(s32[8]{0:T(128)} %bitcast.27, s32[1]{0:T(128)S(6)} %copy.13.length_ref, s32[2,8]{1,0:T(2,128)} %bitcast.26, bf16[16,4096]{1,0:T(8,128)(2,1)} %proj_ref.1), custom_call_target="tpu_custom_call" | custom-call | tf_op jit(solution)/shard_map/ask/pallas_call | solution.py:81
  14.5 4.2 %all-to-all-done = s32[8,1,8]{2,1,0:T(1,128)S(1)} async-done(((s32[8,1,8]{2,1,0:T(1,128)}), s32[8,1,8]{2,1,0:T(1,128)S(1)}, u32[]{:S(2)}, u32[]{:S(2)}) %all-to-all-start) | async-done | bytes 288 | tf_op jit(solution)/shard_map/all_to_all | solution.py:30
  18.7 0.0 copy-start.5
  18.7 6.4 %all-to-all-start.1 = ((bf16[8,32,128]{2,1,0:T(8,128)(2,1)}), bf16[8,32,128]{2,1,0:T(8,128)(2,1)S(1)}, u32[]{:S(2)}, u32[]{:S(2)}) async-start(bf16[8,32,128]{2,1,0:T(8,128)(2,1)} %get-tuple-element.14), calls=%async_computation.1 | async-start | bytes 131072 | tf_op jit(solution)/shard_map/all_to_all | solution.py:30
  25.1 0.0 copy-done.5
  25.1 2.3 %split_pages.1 = bf16[4,8,2,2,32,128]{5,4,3,2,1,0:T(8,128)(2,1)} custom-call(s32[8,8]{1,0:T(8,128)} %bitcast.25, bf16[8,2,32,1024]{3,2,1,0:T(8,128)(2,1)} %pool_ref.1), custom_call_target="tpu_custom_call" | custom-call | tf_op jit(solution)/shard_map/split_pages/pallas_call | solution.py:119
  27.4 2.5 %all-to-all-done.1 = bf16[8,32,128]{2,1,0:T(8,128)(2,1)S(1)} async-done(((bf16[8,32,128]{2,1,0:T(8,128)(2,1)}), bf16[8,32,128]{2,1,0:T(8,128)(2,1)S(1)}, u32[]{:S(2)}, u32[]{:S(2)}) %all-to-all-start.1) | async-done | bytes 65568 | tf_op jit(solution)/shard_map/all_to_all | solution.py:30
  29.9 0.0 copy-start.1
  29.9 0.0 copy-start.2
  29.9 0.0 copy-start.3
  29.9 0.0 copy-start.4
  30.0 5.0 %all-to-all-start.2 = ((bf16[64,2,32,128]{3,2,1,0:T(8,128)(2,1)}), bf16[64,2,32,128]{3,2,1,0:T(8,128)(2,1)S(1)}, u32[]{:S(2)}, u32[]{:S(2)}) async-start(bf16[64,2,32,128]{3,2,1,0:T(8,128)(2,1)} %bitcast.24), calls=%async_computation.2 | async-start | bytes 2097152 | tf_op jit(solution)/shard_map/all_to_all | solution.py:30
  35.0 5.1 %collective-permute-start.1 = (bf16[128,128]{1,0:T(8,128)(2,1)S(1)}, bf16[128,128]{1,0:T(8,128)(2,1)S(1)}, u32[]{:S(2)}, u32[]{:S(2)}) collective-permute-start(bf16[128,128]{1,0:T(8,128)(2,1)S(1)} %bitcast.18), channel_id=1, source_target_pairs={{0,56},{8,0},{16,8},{24,16},{32,24},{40,32},{48,40},{56,48},{1,57}... | collective-permute-start | bytes 98312 | tf_op jit(solution)/shard_map/ppermute | solution.py:35
  40.1 1.9 %collective-permute-start = (bf16[128,128]{1,0:T(8,128)(2,1)S(1)}, bf16[128,128]{1,0:T(8,128)(2,1)S(1)}, u32[]{:S(2)}, u32[]{:S(2)}) collective-permute-start(bf16[128,128]{1,0:T(8,128)(2,1)S(1)} %bitcast.19), channel_id=1, source_target_pairs={{0,8},{8,16},{16,24},{24,32},{32,40},{40,48},{48,56},{56,0},{1,9},... | collective-permute-start | bytes 98312 | tf_op jit(solution)/shard_map/ppermute | solution.py:35
  42.0 0.0 collective-permute-done.1.rest_1_
  42.1 4.7 %collective-permute-start.2 = (bf16[256,128]{1,0:T(8,128)(2,1)S(1)}, bf16[256,128]{1,0:T(8,128)(2,1)S(1)}, u32[]{:S(2)}, u32[]{:S(2)}) collective-permute-start(bf16[256,128]{1,0:T(8,128)(2,1)S(1)} %pad_maximum_fusion.1), channel_id=1, source_target_pairs={{0,24},{8,32},{16,40},{24,48},{32,56},{40,0},{48,8},{56,16},{1,25}... | collective-permute-start | bytes 196616 | tf_op jit(solution)/shard_map/ppermute | solution.py:35
  46.8 0.0 collective-permute-done.rest_0_
  46.8 3.6 %collective-permute-start.3 = (bf16[384,128]{1,0:T(8,128)(2,1)S(1)}, bf16[384,128]{1,0:T(8,128)(2,1)S(1)}, u32[]{:S(2)}, u32[]{:S(2)}) collective-permute-start(bf16[384,128]{1,0:T(8,128)(2,1)S(1)} %pad_maximum_fusion), channel_id=1, source_target_pairs={{0,40},{8,48},{16,56},{24,0},{32,8},{40,16},{48,24},{56,32},{1,41}... | collective-permute-start | bytes 294920 | tf_op jit(solution)/shard_map/ppermute | solution.py:35
  50.4 0.0 collective-permute-done.2.rest_2_
  50.4 4.8 %collective-permute-done.3.rest_3_ = bf16[384,128]{1,0:T(8,128)(2,1)S(1)} collective-permute-done((bf16[384,128]{1,0:T(8,128)(2,1)S(1)}, bf16[384,128]{1,0:T(8,128)(2,1)S(1)}, u32[]{:S(2)}, u32[]{:S(2)}) %collective-permute-start.3) | collective-permute-done | bytes 98336 | tf_op jit(solution)/shard_map/ppermute | solution.py:35
  55.3 8.3 %all-to-all-done.2 = bf16[64,2,32,128]{3,2,1,0:T(8,128)(2,1)S(1)} async-done(((bf16[64,2,32,128]{3,2,1,0:T(8,128)(2,1)}), bf16[64,2,32,128]{3,2,1,0:T(8,128)(2,1)S(1)}, u32[]{:S(2)}, u32[]{:S(2)}) %all-to-all-start.2) | async-done | bytes 1048608 | tf_op jit(solution)/shard_map/all_to_all | solution.py:30
  63.5 2.5 %attend.1 = bf16[4,8,2,16,128]{4,3,2,1,0:T(8,128)(2,1)S(1)} custom-call(bf16[8,128]{1,0:T(8,128)(2,1)S(1)} %slice_bitcast_fusion.info_ref, bf16[128,128]{1,0:T(8,128)(2,1)S(1)} %bitcast.22, bf16[4,8,2,2,32,128]{5,4,3,2,1,0:T(8,128)(2,1)S(1)} %bitcast.15, bf16[128,128]{1,0:T(8,128)(2,1)S(1)} %collective-permute-done.rest_0_, ...), custom_call_target="tpu_custom_call" | custom-call | tf_op jit(solution)/shard_map/attend/pallas_call | solution.py:183
  66.0 22.2 %all_to_all.20 = bf16[64,16,128]{2,1,0:T(8,128)(2,1)S(1)} all-to-all(bf16[64,16,128]{2,1,0:T(8,128)(2,1)S(1)} %bitcast.17), channel_id=1, replica_groups=mesh['z'=8,'y'=8,'x'=4,'c'=2] {'x','y','c'}, dimensions={0} | all-to-all | bytes 524288 | tf_op jit(solution)/shard_map/all_to_all | solution.py:30
  88.3 0.0 copy-done
  88.3 0.0 copy-done.1
  88.3 0.0 copy-done.2
  88.3 0.0 copy-done.3
  88.3 0.0 copy-done.4
  88.3 1.2 %finish.1 = bf16[16,1024]{1,0:T(8,128)(2,1)} custom-call(bf16[4,8,2,16,128]{4,3,2,1,0:T(8,128)(2,1)S(1)} %bitcast.16, f32[16,1024]{1,0:T(8,128)S(1)} %copy-done.1, bf16[16,1024]{1,0:T(8,128)(2,1)S(1)} %copy-done.3, f32[1,1024]{1,0:T(1,128)S(1)} %bitcast.23, bf16[16,1024]{1,0:T(8,128)(2,1)S(1)} %copy-done.2, bf16[1024,1024]{1,0:T(8,128)(2,1)S(1)} %copy-done), custom_call_target="tpu_custom_call" | custom-call | tf_op jit(solution)/shard_map/finish/pallas_call | solution.py:212
  (6 shorter events, 0.1 us)
Async XLA Ops:
  1.3 17.4 %all-to-all-start = ((s32[8,1,8]{2,1,0:T(1,128)}), s32[8,1,8]{2,1,0:T(1,128)S(1)}, u32[]{:S(2)}, u32[]{:S(2)}) async-start(s32[8,1,8]{2,1,0:T(1,128)} %broadcast_in_dim.8), calls=%async_computation | async-start | bytes 8192 | tf_op jit(solution)/shard_map/all_to_all | solution.py:30
  18.7 6.4 %copy-start.5 = (s32[8,1,8]{2,1,0:T(1,128)}, s32[8,1,8]{2,1,0:T(1,128)S(1)}, u32[]{:S(2)}) copy-start(s32[8,1,8]{2,1,0:T(1,128)S(1)} %all-to-all-done) | copy-start | bytes 772
  18.7 11.3 %all-to-all-start.1 = ((bf16[8,32,128]{2,1,0:T(8,128)(2,1)}), bf16[8,32,128]{2,1,0:T(8,128)(2,1)S(1)}, u32[]{:S(2)}, u32[]{:S(2)}) async-start(bf16[8,32,128]{2,1,0:T(8,128)(2,1)} %get-tuple-element.14), calls=%async_computation.1 | async-start | bytes 131072 | tf_op jit(solution)/shard_map/all_to_all | solution.py:30
  29.9 58.3 %copy-start = (bf16[1024,1024]{1,0:T(8,128)(2,1)S(1)}, bf16[1024,1024]{1,0:T(8,128)(2,1)}, u32[]{:S(2)}) copy-start(bf16[1024,1024]{1,0:T(8,128)(2,1)} %weight_ref.1) | copy-start | bytes 6291460
  29.9 58.3 %copy-start.1 = (f32[16,1024]{1,0:T(8,128)S(1)}, f32[16,1024]{1,0:T(8,128)}, u32[]{:S(2)}) copy-start(f32[16,1024]{1,0:T(8,128)} %get-tuple-element.17.own_ref) | copy-start | bytes 196612
  29.9 58.3 %copy-start.2 = (bf16[16,1024]{1,0:T(8,128)(2,1)S(1)}, bf16[16,1024]{1,0:T(8,128)(2,1)}, u32[]{:S(2)}) copy-start(bf16[16,1024]{1,0:T(8,128)(2,1)} %input_ref.1) | copy-start | bytes 98308
  29.9 58.3 %copy-start.3 = (bf16[16,1024]{1,0:T(8,128)(2,1)S(1)}, bf16[16,1024]{1,0:T(8,128)(2,1)}, u32[]{:S(2)}) copy-start(bf16[16,1024]{1,0:T(8,128)(2,1)} %get-tuple-element.18.u_ref) | copy-start | bytes 98308
  29.9 58.3 %copy-start.4 = (f32[1024]{0:T(1024)S(1)}, f32[1024]{0:T(1024)}, u32[]{:S(2)}) copy-start(f32[1024]{0:T(1024)} %param.16) | copy-start | bytes 12292
  30.0 33.6 %all-to-all-start.2 = ((bf16[64,2,32,128]{3,2,1,0:T(8,128)(2,1)}), bf16[64,2,32,128]{3,2,1,0:T(8,128)(2,1)S(1)}, u32[]{:S(2)}, u32[]{:S(2)}) async-start(bf16[64,2,32,128]{3,2,1,0:T(8,128)(2,1)} %bitcast.24), calls=%async_computation.2 | async-start | bytes 2097152 | tf_op jit(solution)/shard_map/all_to_all | solution.py:30
  35.0 7.1 %collective-permute-start.1 = (bf16[128,128]{1,0:T(8,128)(2,1)S(1)}, bf16[128,128]{1,0:T(8,128)(2,1)S(1)}, u32[]{:S(2)}, u32[]{:S(2)}) collective-permute-start(bf16[128,128]{1,0:T(8,128)(2,1)S(1)} %bitcast.18), channel_id=1, source_target_pairs={{0,56},{8,0},{16,8},{24,16},{32,24},{40,32},{48,40},{56,48},{1,57}... | collective-permute-start | bytes 98312 | tf_op jit(solution)/shard_map/ppermute | solution.py:35
  40.1 6.7 %collective-permute-start = (bf16[128,128]{1,0:T(8,128)(2,1)S(1)}, bf16[128,128]{1,0:T(8,128)(2,1)S(1)}, u32[]{:S(2)}, u32[]{:S(2)}) collective-permute-start(bf16[128,128]{1,0:T(8,128)(2,1)S(1)} %bitcast.19), channel_id=1, source_target_pairs={{0,8},{8,16},{16,24},{24,32},{32,40},{40,48},{48,56},{56,0},{1,9},... | collective-permute-start | bytes 98312 | tf_op jit(solution)/shard_map/ppermute | solution.py:35
  42.1 8.3 %collective-permute-start.2 = (bf16[256,128]{1,0:T(8,128)(2,1)S(1)}, bf16[256,128]{1,0:T(8,128)(2,1)S(1)}, u32[]{:S(2)}, u32[]{:S(2)}) collective-permute-start(bf16[256,128]{1,0:T(8,128)(2,1)S(1)} %pad_maximum_fusion.1), channel_id=1, source_target_pairs={{0,24},{8,32},{16,40},{24,48},{32,56},{40,0},{48,8},{56,16},{1,25}... | collective-permute-start | bytes 196616 | tf_op jit(solution)/shard_map/ppermute | solution.py:35
  46.8 8.4 %collective-permute-start.3 = (bf16[384,128]{1,0:T(8,128)(2,1)S(1)}, bf16[384,128]{1,0:T(8,128)(2,1)S(1)}, u32[]{:S(2)}, u32[]{:S(2)}) collective-permute-start(bf16[384,128]{1,0:T(8,128)(2,1)S(1)} %pad_maximum_fusion), channel_id=1, source_target_pairs={{0,40},{8,48},{16,56},{24,0},{32,8},{40,16},{48,24},{56,32},{1,41}... | collective-permute-start | bytes 294920 | tf_op jit(solution)/shard_map/ppermute | solution.py:35

commit v8 on v7

--- a/solution.py
+++ b/solution.py
@@ -147,12 +147,13 @@
     for piece in pieces:
         blocks += [piece[b * height : (b + 1) * height, :] for b in range(piece.shape[0] // height)]
     for step, block in zip(STEPS, blocks):
-        q_ref[pl.ds(lax.rem(y + (step + tiles), tiles) * height, height), :] = block
+        start = pl.multiple_of(lax.rem(y + (step + tiles), tiles) * height, height)
+        q_ref[pl.ds(start, height), :] = block
     place = lax.broadcasted_iota(jnp.int32, (sources, span), 1)
     which = lax.broadcasted_iota(jnp.int32, (sources, span), 0)
     spread = (place // PAGE == which).astype(jnp.bfloat16)
     fields = lax.dot_general(
-        info_ref[...], spread, (((0,), (0,)), ((), ())), preferred_element_type=jnp.float32
+        info_ref[...].astype(jnp.bfloat16), spread, (((0,), (0,)), ((), ())), preferred_element_type=jnp.float32
     )
     within = lax.rem(lax.broadcasted_iota(jnp.int32, (1, span), 1), PAGE).astype(jnp.float32)
     q = q_ref[...]
@@ -236,7 +237,7 @@
     pages = split_pages(told.reshape(n_z, -1), kv_pool)
     pages, asked = lax.optimization_barrier((pages, asked))
     got = exchange(pages.reshape((-1,) + pages.shape[3:]), PAGES).reshape(pages.shape)
-    row, info = asked[:, :rows].reshape(-1, hd), asked[:, rows]
+    row, info = asked[:, :rows].reshape(-1, hd), asked[:, rows].astype(jnp.float32)
     part = attend(info, row, got, gather_queries(row), scale)
     back = exchange(part.reshape(-1, rows, hd), SUMS).reshape(part.shape)
     return finish(back, own, u_act, out_gain, cand_input, out_weight)

time: 90 us -> 90 us (level)
  no operation moved by 1% of the time
where the time goes in v8:
time: 90 us; the launch traced here: 89.5 us
  starting transfers between devices  37.6 us (42%)
  blocking collectives  22.2 us (25%)
  waiting for transfers between devices  19.8 us (22%)
  Pallas kernels  7.71 us (9%)
    all_to_all x3, starting transfers between devices, exchange(): return lax.all_to_all(array, axes, split_axis=0, concat_axis=0, tiled=True)  22.3 us
    all_to_all x1, blocking collectives, exchange(): return lax.all_to_all(array, axes, split_axis=0, concat_axis=0, tiled=True)  22.2 us
    ppermute x4, starting transfers between devices, shift(): return lax.ppermute(array, axis, [(i, (i + step) % n) for i in range(n)])  15.3 us
    all_to_all x3, waiting for transfers between devices, exchange(): return lax.all_to_all(array, axes, split_axis=0, concat_axis=0, tiled=True)  15 us
    ppermute x4, waiting for transfers between devices, shift(): return lax.ppermute(array, axis, [(i, (i + step) % n) for i in range(n)])  4.83 us
    pallas_call x1, Pallas kernels, attend(): pl.pallas_call(functools.partial(attend_kernel, scale), in_specs=[VMEM] *...  2.49 us
    pallas_call x1, Pallas kernels, split_pages(): pl.pallas_call(split_pages_kernel, in_specs=[SMEM, VMEM], out_specs=HBM,...  2.32 us
  transfers between devices with their start and end apart: 7, of which 4 were waited for; matrix products, arithmetic and copies ran while one was open for 0% of the time, Pallas kernels for 5%

profile of v8, /device:TPU:1, one launch (start us, length us, event | category | flops | bytes accessed | tf_op | source)
XLA Modules:
  0.0 89.5 jit_solution(12367292368543716500)
XLA Ops:
  0.0 0.7 add_bitcast_fusion
  0.7 0.6 broadcast_in_dim.8
  1.3 10.9 %all-to-all-start = ((s32[8,1,8]{2,1,0:T(1,128)}), s32[8,1,8]{2,1,0:T(1,128)S(1)}, u32[]{:S(2)}, u32[]{:S(2)}) async-start(s32[8,1,8]{2,1,0:T(1,128)} %broadcast_in_dim.8), calls=%async_computation | async-start | bytes 8192 | tf_op jit(solution)/shard_map/all_to_all | solution.py:30
  12.8 1.7 %ask.1 = (bf16[8,32,128]{2,1,0:T(8,128)(2,1)}, f32[16,1024]{1,0:T(8,128)}, bf16[16,1024]{1,0:T(8,128)(2,1)}) custom-call(s32[8]{0:T(128)} %bitcast.30, s32[1]{0:T(128)S(6)} %copy.13.length_ref, s32[2,8]{1,0:T(2,128)} %bitcast.29, bf16[16,4096]{1,0:T(8,128)(2,1)} %proj_ref.1), custom_call_target="tpu_custom_call" | custom-call | tf_op jit(solution)/shard_map/ask/pallas_call | solution.py:81
  14.5 4.2 %all-to-all-done = s32[8,1,8]{2,1,0:T(1,128)S(1)} async-done(((s32[8,1,8]{2,1,0:T(1,128)}), s32[8,1,8]{2,1,0:T(1,128)S(1)}, u32[]{:S(2)}, u32[]{:S(2)}) %all-to-all-start) | async-done | bytes 288 | tf_op jit(solution)/shard_map/all_to_all | solution.py:30
  18.7 0.0 copy-start.5
  18.7 6.4 %all-to-all-start.1 = ((bf16[8,32,128]{2,1,0:T(8,128)(2,1)}), bf16[8,32,128]{2,1,0:T(8,128)(2,1)S(1)}, u32[]{:S(2)}, u32[]{:S(2)}) async-start(bf16[8,32,128]{2,1,0:T(8,128)(2,1)} %get-tuple-element.14), calls=%async_computation.1 | async-start | bytes 131072 | tf_op jit(solution)/shard_map/all_to_all | solution.py:30
  25.1 0.0 copy-done.5
  25.1 2.3 %split_pages.1 = bf16[4,8,2,2,32,128]{5,4,3,2,1,0:T(8,128)(2,1)} custom-call(s32[8,8]{1,0:T(8,128)} %bitcast.28, bf16[8,2,32,1024]{3,2,1,0:T(8,128)(2,1)} %pool_ref.1), custom_call_target="tpu_custom_call" | custom-call | tf_op jit(solution)/shard_map/split_pages/pallas_call | solution.py:119
  27.4 2.5 %all-to-all-done.1 = bf16[8,32,128]{2,1,0:T(8,128)(2,1)S(1)} async-done(((bf16[8,32,128]{2,1,0:T(8,128)(2,1)}), bf16[8,32,128]{2,1,0:T(8,128)(2,1)S(1)}, u32[]{:S(2)}, u32[]{:S(2)}) %all-to-all-start.1) | async-done | bytes 65568 | tf_op jit(solution)/shard_map/all_to_all | solution.py:30
  29.9 0.0 copy-start
  29.9 0.0 copy-start.1
  29.9 0.0 copy-start.2
  29.9 0.0 copy-start.4
  30.0 5.0 %all-to-all-start.2 = ((bf16[64,2,32,128]{3,2,1,0:T(8,128)(2,1)}), bf16[64,2,32,128]{3,2,1,0:T(8,128)(2,1)S(1)}, u32[]{:S(2)}, u32[]{:S(2)}) async-start(bf16[64,2,32,128]{3,2,1,0:T(8,128)(2,1)} %bitcast.27), calls=%async_computation.2 | async-start | bytes 2097152 | tf_op jit(solution)/shard_map/all_to_all | solution.py:30
  35.0 5.1 %collective-permute-start.1 = (bf16[128,128]{1,0:T(8,128)(2,1)S(1)}, bf16[128,128]{1,0:T(8,128)(2,1)S(1)}, u32[]{:S(2)}, u32[]{:S(2)}) collective-permute-start(bf16[128,128]{1,0:T(8,128)(2,1)S(1)} %bitcast.21), channel_id=1, source_target_pairs={{0,56},{8,0},{16,8},{24,16},{32,24},{40,32},{48,40},{56,48},{1,57}... | collective-permute-start | bytes 98312 | tf_op jit(solution)/shard_map/ppermute | solution.py:35
  40.1 1.9 %collective-permute-start = (bf16[128,128]{1,0:T(8,128)(2,1)S(1)}, bf16[128,128]{1,0:T(8,128)(2,1)S(1)}, u32[]{:S(2)}, u32[]{:S(2)}) collective-permute-start(bf16[128,128]{1,0:T(8,128)(2,1)S(1)} %bitcast.22), channel_id=1, source_target_pairs={{0,8},{8,16},{16,24},{24,32},{32,40},{40,48},{48,56},{56,0},{1,9},... | collective-permute-start | bytes 98312 | tf_op jit(solution)/shard_map/ppermute | solution.py:35
  42.0 0.0 collective-permute-done.1.rest_1_
  42.1 4.7 %collective-permute-start.2 = (bf16[256,128]{1,0:T(8,128)(2,1)S(1)}, bf16[256,128]{1,0:T(8,128)(2,1)S(1)}, u32[]{:S(2)}, u32[]{:S(2)}) collective-permute-start(bf16[256,128]{1,0:T(8,128)(2,1)S(1)} %pad_maximum_fusion.1), channel_id=1, source_target_pairs={{0,24},{8,32},{16,40},{24,48},{32,56},{40,0},{48,8},{56,16},{1,25}... | collective-permute-start | bytes 196616 | tf_op jit(solution)/shard_map/ppermute | solution.py:35
  46.8 0.0 collective-permute-done.rest_0_
  46.8 3.6 %collective-permute-start.3 = (bf16[384,128]{1,0:T(8,128)(2,1)S(1)}, bf16[384,128]{1,0:T(8,128)(2,1)S(1)}, u32[]{:S(2)}, u32[]{:S(2)}) collective-permute-start(bf16[384,128]{1,0:T(8,128)(2,1)S(1)} %pad_maximum_fusion), channel_id=1, source_target_pairs={{0,40},{8,48},{16,56},{24,0},{32,8},{40,16},{48,24},{56,32},{1,41}... | collective-permute-start | bytes 294920 | tf_op jit(solution)/shard_map/ppermute | solution.py:35
  50.4 0.0 collective-permute-done.2.rest_2_
  50.4 4.8 %collective-permute-done.3.rest_3_ = bf16[384,128]{1,0:T(8,128)(2,1)S(1)} collective-permute-done((bf16[384,128]{1,0:T(8,128)(2,1)S(1)}, bf16[384,128]{1,0:T(8,128)(2,1)S(1)}, u32[]{:S(2)}, u32[]{:S(2)}) %collective-permute-start.3) | collective-permute-done | bytes 98336 | tf_op jit(solution)/shard_map/ppermute | solution.py:35
  55.3 8.3 %all-to-all-done.2 = bf16[64,2,32,128]{3,2,1,0:T(8,128)(2,1)S(1)} async-done(((bf16[64,2,32,128]{3,2,1,0:T(8,128)(2,1)}), bf16[64,2,32,128]{3,2,1,0:T(8,128)(2,1)S(1)}, u32[]{:S(2)}, u32[]{:S(2)}) %all-to-all-start.2) | async-done | bytes 1048608 | tf_op jit(solution)/shard_map/all_to_all | solution.py:30
  63.5 2.5 %attend.1 = bf16[4,8,2,16,128]{4,3,2,1,0:T(8,128)(2,1)S(1)} custom-call(f32[8,128]{1,0:T(8,128)S(1)} %fusion.info_ref, bf16[128,128]{1,0:T(8,128)(2,1)S(1)} %bitcast.25, bf16[4,8,2,2,32,128]{5,4,3,2,1,0:T(8,128)(2,1)S(1)} %bitcast.18, bf16[128,128]{1,0:T(8,128)(2,1)S(1)} %collective-permute-done.rest_0_, ...), custom_call_target="tpu_custom_call" | custom-call | tf_op jit(solution)/shard_map/attend/pallas_call | solution.py:184
  66.0 22.2 %all_to_all.20 = bf16[64,16,128]{2,1,0:T(8,128)(2,1)S(1)} all-to-all(bf16[64,16,128]{2,1,0:T(8,128)(2,1)S(1)} %bitcast.20), channel_id=1, replica_groups=mesh['z'=8,'y'=8,'x'=4,'c'=2] {'x','y','c'}, dimensions={0} | all-to-all | bytes 524288 | tf_op jit(solution)/shard_map/all_to_all | solution.py:30
  88.3 0.0 copy-done
  88.3 0.0 copy-done.1
  88.3 0.0 copy-done.2
  88.3 0.0 copy-done.3
  88.3 0.0 copy-done.4
  88.3 1.2 %finish.1 = bf16[16,1024]{1,0:T(8,128)(2,1)} custom-call(bf16[4,8,2,16,128]{4,3,2,1,0:T(8,128)(2,1)S(1)} %bitcast.19, f32[16,1024]{1,0:T(8,128)S(1)} %copy-done.1, bf16[16,1024]{1,0:T(8,128)(2,1)S(1)} %copy-done.3, f32[1,1024]{1,0:T(1,128)S(1)} %bitcast.26, bf16[16,1024]{1,0:T(8,128)(2,1)S(1)} %copy-done.2, bf16[1024,1024]{1,0:T(8,128)(2,1)S(1)} %copy-done), custom_call_target="tpu_custom_call" | custom-call | tf_op jit(solution)/shard_map/finish/pallas_call | solution.py:213
  (6 shorter events, 0.1 us)
Async XLA Ops:
  1.3 17.4 %all-to-all-start = ((s32[8,1,8]{2,1,0:T(1,128)}), s32[8,1,8]{2,1,0:T(1,128)S(1)}, u32[]{:S(2)}, u32[]{:S(2)}) async-start(s32[8,1,8]{2,1,0:T(1,128)} %broadcast_in_dim.8), calls=%async_computation | async-start | bytes 8192 | tf_op jit(solution)/shard_map/all_to_all | solution.py:30
  18.7 6.4 %copy-start.5 = (s32[8,1,8]{2,1,0:T(1,128)}, s32[8,1,8]{2,1,0:T(1,128)S(1)}, u32[]{:S(2)}) copy-start(s32[8,1,8]{2,1,0:T(1,128)S(1)} %all-to-all-done) | copy-start | bytes 772
  18.7 11.3 %all-to-all-start.1 = ((bf16[8,32,128]{2,1,0:T(8,128)(2,1)}), bf16[8,32,128]{2,1,0:T(8,128)(2,1)S(1)}, u32[]{:S(2)}, u32[]{:S(2)}) async-start(bf16[8,32,128]{2,1,0:T(8,128)(2,1)} %get-tuple-element.14), calls=%async_computation.1 | async-start | bytes 131072 | tf_op jit(solution)/shard_map/all_to_all | solution.py:30
  29.9 58.3 %copy-start = (bf16[1024,1024]{1,0:T(8,128)(2,1)S(1)}, bf16[1024,1024]{1,0:T(8,128)(2,1)}, u32[]{:S(2)}) copy-start(bf16[1024,1024]{1,0:T(8,128)(2,1)} %weight_ref.1) | copy-start | bytes 6291460
  29.9 58.3 %copy-start.1 = (f32[16,1024]{1,0:T(8,128)S(1)}, f32[16,1024]{1,0:T(8,128)}, u32[]{:S(2)}) copy-start(f32[16,1024]{1,0:T(8,128)} %get-tuple-element.17.own_ref) | copy-start | bytes 196612
  29.9 58.3 %copy-start.2 = (bf16[16,1024]{1,0:T(8,128)(2,1)S(1)}, bf16[16,1024]{1,0:T(8,128)(2,1)}, u32[]{:S(2)}) copy-start(bf16[16,1024]{1,0:T(8,128)(2,1)} %input_ref.1) | copy-start | bytes 98308
  29.9 58.3 %copy-start.3 = (bf16[16,1024]{1,0:T(8,128)(2,1)S(1)}, bf16[16,1024]{1,0:T(8,128)(2,1)}, u32[]{:S(2)}) copy-start(bf16[16,1024]{1,0:T(8,128)(2,1)} %get-tuple-element.18.u_ref) | copy-start | bytes 98308
  29.9 58.3 %copy-start.4 = (f32[1024]{0:T(1024)S(1)}, f32[1024]{0:T(1024)}, u32[]{:S(2)}) copy-start(f32[1024]{0:T(1024)} %param.16) | copy-start | bytes 12292
  30.0 33.6 %all-to-all-start.2 = ((bf16[64,2,32,128]{3,2,1,0:T(8,128)(2,1)}), bf16[64,2,32,128]{3,2,1,0:T(8,128)(2,1)S(1)}, u32[]{:S(2)}, u32[]{:S(2)}) async-start(bf16[64,2,32,128]{3,2,1,0:T(8,128)(2,1)} %bitcast.27), calls=%async_computation.2 | async-start | bytes 2097152 | tf_op jit(solution)/shard_map/all_to_all | solution.py:30
  35.0 7.1 %collective-permute-start.1 = (bf16[128,128]{1,0:T(8,128)(2,1)S(1)}, bf16[128,128]{1,0:T(8,128)(2,1)S(1)}, u32[]{:S(2)}, u32[]{:S(2)}) collective-permute-start(bf16[128,128]{1,0:T(8,128)(2,1)S(1)} %bitcast.21), channel_id=1, source_target_pairs={{0,56},{8,0},{16,8},{24,16},{32,24},{40,32},{48,40},{56,48},{1,57}... | collective-permute-start | bytes 98312 | tf_op jit(solution)/shard_map/ppermute | solution.py:35
  40.1 6.7 %collective-permute-start = (bf16[128,128]{1,0:T(8,128)(2,1)S(1)}, bf16[128,128]{1,0:T(8,128)(2,1)S(1)}, u32[]{:S(2)}, u32[]{:S(2)}) collective-permute-start(bf16[128,128]{1,0:T(8,128)(2,1)S(1)} %bitcast.22), channel_id=1, source_target_pairs={{0,8},{8,16},{16,24},{24,32},{32,40},{40,48},{48,56},{56,0},{1,9},... | collective-permute-start | bytes 98312 | tf_op jit(solution)/shard_map/ppermute | solution.py:35
  42.1 8.3 %collective-permute-start.2 = (bf16[256,128]{1,0:T(8,128)(2,1)S(1)}, bf16[256,128]{1,0:T(8,128)(2,1)S(1)}, u32[]{:S(2)}, u32[]{:S(2)}) collective-permute-start(bf16[256,128]{1,0:T(8,128)(2,1)S(1)} %pad_maximum_fusion.1), channel_id=1, source_target_pairs={{0,24},{8,32},{16,40},{24,48},{32,56},{40,0},{48,8},{56,16},{1,25}... | collective-permute-start | bytes 196616 | tf_op jit(solution)/shard_map/ppermute | solution.py:35
  46.8 8.4 %collective-permute-start.3 = (bf16[384,128]{1,0:T(8,128)(2,1)S(1)}, bf16[384,128]{1,0:T(8,128)(2,1)S(1)}, u32[]{:S(2)}, u32[]{:S(2)}) collective-permute-start(bf16[384,128]{1,0:T(8,128)(2,1)S(1)} %pad_maximum_fusion), channel_id=1, source_target_pairs={{0,40},{8,48},{16,56},{24,0},{32,8},{40,16},{48,24},{56,32},{1,41}... | collective-permute-start | bytes 294920 | tf_op jit(solution)/shard_map/ppermute | solution.py:35

commit v9 on v8

--- a/solution.py
+++ b/solution.py
@@ -15,7 +15,7 @@
 PLANE = ("y", "x", "c")
 SPREAD = ("z", "x", "c")
 PAGES = ("x", "z", "c")
-SUMS = ("x", "y", "c")
+SUMS = ("x", "c", "y")
 CORES = 2
 
 FIELDS = 16
@@ -138,7 +138,7 @@
 
 def attend_kernel(scale, info_ref, row_ref, kv_ref, *rest):
     pieces, (out_ref, q_ref, acc_ref) = rest[:-3], rest[-3:]
-    n_x, n_y, cores, rows, hd = out_ref.shape
+    n_x, cores, n_y, rows, hd = out_ref.shape
     sources, tiles = n_x * cores, len(STEPS)
     span = sources * PAGE
     height = n_x * cores * rows
@@ -173,13 +173,13 @@
             acc_ref[...] += part
     total = acc_ref[...].astype(out_ref.dtype).reshape(n_y, n_x, cores, rows, hd)
     for t in range(n_y):
-        out_ref[:, t] = total[t]
+        out_ref[:, :, t] = total[t]
 
 
 def attend(info, row, pages, pieces, scale):
     n_x, _, cores, _, _, hd = pages.shape
     rows = row.shape[0] // (n_x * cores)
-    out = jax.ShapeDtypeStruct((n_x, len(STEPS), cores, rows, hd), jnp.bfloat16)
+    out = jax.ShapeDtypeStruct((n_x, cores, len(STEPS), rows, hd), jnp.bfloat16)
     height = out.size // hd
     return pl.pallas_call(
         functools.partial(attend_kernel, scale),
@@ -195,9 +195,9 @@
 def finish_kernel(back_ref, own_ref, u_ref, gain_ref, input_ref, weight_ref, out_ref):
     attn = []
     for h in range(HEADS):
-        total = back_ref[h // CORES, 0, h % CORES].astype(jnp.float32)
-        for y in range(1, back_ref.shape[1]):
-            total += back_ref[h // CORES, y, h % CORES].astype(jnp.float32)
+        total = back_ref[h // CORES, h % CORES, 0].astype(jnp.float32)
+        for y in range(1, back_ref.shape[2]):
+            total += back_ref[h // CORES, h % CORES, y].astype(jnp.float32)
         attn.append(total)
     attn = jnp.concatenate(attn, axis=1) + own_ref[...]
     mean = jnp.mean(attn, axis=1, keepdims=True)
@@ -235,7 +235,7 @@
     told, asked = lax.optimization_barrier((told, asked))
     asked = exchange(asked, ("x", "c"))
     pages = split_pages(told.reshape(n_z, -1), kv_pool)
-    pages, asked = lax.optimization_barrier((pages, asked))
+    _, asked = lax.optimization_barrier((pages, asked))
     got = exchange(pages.reshape((-1,) + pages.shape[3:]), PAGES).reshape(pages.shape)
     row, info = asked[:, :rows].reshape(-1, hd), asked[:, rows].astype(jnp.float32)
     part = attend(info, row, got, gather_queries(row), scale)

time: 90 us -> 90.1 us (level)
  no operation moved by 1% of the time
where the time goes in v9:
time: 90.1 us; the launch traced here: 89.5 us
  starting transfers between devices  37.6 us (42%)
  blocking collectives  22.2 us (25%)
  waiting for transfers between devices  19.8 us (22%)
  Pallas kernels  7.71 us (9%)
    all_to_all x3, starting transfers between devices, exchange(): return lax.all_to_all(array, axes, split_axis=0, concat_axis=0, tiled=True)  22.3 us
    all_to_all x1, blocking collectives, exchange(): return lax.all_to_all(array, axes, split_axis=0, concat_axis=0, tiled=True)  22.2 us
    ppermute x4, starting transfers between devices, shift(): return lax.ppermute(array, axis, [(i, (i + step) % n) for i in range(n)])  15.3 us
    all_to_all x3, waiting for transfers between devices, exchange(): return lax.all_to_all(array, axes, split_axis=0, concat_axis=0, tiled=True)  15 us
    ppermute x4, waiting for transfers between devices, shift(): return lax.ppermute(array, axis, [(i, (i + step) % n) for i in range(n)])  4.83 us
    pallas_call x1, Pallas kernels, attend(): pl.pallas_call(functools.partial(attend_kernel, scale), in_specs=[VMEM] *...  2.49 us
    pallas_call x1, Pallas kernels, split_pages(): pl.pallas_call(split_pages_kernel, in_specs=[SMEM, VMEM], out_specs=HBM,...  2.32 us
  transfers between devices with their start and end apart: 7, of which 4 were waited for; matrix products, arithmetic and copies ran while one was open for 0% of the time, Pallas kernels for 5%

profile of v9, /device:TPU:1, one launch (start us, length us, event | category | flops | bytes accessed | tf_op | source)
XLA Modules:
  0.0 89.5 jit_solution(13173511000854573638)
XLA Ops:
  0.0 0.7 add_bitcast_fusion
  0.7 0.6 broadcast_in_dim.8
  1.3 10.9 %all-to-all-start = ((s32[8,1,8]{2,1,0:T(1,128)}), s32[8,1,8]{2,1,0:T(1,128)S(1)}, u32[]{:S(2)}, u32[]{:S(2)}) async-start(s32[8,1,8]{2,1,0:T(1,128)} %broadcast_in_dim.8), calls=%async_computation | async-start | bytes 8192 | tf_op jit(solution)/shard_map/all_to_all | solution.py:30
  12.8 1.7 %ask.1 = (bf16[8,32,128]{2,1,0:T(8,128)(2,1)}, f32[16,1024]{1,0:T(8,128)}, bf16[16,1024]{1,0:T(8,128)(2,1)}) custom-call(s32[8]{0:T(128)} %bitcast.30, s32[1]{0:T(128)S(6)} %copy.13.length_ref, s32[2,8]{1,0:T(2,128)} %bitcast.29, bf16[16,4096]{1,0:T(8,128)(2,1)} %proj_ref.1), custom_call_target="tpu_custom_call" | custom-call | tf_op jit(solution)/shard_map/ask/pallas_call | solution.py:81
  14.5 4.2 %all-to-all-done = s32[8,1,8]{2,1,0:T(1,128)S(1)} async-done(((s32[8,1,8]{2,1,0:T(1,128)}), s32[8,1,8]{2,1,0:T(1,128)S(1)}, u32[]{:S(2)}, u32[]{:S(2)}) %all-to-all-start) | async-done | bytes 288 | tf_op jit(solution)/shard_map/all_to_all | solution.py:30
  18.7 0.0 copy-start.5
  18.7 6.4 %all-to-all-start.1 = ((bf16[8,32,128]{2,1,0:T(8,128)(2,1)}), bf16[8,32,128]{2,1,0:T(8,128)(2,1)S(1)}, u32[]{:S(2)}, u32[]{:S(2)}) async-start(bf16[8,32,128]{2,1,0:T(8,128)(2,1)} %get-tuple-element.13), calls=%async_computation.1 | async-start | bytes 131072 | tf_op jit(solution)/shard_map/all_to_all | solution.py:30
  25.1 0.0 copy-done.5
  25.1 2.3 %split_pages.1 = bf16[4,8,2,2,32,128]{5,4,3,2,1,0:T(8,128)(2,1)} custom-call(s32[8,8]{1,0:T(8,128)} %bitcast.28, bf16[8,2,32,1024]{3,2,1,0:T(8,128)(2,1)} %pool_ref.1), custom_call_target="tpu_custom_call" | custom-call | tf_op jit(solution)/shard_map/split_pages/pallas_call | solution.py:119
  27.4 2.5 %all-to-all-done.1 = bf16[8,32,128]{2,1,0:T(8,128)(2,1)S(1)} async-done(((bf16[8,32,128]{2,1,0:T(8,128)(2,1)}), bf16[8,32,128]{2,1,0:T(8,128)(2,1)S(1)}, u32[]{:S(2)}, u32[]{:S(2)}) %all-to-all-start.1) | async-done | bytes 65568 | tf_op jit(solution)/shard_map/all_to_all | solution.py:30
  29.9 0.0 copy-start
  29.9 0.0 copy-start.1
  29.9 0.0 copy-start.2
  29.9 0.0 copy-start.4
  30.0 5.0 %all-to-all-start.2 = ((bf16[64,2,32,128]{3,2,1,0:T(8,128)(2,1)}), bf16[64,2,32,128]{3,2,1,0:T(8,128)(2,1)S(1)}, u32[]{:S(2)}, u32[]{:S(2)}) async-start(bf16[64,2,32,128]{3,2,1,0:T(8,128)(2,1)} %bitcast.27), calls=%async_computation.2 | async-start | bytes 2097152 | tf_op jit(solution)/shard_map/all_to_all | solution.py:30
  35.0 5.1 %collective-permute-start.1 = (bf16[128,128]{1,0:T(8,128)(2,1)S(1)}, bf16[128,128]{1,0:T(8,128)(2,1)S(1)}, u32[]{:S(2)}, u32[]{:S(2)}) collective-permute-start(bf16[128,128]{1,0:T(8,128)(2,1)S(1)} %bitcast.21), channel_id=1, source_target_pairs={{0,56},{8,0},{16,8},{24,16},{32,24},{40,32},{48,40},{56,48},{1,57}... | collective-permute-start | bytes 98312 | tf_op jit(solution)/shard_map/ppermute | solution.py:35
  40.1 1.9 %collective-permute-start = (bf16[128,128]{1,0:T(8,128)(2,1)S(1)}, bf16[128,128]{1,0:T(8,128)(2,1)S(1)}, u32[]{:S(2)}, u32[]{:S(2)}) collective-permute-start(bf16[128,128]{1,0:T(8,128)(2,1)S(1)} %bitcast.22), channel_id=1, source_target_pairs={{0,8},{8,16},{16,24},{24,32},{32,40},{40,48},{48,56},{56,0},{1,9},... | collective-permute-start | bytes 98312 | tf_op jit(solution)/shard_map/ppermute | solution.py:35
  42.0 0.0 collective-permute-done.1.rest_1_
  42.1 4.7 %collective-permute-start.2 = (bf16[256,128]{1,0:T(8,128)(2,1)S(1)}, bf16[256,128]{1,0:T(8,128)(2,1)S(1)}, u32[]{:S(2)}, u32[]{:S(2)}) collective-permute-start(bf16[256,128]{1,0:T(8,128)(2,1)S(1)} %pad_maximum_fusion.1), channel_id=1, source_target_pairs={{0,24},{8,32},{16,40},{24,48},{32,56},{40,0},{48,8},{56,16},{1,25}... | collective-permute-start | bytes 196616 | tf_op jit(solution)/shard_map/ppermute | solution.py:35
  46.8 0.0 collective-permute-done.rest_0_
  46.8 3.6 %collective-permute-start.3 = (bf16[384,128]{1,0:T(8,128)(2,1)S(1)}, bf16[384,128]{1,0:T(8,128)(2,1)S(1)}, u32[]{:S(2)}, u32[]{:S(2)}) collective-permute-start(bf16[384,128]{1,0:T(8,128)(2,1)S(1)} %pad_maximum_fusion), channel_id=1, source_target_pairs={{0,40},{8,48},{16,56},{24,0},{32,8},{40,16},{48,24},{56,32},{1,41}... | collective-permute-start | bytes 294920 | tf_op jit(solution)/shard_map/ppermute | solution.py:35
  50.4 0.0 collective-permute-done.2.rest_2_
  50.4 4.8 %collective-permute-done.3.rest_3_ = bf16[384,128]{1,0:T(8,128)(2,1)S(1)} collective-permute-done((bf16[384,128]{1,0:T(8,128)(2,1)S(1)}, bf16[384,128]{1,0:T(8,128)(2,1)S(1)}, u32[]{:S(2)}, u32[]{:S(2)}) %collective-permute-start.3) | collective-permute-done | bytes 98336 | tf_op jit(solution)/shard_map/ppermute | solution.py:35
  55.3 8.3 %all-to-all-done.2 = bf16[64,2,32,128]{3,2,1,0:T(8,128)(2,1)S(1)} async-done(((bf16[64,2,32,128]{3,2,1,0:T(8,128)(2,1)}), bf16[64,2,32,128]{3,2,1,0:T(8,128)(2,1)S(1)}, u32[]{:S(2)}, u32[]{:S(2)}) %all-to-all-start.2) | async-done | bytes 1048608 | tf_op jit(solution)/shard_map/all_to_all | solution.py:30
  63.5 2.5 %attend.1 = bf16[4,2,8,16,128]{4,3,2,1,0:T(8,128)(2,1)S(1)} custom-call(f32[8,128]{1,0:T(8,128)S(1)} %fusion.info_ref, bf16[128,128]{1,0:T(8,128)(2,1)S(1)} %bitcast.25, bf16[4,8,2,2,32,128]{5,4,3,2,1,0:T(8,128)(2,1)S(1)} %bitcast.18, bf16[128,128]{1,0:T(8,128)(2,1)S(1)} %collective-permute-done.rest_0_, ...), custom_call_target="tpu_custom_call" | custom-call | tf_op jit(solution)/shard_map/attend/pallas_call | solution.py:184
  66.0 22.2 %all_to_all.20 = bf16[64,16,128]{2,1,0:T(8,128)(2,1)S(1)} all-to-all(bf16[64,16,128]{2,1,0:T(8,128)(2,1)S(1)} %bitcast.20), channel_id=1, replica_groups=mesh['z'=8,'y'=8,'x'=4,'c'=2] {'x','c','y'}, dimensions={0} | all-to-all | bytes 524288 | tf_op jit(solution)/shard_map/all_to_all | solution.py:30
  88.3 0.0 copy-done
  88.3 0.0 copy-done.1
  88.3 0.0 copy-done.2
  88.3 0.0 copy-done.3
  88.3 0.0 copy-done.4
  88.3 1.2 %finish.1 = bf16[16,1024]{1,0:T(8,128)(2,1)} custom-call(bf16[4,2,8,16,128]{4,3,2,1,0:T(8,128)(2,1)S(1)} %bitcast.19, f32[16,1024]{1,0:T(8,128)S(1)} %copy-done.1, bf16[16,1024]{1,0:T(8,128)(2,1)S(1)} %copy-done.3, f32[1,1024]{1,0:T(1,128)S(1)} %bitcast.26, bf16[16,1024]{1,0:T(8,128)(2,1)S(1)} %copy-done.2, bf16[1024,1024]{1,0:T(8,128)(2,1)S(1)} %copy-done), custom_call_target="tpu_custom_call" | custom-call | tf_op jit(solution)/shard_map/finish/pallas_call | solution.py:213
  (6 shorter events, 0.1 us)
Async XLA Ops:
  1.3 17.4 %all-to-all-start = ((s32[8,1,8]{2,1,0:T(1,128)}), s32[8,1,8]{2,1,0:T(1,128)S(1)}, u32[]{:S(2)}, u32[]{:S(2)}) async-start(s32[8,1,8]{2,1,0:T(1,128)} %broadcast_in_dim.8), calls=%async_computation | async-start | bytes 8192 | tf_op jit(solution)/shard_map/all_to_all | solution.py:30
  18.7 6.4 %copy-start.5 = (s32[8,1,8]{2,1,0:T(1,128)}, s32[8,1,8]{2,1,0:T(1,128)S(1)}, u32[]{:S(2)}) copy-start(s32[8,1,8]{2,1,0:T(1,128)S(1)} %all-to-all-done) | copy-start | bytes 772
  18.7 11.3 %all-to-all-start.1 = ((bf16[8,32,128]{2,1,0:T(8,128)(2,1)}), bf16[8,32,128]{2,1,0:T(8,128)(2,1)S(1)}, u32[]{:S(2)}, u32[]{:S(2)}) async-start(bf16[8,32,128]{2,1,0:T(8,128)(2,1)} %get-tuple-element.13), calls=%async_computation.1 | async-start | bytes 131072 | tf_op jit(solution)/shard_map/all_to_all | solution.py:30
  29.9 58.4 %copy-start = (bf16[1024,1024]{1,0:T(8,128)(2,1)S(1)}, bf16[1024,1024]{1,0:T(8,128)(2,1)}, u32[]{:S(2)}) copy-start(bf16[1024,1024]{1,0:T(8,128)(2,1)} %weight_ref.1) | copy-start | bytes 6291460
  29.9 58.4 %copy-start.1 = (f32[16,1024]{1,0:T(8,128)S(1)}, f32[16,1024]{1,0:T(8,128)}, u32[]{:S(2)}) copy-start(f32[16,1024]{1,0:T(8,128)} %get-tuple-element.15.own_ref) | copy-start | bytes 196612
  29.9 58.4 %copy-start.2 = (bf16[16,1024]{1,0:T(8,128)(2,1)S(1)}, bf16[16,1024]{1,0:T(8,128)(2,1)}, u32[]{:S(2)}) copy-start(bf16[16,1024]{1,0:T(8,128)(2,1)} %input_ref.1) | copy-start | bytes 98308
  29.9 58.4 %copy-start.3 = (bf16[16,1024]{1,0:T(8,128)(2,1)S(1)}, bf16[16,1024]{1,0:T(8,128)(2,1)}, u32[]{:S(2)}) copy-start(bf16[16,1024]{1,0:T(8,128)(2,1)} %get-tuple-element.16.u_ref) | copy-start | bytes 98308
  29.9 58.4 %copy-start.4 = (f32[1024]{0:T(1024)S(1)}, f32[1024]{0:T(1024)}, u32[]{:S(2)}) copy-start(f32[1024]{0:T(1024)} %param.16) | copy-start | bytes 12292
  30.0 33.6 %all-to-all-start.2 = ((bf16[64,2,32,128]{3,2,1,0:T(8,128)(2,1)}), bf16[64,2,32,128]{3,2,1,0:T(8,128)(2,1)S(1)}, u32[]{:S(2)}, u32[]{:S(2)}) async-start(bf16[64,2,32,128]{3,2,1,0:T(8,128)(2,1)} %bitcast.27), calls=%async_computation.2 | async-start | bytes 2097152 | tf_op jit(solution)/shard_map/all_to_all | solution.py:30
  35.0 7.1 %collective-permute-start.1 = (bf16[128,128]{1,0:T(8,128)(2,1)S(1)}, bf16[128,128]{1,0:T(8,128)(2,1)S(1)}, u32[]{:S(2)}, u32[]{:S(2)}) collective-permute-start(bf16[128,128]{1,0:T(8,128)(2,1)S(1)} %bitcast.21), channel_id=1, source_target_pairs={{0,56},{8,0},{16,8},{24,16},{32,24},{40,32},{48,40},{56,48},{1,57}... | collective-permute-start | bytes 98312 | tf_op jit(solution)/shard_map/ppermute | solution.py:35
  40.1 6.7 %collective-permute-start = (bf16[128,128]{1,0:T(8,128)(2,1)S(1)}, bf16[128,128]{1,0:T(8,128)(2,1)S(1)}, u32[]{:S(2)}, u32[]{:S(2)}) collective-permute-start(bf16[128,128]{1,0:T(8,128)(2,1)S(1)} %bitcast.22), channel_id=1, source_target_pairs={{0,8},{8,16},{16,24},{24,32},{32,40},{40,48},{48,56},{56,0},{1,9},... | collective-permute-start | bytes 98312 | tf_op jit(solution)/shard_map/ppermute | solution.py:35
  42.1 8.3 %collective-permute-start.2 = (bf16[256,128]{1,0:T(8,128)(2,1)S(1)}, bf16[256,128]{1,0:T(8,128)(2,1)S(1)}, u32[]{:S(2)}, u32[]{:S(2)}) collective-permute-start(bf16[256,128]{1,0:T(8,128)(2,1)S(1)} %pad_maximum_fusion.1), channel_id=1, source_target_pairs={{0,24},{8,32},{16,40},{24,48},{32,56},{40,0},{48,8},{56,16},{1,25}... | collective-permute-start | bytes 196616 | tf_op jit(solution)/shard_map/ppermute | solution.py:35
  46.8 8.4 %collective-permute-start.3 = (bf16[384,128]{1,0:T(8,128)(2,1)S(1)}, bf16[384,128]{1,0:T(8,128)(2,1)S(1)}, u32[]{:S(2)}, u32[]{:S(2)}) collective-permute-start(bf16[384,128]{1,0:T(8,128)(2,1)S(1)} %pad_maximum_fusion), channel_id=1, source_target_pairs={{0,40},{8,48},{16,56},{24,0},{32,8},{40,16},{48,24},{56,32},{1,41}... | collective-permute-start | bytes 294920 | tf_op jit(solution)/shard_map/ppermute | solution.py:35

commit v10 on v9

--- a/solution.py
+++ b/solution.py
@@ -36,8 +36,7 @@
 
 
 def silu(value):
-    half = value * 0.5
-    return half + half * jnp.tanh(half)
+    return value / (1.0 + jnp.exp(-value))
 
 
 def ask_kernel(scale, owner_ref, length_ref, seen_ref, proj_ref, out_ref, own_ref, u_ref):

time: 90.1 us -> 90.4 us (level)
  no operation moved by 1% of the time
where the time goes in v10:
time: 90.4 us; the launch traced here: 89.8 us
  starting transfers between devices  37.6 us (42%)
  blocking collectives  22.3 us (25%)
  waiting for transfers between devices  19.8 us (22%)
  Pallas kernels  8.06 us (9%)
    all_to_all x3, starting transfers between devices, exchange(): return lax.all_to_all(array, axes, split_axis=0, concat_axis=0, tiled=True)  22.3 us
    all_to_all x1, blocking collectives, exchange(): return lax.all_to_all(array, axes, split_axis=0, concat_axis=0, tiled=True)  22.3 us
    ppermute x4, starting transfers between devices, shift(): return lax.ppermute(array, axis, [(i, (i + step) % n) for i in range(n)])  15.3 us
    all_to_all x3, waiting for transfers between devices, exchange(): return lax.all_to_all(array, axes, split_axis=0, concat_axis=0, tiled=True)  14.9 us
    ppermute x4, waiting for transfers between devices, shift(): return lax.ppermute(array, axis, [(i, (i + step) % n) for i in range(n)])  4.83 us
    pallas_call x1, Pallas kernels, attend(): pl.pallas_call(functools.partial(attend_kernel, scale), in_specs=[VMEM] *...  2.83 us
    pallas_call x1, Pallas kernels, split_pages(): pl.pallas_call(split_pages_kernel, in_specs=[SMEM, VMEM], out_specs=HBM,...  2.32 us
  transfers between devices with their start and end apart: 7, of which 4 were waited for; matrix products, arithmetic and copies ran while one was open for 0% of the time, Pallas kernels for 5%

profile of v10, /device:TPU:1, one launch (start us, length us, event | category | flops | bytes accessed | tf_op | source)
XLA Modules:
  0.0 89.8 jit_solution(14560957941018562156)
XLA Ops:
  0.0 0.7 add_bitcast_fusion
  0.7 0.6 broadcast_in_dim.8
  1.3 10.9 %all-to-all-start = ((s32[8,1,8]{2,1,0:T(1,128)}), s32[8,1,8]{2,1,0:T(1,128)S(1)}, u32[]{:S(2)}, u32[]{:S(2)}) async-start(s32[8,1,8]{2,1,0:T(1,128)} %broadcast_in_dim.8), calls=%async_computation | async-start | bytes 8192 | tf_op jit(solution)/shard_map/all_to_all | solution.py:30
  12.8 1.7 %ask.1 = (bf16[8,32,128]{2,1,0:T(8,128)(2,1)}, f32[16,1024]{1,0:T(8,128)}, bf16[16,1024]{1,0:T(8,128)(2,1)}) custom-call(s32[8]{0:T(128)} %bitcast.30, s32[1]{0:T(128)S(6)} %copy.13.length_ref, s32[2,8]{1,0:T(2,128)} %bitcast.29, bf16[16,4096]{1,0:T(8,128)(2,1)} %proj_ref.1), custom_call_target="tpu_custom_call" | custom-call | tf_op jit(solution)/shard_map/ask/pallas_call | solution.py:80
  14.5 4.1 %all-to-all-done = s32[8,1,8]{2,1,0:T(1,128)S(1)} async-done(((s32[8,1,8]{2,1,0:T(1,128)}), s32[8,1,8]{2,1,0:T(1,128)S(1)}, u32[]{:S(2)}, u32[]{:S(2)}) %all-to-all-start) | async-done | bytes 288 | tf_op jit(solution)/shard_map/all_to_all | solution.py:30
  18.7 0.0 copy-start.5
  18.7 6.4 %all-to-all-start.1 = ((bf16[8,32,128]{2,1,0:T(8,128)(2,1)}), bf16[8,32,128]{2,1,0:T(8,128)(2,1)S(1)}, u32[]{:S(2)}, u32[]{:S(2)}) async-start(bf16[8,32,128]{2,1,0:T(8,128)(2,1)} %get-tuple-element.13), calls=%async_computation.1 | async-start | bytes 131072 | tf_op jit(solution)/shard_map/all_to_all | solution.py:30
  25.1 0.0 copy-done.5
  25.1 2.3 %split_pages.1 = bf16[4,8,2,2,32,128]{5,4,3,2,1,0:T(8,128)(2,1)} custom-call(s32[8,8]{1,0:T(8,128)} %bitcast.28, bf16[8,2,32,1024]{3,2,1,0:T(8,128)(2,1)} %pool_ref.1), custom_call_target="tpu_custom_call" | custom-call | tf_op jit(solution)/shard_map/split_pages/pallas_call | solution.py:118
  27.4 2.5 %all-to-all-done.1 = bf16[8,32,128]{2,1,0:T(8,128)(2,1)S(1)} async-done(((bf16[8,32,128]{2,1,0:T(8,128)(2,1)}), bf16[8,32,128]{2,1,0:T(8,128)(2,1)S(1)}, u32[]{:S(2)}, u32[]{:S(2)}) %all-to-all-start.1) | async-done | bytes 65568 | tf_op jit(solution)/shard_map/all_to_all | solution.py:30
  29.9 0.0 copy-start
  29.9 0.0 copy-start.1
  29.9 0.0 copy-start.2
  29.9 0.0 copy-start.4
  30.0 5.0 %all-to-all-start.2 = ((bf16[64,2,32,128]{3,2,1,0:T(8,128)(2,1)}), bf16[64,2,32,128]{3,2,1,0:T(8,128)(2,1)S(1)}, u32[]{:S(2)}, u32[]{:S(2)}) async-start(bf16[64,2,32,128]{3,2,1,0:T(8,128)(2,1)} %bitcast.27), calls=%async_computation.2 | async-start | bytes 2097152 | tf_op jit(solution)/shard_map/all_to_all | solution.py:30
  35.0 5.1 %collective-permute-start.1 = (bf16[128,128]{1,0:T(8,128)(2,1)S(1)}, bf16[128,128]{1,0:T(8,128)(2,1)S(1)}, u32[]{:S(2)}, u32[]{:S(2)}) collective-permute-start(bf16[128,128]{1,0:T(8,128)(2,1)S(1)} %bitcast.21), channel_id=1, source_target_pairs={{0,56},{8,0},{16,8},{24,16},{32,24},{40,32},{48,40},{56,48},{1,57}... | collective-permute-start | bytes 98312 | tf_op jit(solution)/shard_map/ppermute | solution.py:35
  40.1 1.9 %collective-permute-start = (bf16[128,128]{1,0:T(8,128)(2,1)S(1)}, bf16[128,128]{1,0:T(8,128)(2,1)S(1)}, u32[]{:S(2)}, u32[]{:S(2)}) collective-permute-start(bf16[128,128]{1,0:T(8,128)(2,1)S(1)} %bitcast.22), channel_id=1, source_target_pairs={{0,8},{8,16},{16,24},{24,32},{32,40},{40,48},{48,56},{56,0},{1,9},... | collective-permute-start | bytes 98312 | tf_op jit(solution)/shard_map/ppermute | solution.py:35
  42.0 0.0 collective-permute-done.1.rest_1_
  42.1 4.7 %collective-permute-start.2 = (bf16[256,128]{1,0:T(8,128)(2,1)S(1)}, bf16[256,128]{1,0:T(8,128)(2,1)S(1)}, u32[]{:S(2)}, u32[]{:S(2)}) collective-permute-start(bf16[256,128]{1,0:T(8,128)(2,1)S(1)} %pad_maximum_fusion.1), channel_id=1, source_target_pairs={{0,24},{8,32},{16,40},{24,48},{32,56},{40,0},{48,8},{56,16},{1,25}... | collective-permute-start | bytes 196616 | tf_op jit(solution)/shard_map/ppermute | solution.py:35
  46.8 0.0 collective-permute-done.rest_0_
  46.8 3.6 %collective-permute-start.3 = (bf16[384,128]{1,0:T(8,128)(2,1)S(1)}, bf16[384,128]{1,0:T(8,128)(2,1)S(1)}, u32[]{:S(2)}, u32[]{:S(2)}) collective-permute-start(bf16[384,128]{1,0:T(8,128)(2,1)S(1)} %pad_maximum_fusion), channel_id=1, source_target_pairs={{0,40},{8,48},{16,56},{24,0},{32,8},{40,16},{48,24},{56,32},{1,41}... | collective-permute-start | bytes 294920 | tf_op jit(solution)/shard_map/ppermute | solution.py:35
  50.4 0.0 collective-permute-done.2.rest_2_
  50.4 4.8 %collective-permute-done.3.rest_3_ = bf16[384,128]{1,0:T(8,128)(2,1)S(1)} collective-permute-done((bf16[384,128]{1,0:T(8,128)(2,1)S(1)}, bf16[384,128]{1,0:T(8,128)(2,1)S(1)}, u32[]{:S(2)}, u32[]{:S(2)}) %collective-permute-start.3) | collective-permute-done | bytes 98336 | tf_op jit(solution)/shard_map/ppermute | solution.py:35
  55.3 8.3 %all-to-all-done.2 = bf16[64,2,32,128]{3,2,1,0:T(8,128)(2,1)S(1)} async-done(((bf16[64,2,32,128]{3,2,1,0:T(8,128)(2,1)}), bf16[64,2,32,128]{3,2,1,0:T(8,128)(2,1)S(1)}, u32[]{:S(2)}, u32[]{:S(2)}) %all-to-all-start.2) | async-done | bytes 1048608 | tf_op jit(solution)/shard_map/all_to_all | solution.py:30
  63.5 2.8 %attend.1 = bf16[4,2,8,16,128]{4,3,2,1,0:T(8,128)(2,1)S(1)} custom-call(f32[8,128]{1,0:T(8,128)S(1)} %fusion.info_ref, bf16[128,128]{1,0:T(8,128)(2,1)S(1)} %bitcast.25, bf16[4,8,2,2,32,128]{5,4,3,2,1,0:T(8,128)(2,1)S(1)} %bitcast.18, bf16[128,128]{1,0:T(8,128)(2,1)S(1)} %collective-permute-done.rest_0_, ...), custom_call_target="tpu_custom_call" | custom-call | tf_op jit(solution)/shard_map/attend/pallas_call | solution.py:183
  66.4 22.3 %all_to_all.20 = bf16[64,16,128]{2,1,0:T(8,128)(2,1)S(1)} all-to-all(bf16[64,16,128]{2,1,0:T(8,128)(2,1)S(1)} %bitcast.20), channel_id=1, replica_groups=mesh['z'=8,'y'=8,'x'=4,'c'=2] {'x','c','y'}, dimensions={0} | all-to-all | bytes 524288 | tf_op jit(solution)/shard_map/all_to_all | solution.py:30
  88.6 0.0 copy-done
  88.6 0.0 copy-done.1
  88.6 0.0 copy-done.2
  88.6 0.0 copy-done.3
  88.6 0.0 copy-done.4
  88.7 1.2 %finish.1 = bf16[16,1024]{1,0:T(8,128)(2,1)} custom-call(bf16[4,2,8,16,128]{4,3,2,1,0:T(8,128)(2,1)S(1)} %bitcast.19, f32[16,1024]{1,0:T(8,128)S(1)} %copy-done.1, bf16[16,1024]{1,0:T(8,128)(2,1)S(1)} %copy-done.3, f32[1,1024]{1,0:T(1,128)S(1)} %bitcast.26, bf16[16,1024]{1,0:T(8,128)(2,1)S(1)} %copy-done.2, bf16[1024,1024]{1,0:T(8,128)(2,1)S(1)} %copy-done), custom_call_target="tpu_custom_call" | custom-call | tf_op jit(solution)/shard_map/finish/pallas_call | solution.py:212
  (6 shorter events, 0.1 us)
Async XLA Ops:
  1.3 17.4 %all-to-all-start = ((s32[8,1,8]{2,1,0:T(1,128)}), s32[8,1,8]{2,1,0:T(1,128)S(1)}, u32[]{:S(2)}, u32[]{:S(2)}) async-start(s32[8,1,8]{2,1,0:T(1,128)} %broadcast_in_dim.8), calls=%async_computation | async-start | bytes 8192 | tf_op jit(solution)/shard_map/all_to_all | solution.py:30
  18.7 6.4 %copy-start.5 = (s32[8,1,8]{2,1,0:T(1,128)}, s32[8,1,8]{2,1,0:T(1,128)S(1)}, u32[]{:S(2)}) copy-start(s32[8,1,8]{2,1,0:T(1,128)S(1)} %all-to-all-done) | copy-start | bytes 772
  18.7 11.3 %all-to-all-start.1 = ((bf16[8,32,128]{2,1,0:T(8,128)(2,1)}), bf16[8,32,128]{2,1,0:T(8,128)(2,1)S(1)}, u32[]{:S(2)}, u32[]{:S(2)}) async-start(bf16[8,32,128]{2,1,0:T(8,128)(2,1)} %get-tuple-element.13), calls=%async_computation.1 | async-start | bytes 131072 | tf_op jit(solution)/shard_map/all_to_all | solution.py:30
  29.9 58.7 %copy-start = (bf16[1024,1024]{1,0:T(8,128)(2,1)S(1)}, bf16[1024,1024]{1,0:T(8,128)(2,1)}, u32[]{:S(2)}) copy-start(bf16[1024,1024]{1,0:T(8,128)(2,1)} %weight_ref.1) | copy-start | bytes 6291460
  29.9 58.7 %copy-start.1 = (f32[16,1024]{1,0:T(8,128)S(1)}, f32[16,1024]{1,0:T(8,128)}, u32[]{:S(2)}) copy-start(f32[16,1024]{1,0:T(8,128)} %get-tuple-element.15.own_ref) | copy-start | bytes 196612
  29.9 58.7 %copy-start.2 = (bf16[16,1024]{1,0:T(8,128)(2,1)S(1)}, bf16[16,1024]{1,0:T(8,128)(2,1)}, u32[]{:S(2)}) copy-start(bf16[16,1024]{1,0:T(8,128)(2,1)} %input_ref.1) | copy-start | bytes 98308
  29.9 58.7 %copy-start.3 = (bf16[16,1024]{1,0:T(8,128)(2,1)S(1)}, bf16[16,1024]{1,0:T(8,128)(2,1)}, u32[]{:S(2)}) copy-start(bf16[16,1024]{1,0:T(8,128)(2,1)} %get-tuple-element.16.u_ref) | copy-start | bytes 98308
  29.9 58.7 %copy-start.4 = (f32[1024]{0:T(1024)S(1)}, f32[1024]{0:T(1024)}, u32[]{:S(2)}) copy-start(f32[1024]{0:T(1024)} %param.16) | copy-start | bytes 12292
  30.0 33.6 %all-to-all-start.2 = ((bf16[64,2,32,128]{3,2,1,0:T(8,128)(2,1)}), bf16[64,2,32,128]{3,2,1,0:T(8,128)(2,1)S(1)}, u32[]{:S(2)}, u32[]{:S(2)}) async-start(bf16[64,2,32,128]{3,2,1,0:T(8,128)(2,1)} %bitcast.27), calls=%async_computation.2 | async-start | bytes 2097152 | tf_op jit(solution)/shard_map/all_to_all | solution.py:30
  35.0 7.1 %collective-permute-start.1 = (bf16[128,128]{1,0:T(8,128)(2,1)S(1)}, bf16[128,128]{1,0:T(8,128)(2,1)S(1)}, u32[]{:S(2)}, u32[]{:S(2)}) collective-permute-start(bf16[128,128]{1,0:T(8,128)(2,1)S(1)} %bitcast.21), channel_id=1, source_target_pairs={{0,56},{8,0},{16,8},{24,16},{32,24},{40,32},{48,40},{56,48},{1,57}... | collective-permute-start | bytes 98312 | tf_op jit(solution)/shard_map/ppermute | solution.py:35
  40.1 6.7 %collective-permute-start = (bf16[128,128]{1,0:T(8,128)(2,1)S(1)}, bf16[128,128]{1,0:T(8,128)(2,1)S(1)}, u32[]{:S(2)}, u32[]{:S(2)}) collective-permute-start(bf16[128,128]{1,0:T(8,128)(2,1)S(1)} %bitcast.22), channel_id=1, source_target_pairs={{0,8},{8,16},{16,24},{24,32},{32,40},{40,48},{48,56},{56,0},{1,9},... | collective-permute-start | bytes 98312 | tf_op jit(solution)/shard_map/ppermute | solution.py:35
  42.1 8.3 %collective-permute-start.2 = (bf16[256,128]{1,0:T(8,128)(2,1)S(1)}, bf16[256,128]{1,0:T(8,128)(2,1)S(1)}, u32[]{:S(2)}, u32[]{:S(2)}) collective-permute-start(bf16[256,128]{1,0:T(8,128)(2,1)S(1)} %pad_maximum_fusion.1), channel_id=1, source_target_pairs={{0,24},{8,32},{16,40},{24,48},{32,56},{40,0},{48,8},{56,16},{1,25}... | collective-permute-start | bytes 196616 | tf_op jit(solution)/shard_map/ppermute | solution.py:35
  46.8 8.4 %collective-permute-start.3 = (bf16[384,128]{1,0:T(8,128)(2,1)S(1)}, bf16[384,128]{1,0:T(8,128)(2,1)S(1)}, u32[]{:S(2)}, u32[]{:S(2)}) collective-permute-start(bf16[384,128]{1,0:T(8,128)(2,1)S(1)} %pad_maximum_fusion), channel_id=1, source_target_pairs={{0,40},{8,48},{16,56},{24,0},{32,8},{40,16},{48,24},{56,32},{1,41}... | collective-permute-start | bytes 294920 | tf_op jit(solution)/shard_map/ppermute | solution.py:35

commit v11 on v10

--- a/solution.py
+++ b/solution.py
@@ -20,6 +20,8 @@
 
 FIELDS = 16
 LIVE = 8
+
+LOG2_E = 1.4426950408889634
 
 VMEM = pl.BlockSpec(memory_space=pltpu.VMEM)
 SMEM = pl.BlockSpec(memory_space=pltpu.SMEM)
@@ -163,7 +165,8 @@
         live = fields[o * FIELDS + LIVE : o * FIELDS + LIVE + 1]
         allowed = jnp.where(within < live, seen, 0.0).astype(jnp.bfloat16)
         score = lax.dot_general(q, keys, (((1,), (1,)), ((), ())), preferred_element_type=jnp.float32)
-        weight = silu(score * scale).astype(jnp.bfloat16)
+        odds = jnp.exp2(score * (-scale * LOG2_E))
+        weight = (score * scale / (1.0 + odds)).astype(jnp.bfloat16)
         weight = weight.reshape(tiles, height, span) * allowed[:, None, :]
         part = jnp.dot(weight.reshape(tiles * height, span), values, preferred_element_type=jnp.float32)
         if o == 0:

time: 90.4 us -> 90.1 us (level)
  no operation moved by 1% of the time
where the time goes in v11:
time: 90.1 us; the launch traced here: 89.5 us
  starting transfers between devices  37.6 us (42%)
  blocking collectives  22.3 us (25%)
  waiting for transfers between devices  19.8 us (22%)
  Pallas kernels  7.73 us (9%)
    all_to_all x3, starting transfers between devices, exchange(): return lax.all_to_all(array, axes, split_axis=0, concat_axis=0, tiled=True)  22.3 us
    all_to_all x1, blocking collectives, exchange(): return lax.all_to_all(array, axes, split_axis=0, concat_axis=0, tiled=True)  22.3 us
    ppermute x4, starting transfers between devices, shift(): return lax.ppermute(array, axis, [(i, (i + step) % n) for i in range(n)])  15.3 us
    all_to_all x3, waiting for transfers between devices, exchange(): return lax.all_to_all(array, axes, split_axis=0, concat_axis=0, tiled=True)  14.9 us
    ppermute x4, waiting for transfers between devices, shift(): return lax.ppermute(array, axis, [(i, (i + step) % n) for i in range(n)])  4.83 us
    pallas_call x1, Pallas kernels, attend(): pl.pallas_call(functools.partial(attend_kernel, scale), in_specs=[VMEM] *...  2.5 us
    pallas_call x1, Pallas kernels, split_pages(): pl.pallas_call(split_pages_kernel, in_specs=[SMEM, VMEM], out_specs=HBM,...  2.32 us
  transfers between devices with their start and end apart: 7, of which 4 were waited for; matrix products, arithmetic and copies ran while one was open for 0% of the time, Pallas kernels for 5%

profile of v11, /device:TPU:1, one launch (start us, length us, event | category | flops | bytes accessed | tf_op | source)
XLA Modules:
  0.0 89.5 jit_solution(1581951180950703299)
XLA Ops:
  0.0 0.7 add_bitcast_fusion
  0.7 0.6 broadcast_in_dim.8
  1.3 10.9 %all-to-all-start = ((s32[8,1,8]{2,1,0:T(1,128)}), s32[8,1,8]{2,1,0:T(1,128)S(1)}, u32[]{:S(2)}, u32[]{:S(2)}) async-start(s32[8,1,8]{2,1,0:T(1,128)} %broadcast_in_dim.8), calls=%async_computation | async-start | bytes 8192 | tf_op jit(solution)/shard_map/all_to_all | solution.py:32
  12.8 1.7 %ask.1 = (bf16[8,32,128]{2,1,0:T(8,128)(2,1)}, f32[16,1024]{1,0:T(8,128)}, bf16[16,1024]{1,0:T(8,128)(2,1)}) custom-call(s32[8]{0:T(128)} %bitcast.30, s32[1]{0:T(128)S(6)} %copy.13.length_ref, s32[2,8]{1,0:T(2,128)} %bitcast.29, bf16[16,4096]{1,0:T(8,128)(2,1)} %proj_ref.1), custom_call_target="tpu_custom_call" | custom-call | tf_op jit(solution)/shard_map/ask/pallas_call | solution.py:82
  14.5 4.1 %all-to-all-done = s32[8,1,8]{2,1,0:T(1,128)S(1)} async-done(((s32[8,1,8]{2,1,0:T(1,128)}), s32[8,1,8]{2,1,0:T(1,128)S(1)}, u32[]{:S(2)}, u32[]{:S(2)}) %all-to-all-start) | async-done | bytes 288 | tf_op jit(solution)/shard_map/all_to_all | solution.py:32
  18.7 0.0 copy-start.5
  18.7 6.4 %all-to-all-start.1 = ((bf16[8,32,128]{2,1,0:T(8,128)(2,1)}), bf16[8,32,128]{2,1,0:T(8,128)(2,1)S(1)}, u32[]{:S(2)}, u32[]{:S(2)}) async-start(bf16[8,32,128]{2,1,0:T(8,128)(2,1)} %get-tuple-element.13), calls=%async_computation.1 | async-start | bytes 131072 | tf_op jit(solution)/shard_map/all_to_all | solution.py:32
  25.1 0.0 copy-done.5
  25.1 2.3 %split_pages.1 = bf16[4,8,2,2,32,128]{5,4,3,2,1,0:T(8,128)(2,1)} custom-call(s32[8,8]{1,0:T(8,128)} %bitcast.28, bf16[8,2,32,1024]{3,2,1,0:T(8,128)(2,1)} %pool_ref.1), custom_call_target="tpu_custom_call" | custom-call | tf_op jit(solution)/shard_map/split_pages/pallas_call | solution.py:120
  27.4 2.5 %all-to-all-done.1 = bf16[8,32,128]{2,1,0:T(8,128)(2,1)S(1)} async-done(((bf16[8,32,128]{2,1,0:T(8,128)(2,1)}), bf16[8,32,128]{2,1,0:T(8,128)(2,1)S(1)}, u32[]{:S(2)}, u32[]{:S(2)}) %all-to-all-start.1) | async-done | bytes 65568 | tf_op jit(solution)/shard_map/all_to_all | solution.py:32
  29.9 0.0 copy-start
  29.9 0.0 copy-start.1
  29.9 0.0 copy-start.2
  29.9 0.0 copy-start.4
  30.0 5.0 %all-to-all-start.2 = ((bf16[64,2,32,128]{3,2,1,0:T(8,128)(2,1)}), bf16[64,2,32,128]{3,2,1,0:T(8,128)(2,1)S(1)}, u32[]{:S(2)}, u32[]{:S(2)}) async-start(bf16[64,2,32,128]{3,2,1,0:T(8,128)(2,1)} %bitcast.27), calls=%async_computation.2 | async-start | bytes 2097152 | tf_op jit(solution)/shard_map/all_to_all | solution.py:32
  35.0 5.1 %collective-permute-start.1 = (bf16[128,128]{1,0:T(8,128)(2,1)S(1)}, bf16[128,128]{1,0:T(8,128)(2,1)S(1)}, u32[]{:S(2)}, u32[]{:S(2)}) collective-permute-start(bf16[128,128]{1,0:T(8,128)(2,1)S(1)} %bitcast.21), channel_id=1, source_target_pairs={{0,56},{8,0},{16,8},{24,16},{32,24},{40,32},{48,40},{56,48},{1,57}... | collective-permute-start | bytes 98312 | tf_op jit(solution)/shard_map/ppermute | solution.py:37
  40.1 1.9 %collective-permute-start = (bf16[128,128]{1,0:T(8,128)(2,1)S(1)}, bf16[128,128]{1,0:T(8,128)(2,1)S(1)}, u32[]{:S(2)}, u32[]{:S(2)}) collective-permute-start(bf16[128,128]{1,0:T(8,128)(2,1)S(1)} %bitcast.22), channel_id=1, source_target_pairs={{0,8},{8,16},{16,24},{24,32},{32,40},{40,48},{48,56},{56,0},{1,9},... | collective-permute-start | bytes 98312 | tf_op jit(solution)/shard_map/ppermute | solution.py:37
  42.0 0.0 collective-permute-done.1.rest_1_
  42.1 4.7 %collective-permute-start.2 = (bf16[256,128]{1,0:T(8,128)(2,1)S(1)}, bf16[256,128]{1,0:T(8,128)(2,1)S(1)}, u32[]{:S(2)}, u32[]{:S(2)}) collective-permute-start(bf16[256,128]{1,0:T(8,128)(2,1)S(1)} %pad_maximum_fusion.1), channel_id=1, source_target_pairs={{0,24},{8,32},{16,40},{24,48},{32,56},{40,0},{48,8},{56,16},{1,25}... | collective-permute-start | bytes 196616 | tf_op jit(solution)/shard_map/ppermute | solution.py:37
  46.8 0.0 collective-permute-done.rest_0_
  46.8 3.6 %collective-permute-start.3 = (bf16[384,128]{1,0:T(8,128)(2,1)S(1)}, bf16[384,128]{1,0:T(8,128)(2,1)S(1)}, u32[]{:S(2)}, u32[]{:S(2)}) collective-permute-start(bf16[384,128]{1,0:T(8,128)(2,1)S(1)} %pad_maximum_fusion), channel_id=1, source_target_pairs={{0,40},{8,48},{16,56},{24,0},{32,8},{40,16},{48,24},{56,32},{1,41}... | collective-permute-start | bytes 294920 | tf_op jit(solution)/shard_map/ppermute | solution.py:37
  50.4 0.0 collective-permute-done.2.rest_2_
  50.4 4.8 %collective-permute-done.3.rest_3_ = bf16[384,128]{1,0:T(8,128)(2,1)S(1)} collective-permute-done((bf16[384,128]{1,0:T(8,128)(2,1)S(1)}, bf16[384,128]{1,0:T(8,128)(2,1)S(1)}, u32[]{:S(2)}, u32[]{:S(2)}) %collective-permute-start.3) | collective-permute-done | bytes 98336 | tf_op jit(solution)/shard_map/ppermute | solution.py:37
  55.3 8.3 %all-to-all-done.2 = bf16[64,2,32,128]{3,2,1,0:T(8,128)(2,1)S(1)} async-done(((bf16[64,2,32,128]{3,2,1,0:T(8,128)(2,1)}), bf16[64,2,32,128]{3,2,1,0:T(8,128)(2,1)S(1)}, u32[]{:S(2)}, u32[]{:S(2)}) %all-to-all-start.2) | async-done | bytes 1048608 | tf_op jit(solution)/shard_map/all_to_all | solution.py:32
  63.5 2.5 %attend.1 = bf16[4,2,8,16,128]{4,3,2,1,0:T(8,128)(2,1)S(1)} custom-call(f32[8,128]{1,0:T(8,128)S(1)} %fusion.info_ref, bf16[128,128]{1,0:T(8,128)(2,1)S(1)} %bitcast.25, bf16[4,8,2,2,32,128]{5,4,3,2,1,0:T(8,128)(2,1)S(1)} %bitcast.18, bf16[128,128]{1,0:T(8,128)(2,1)S(1)} %collective-permute-done.rest_0_, ...), custom_call_target="tpu_custom_call" | custom-call | tf_op jit(solution)/shard_map/attend/pallas_call | solution.py:186
  66.0 22.3 %all_to_all.20 = bf16[64,16,128]{2,1,0:T(8,128)(2,1)S(1)} all-to-all(bf16[64,16,128]{2,1,0:T(8,128)(2,1)S(1)} %bitcast.20), channel_id=1, replica_groups=mesh['z'=8,'y'=8,'x'=4,'c'=2] {'x','c','y'}, dimensions={0} | all-to-all | bytes 524288 | tf_op jit(solution)/shard_map/all_to_all | solution.py:32
  88.3 0.0 copy-done
  88.3 0.0 copy-done.1
  88.3 0.0 copy-done.2
  88.3 0.0 copy-done.3
  88.3 0.0 copy-done.4
  88.3 1.2 %finish.1 = bf16[16,1024]{1,0:T(8,128)(2,1)} custom-call(bf16[4,2,8,16,128]{4,3,2,1,0:T(8,128)(2,1)S(1)} %bitcast.19, f32[16,1024]{1,0:T(8,128)S(1)} %copy-done.1, bf16[16,1024]{1,0:T(8,128)(2,1)S(1)} %copy-done.3, f32[1,1024]{1,0:T(1,128)S(1)} %bitcast.26, bf16[16,1024]{1,0:T(8,128)(2,1)S(1)} %copy-done.2, bf16[1024,1024]{1,0:T(8,128)(2,1)S(1)} %copy-done), custom_call_target="tpu_custom_call" | custom-call | tf_op jit(solution)/shard_map/finish/pallas_call | solution.py:215
  (6 shorter events, 0.1 us)
Async XLA Ops:
  1.3 17.4 %all-to-all-start = ((s32[8,1,8]{2,1,0:T(1,128)}), s32[8,1,8]{2,1,0:T(1,128)S(1)}, u32[]{:S(2)}, u32[]{:S(2)}) async-start(s32[8,1,8]{2,1,0:T(1,128)} %broadcast_in_dim.8), calls=%async_computation | async-start | bytes 8192 | tf_op jit(solution)/shard_map/all_to_all | solution.py:32
  18.7 6.4 %copy-start.5 = (s32[8,1,8]{2,1,0:T(1,128)}, s32[8,1,8]{2,1,0:T(1,128)S(1)}, u32[]{:S(2)}) copy-start(s32[8,1,8]{2,1,0:T(1,128)S(1)} %all-to-all-done) | copy-start | bytes 772
  18.7 11.3 %all-to-all-start.1 = ((bf16[8,32,128]{2,1,0:T(8,128)(2,1)}), bf16[8,32,128]{2,1,0:T(8,128)(2,1)S(1)}, u32[]{:S(2)}, u32[]{:S(2)}) async-start(bf16[8,32,128]{2,1,0:T(8,128)(2,1)} %get-tuple-element.13), calls=%async_computation.1 | async-start | bytes 131072 | tf_op jit(solution)/shard_map/all_to_all | solution.py:32
  29.9 58.4 %copy-start = (bf16[1024,1024]{1,0:T(8,128)(2,1)S(1)}, bf16[1024,1024]{1,0:T(8,128)(2,1)}, u32[]{:S(2)}) copy-start(bf16[1024,1024]{1,0:T(8,128)(2,1)} %weight_ref.1) | copy-start | bytes 6291460
  29.9 58.4 %copy-start.1 = (f32[16,1024]{1,0:T(8,128)S(1)}, f32[16,1024]{1,0:T(8,128)}, u32[]{:S(2)}) copy-start(f32[16,1024]{1,0:T(8,128)} %get-tuple-element.15.own_ref) | copy-start | bytes 196612
  29.9 58.4 %copy-start.2 = (bf16[16,1024]{1,0:T(8,128)(2,1)S(1)}, bf16[16,1024]{1,0:T(8,128)(2,1)}, u32[]{:S(2)}) copy-start(bf16[16,1024]{1,0:T(8,128)(2,1)} %input_ref.1) | copy-start | bytes 98308
  29.9 58.4 %copy-start.3 = (bf16[16,1024]{1,0:T(8,128)(2,1)S(1)}, bf16[16,1024]{1,0:T(8,128)(2,1)}, u32[]{:S(2)}) copy-start(bf16[16,1024]{1,0:T(8,128)(2,1)} %get-tuple-element.16.u_ref) | copy-start | bytes 98308
  29.9 58.4 %copy-start.4 = (f32[1024]{0:T(1024)S(1)}, f32[1024]{0:T(1024)}, u32[]{:S(2)}) copy-start(f32[1024]{0:T(1024)} %param.16) | copy-start | bytes 12292
  30.0 33.6 %all-to-all-start.2 = ((bf16[64,2,32,128]{3,2,1,0:T(8,128)(2,1)}), bf16[64,2,32,128]{3,2,1,0:T(8,128)(2,1)S(1)}, u32[]{:S(2)}, u32[]{:S(2)}) async-start(bf16[64,2,32,128]{3,2,1,0:T(8,128)(2,1)} %bitcast.27), calls=%async_computation.2 | async-start | bytes 2097152 | tf_op jit(solution)/shard_map/all_to_all | solution.py:32
  35.0 7.1 %collective-permute-start.1 = (bf16[128,128]{1,0:T(8,128)(2,1)S(1)}, bf16[128,128]{1,0:T(8,128)(2,1)S(1)}, u32[]{:S(2)}, u32[]{:S(2)}) collective-permute-start(bf16[128,128]{1,0:T(8,128)(2,1)S(1)} %bitcast.21), channel_id=1, source_target_pairs={{0,56},{8,0},{16,8},{24,16},{32,24},{40,32},{48,40},{56,48},{1,57}... | collective-permute-start | bytes 98312 | tf_op jit(solution)/shard_map/ppermute | solution.py:37
  40.1 6.7 %collective-permute-start = (bf16[128,128]{1,0:T(8,128)(2,1)S(1)}, bf16[128,128]{1,0:T(8,128)(2,1)S(1)}, u32[]{:S(2)}, u32[]{:S(2)}) collective-permute-start(bf16[128,128]{1,0:T(8,128)(2,1)S(1)} %bitcast.22), channel_id=1, source_target_pairs={{0,8},{8,16},{16,24},{24,32},{32,40},{40,48},{48,56},{56,0},{1,9},... | collective-permute-start | bytes 98312 | tf_op jit(solution)/shard_map/ppermute | solution.py:37
  42.1 8.3 %collective-permute-start.2 = (bf16[256,128]{1,0:T(8,128)(2,1)S(1)}, bf16[256,128]{1,0:T(8,128)(2,1)S(1)}, u32[]{:S(2)}, u32[]{:S(2)}) collective-permute-start(bf16[256,128]{1,0:T(8,128)(2,1)S(1)} %pad_maximum_fusion.1), channel_id=1, source_target_pairs={{0,24},{8,32},{16,40},{24,48},{32,56},{40,0},{48,8},{56,16},{1,25}... | collective-permute-start | bytes 196616 | tf_op jit(solution)/shard_map/ppermute | solution.py:37
  46.8 8.4 %collective-permute-start.3 = (bf16[384,128]{1,0:T(8,128)(2,1)S(1)}, bf16[384,128]{1,0:T(8,128)(2,1)S(1)}, u32[]{:S(2)}, u32[]{:S(2)}) collective-permute-start(bf16[384,128]{1,0:T(8,128)(2,1)S(1)} %pad_maximum_fusion), channel_id=1, source_target_pairs={{0,40},{8,48},{16,56},{24,0},{32,8},{40,16},{48,24},{56,32},{1,41}... | collective-permute-start | bytes 294920 | tf_op jit(solution)/shard_map/ppermute | solution.py:37
